TPU v7x, 128 devices: a whole 4x4x4 slice. The times are simulated.
128 devices in a mesh: seq: 16 (over x_lo, z, core), head: 8 (over y, x_hi).
Axes of the slice: x: 4 (x_hi: 2, x_lo: 2; x = x_hi * 2 + x_lo), y: 4, z: 4, core: 2. Of those that a mesh axis runs over, the one named last changes fastest.
Arguments:
- base_ids: int32 [16384], P('seq'), may hold values from 0 to 4
- embedding: bfloat16 [5, 1024], replicated, may hold values from -6 to 6
- in_weight: bfloat16 [1024, 4384], replicated, may hold values from -0.1875 to 0.1875
- conv_weight: float32 [4, 2304], replicated, may hold values from -3 to 3
- conv_bias: float32 [2304], replicated, may hold values from -3 to 3
- dt_bias: float32 [32], replicated, may hold values from -1.5 to 0
- a_log: float32 [32], replicated, may hold values from -14 to 0
- skip_weight: float32 [32], replicated, may hold values from 0.5 to 1.5
- norm_gain: float32 [2048], replicated, may hold values from 0.25 to 1.75
- out_weight: bfloat16 [2048, 1024], replicated, may hold values from -0.125 to 0.125
- cotangent: bfloat16 [16384, 1024], P(('seq', 'head')), may hold values from -24 to 24
Outputs:
- layer_out: bfloat16 [16384, 1024], P(('seq', 'head'))
- grad_w_in: float32 [1024, 4384], P('seq')
- grad_w_out: float32 [2048, 1024], P('head', 'seq')
- grad_embedding: float32 [5, 1024], replicated
- grad_conv: float32 [4, 2304], replicated
- grad_conv_bias: float32 [2304], replicated
- grad_dt_bias: float32 [32], replicated
- grad_a_log: float32 [32], replicated
- grad_skip: float32 [32], replicated
- grad_gain: float32 [2048], replicated
Inputs may be any that keep to these rules, and one draw needn't show every extreme that they name: `base_ids`: 0 A, 1 C, 2 G, 3 T, 4 N; comp pairs A with T and C with G.
All inputs are finite; a program needn't handle non-finite values.
Results may differ from a plain program's by a relative error of at most 0.0046.
Values may be sent and summed in bfloat16 or wider, within the bound.
No kernel may reach another device: no remote copies, remote signals or barrier semaphores. Data moves between devices by JAX's collectives and lax.ppermute only.
A program may use at most 320 MiB of HBM per device.

v0:
```python
import jax
import jax.numpy as jnp
from jax import lax
from jax.sharding import PartitionSpec as P

D = 1024
HEADS = 32
HDIM = 64
STATE = 128
SPAN = 256
KCONV = 4
INNER = 2048


EPSILON = 1e-05
HIGHEST = lax.Precision.HIGHEST


def prefix(shard, axis, combine, identity, reverse):
    devices, index = (lax.axis_size(axis), lax.axis_index(axis))
    everything = jax.tree.map(lambda part: lax.all_gather(part, axis), shard)
    start = jax.tree.map(
        lambda part, zero: jnp.broadcast_to(jnp.asarray(zero, part.dtype), part.shape),
        shard,
        identity,
    )

    def step(k, before):
        at = devices - 1 - k if reverse else k
        reached = at > index if reverse else at < index
        new = combine(before, jax.tree.map(lambda part: part[at], everything))
        return jax.tree.map(lambda a, b: jnp.where(reached, a, b), new, before)

    return lax.fori_loop(0, devices, step, start)


def with_halo(shard, sides, width):
    for axis, dim in sides:
        devices, length = (lax.axis_size(axis), shard.shape[dim])
        up = [(i, (i + 1) % devices) for i in range(devices - 1)]
        down = [(j, i) for i, j in up]
        last = lax.slice_in_dim(shard, length - width, length, axis=dim)
        initial = lax.slice_in_dim(shard, 0, width, axis=dim)
        before = lax.ppermute(last, axis, up)
        after = lax.ppermute(initial, axis, down)
        shard = jnp.concatenate([before, shard, after], axis=dim)
    return shard


def complement_padded(symbols):
    return jnp.where((symbols >= 1) & (symbols <= 4), 5 - symbols, symbols)


def lookup(symbols, source):
    alphabet = jnp.arange(1, source.shape[0] + 1, dtype=jnp.int32)
    onehot = (symbols[:, None] == alphabet[None, :]).astype(jnp.float32)
    return jnp.dot(onehot, source, precision=HIGHEST)


def count_rows(symbols, values, vocab_size):
    alphabet = jnp.arange(1, vocab_size + 1, dtype=jnp.int32)
    onehot = (symbols[:, None] == alphabet[None, :]).astype(values.dtype)
    return lax.dot_general(
        onehot,
        values,
        (((0,), (0,)), ((), ())),
        precision=HIGHEST,
        preferred_element_type=jnp.float32,
    )


def silu_slope(values):
    logistic = jax.nn.sigmoid(values)
    return logistic * (1.0 + values * (1.0 - logistic))


def ssd_mixer(
    tab_x, tab_bc, tab_step, conv_x, conv_bc, bias_x, bias_bc, step_bias, log_rate, skip, symbols
):
    length = symbols.shape[0] - (KCONV - 1)
    head_count = step_bias.shape[0]
    head_width = tab_x.shape[1] // head_count
    state_size = tab_bc.shape[1] // 2
    x_values = lookup(symbols, tab_x)
    bc_values = lookup(symbols, tab_bc)
    x_conv = jnp.zeros((length, tab_x.shape[1]), jnp.float32) + bias_x[None, :]
    bc_conv = jnp.zeros((length, tab_bc.shape[1]), jnp.float32) + bias_bc[None, :]
    for tap in range(KCONV):
        x_conv = x_conv + conv_x[tap][None, :] * x_values[tap : tap + length]
        bc_conv = bc_conv + conv_bc[tap][None, :] * bc_values[tap : tap + length]
    x_act = jax.nn.silu(x_conv)
    bc_act = jax.nn.silu(bc_conv)
    b_rows = bc_act[:, :state_size]
    c_rows = bc_act[:, state_size:]
    step_size = jax.nn.softplus(lookup(symbols[KCONV - 1 :], tab_step) + step_bias[None, :])
    log_decay = -(jnp.exp(log_rate)[None, :] * step_size)
    block_count = length // SPAN
    x_blocks = x_act.reshape(block_count, SPAN, head_count, head_width)
    decay_blocks = log_decay.T.reshape(head_count, block_count, SPAN).transpose(1, 0, 2)
    step_blocks = step_size.T.reshape(head_count, block_count, SPAN).transpose(1, 0, 2)
    b_blocks = b_rows.reshape(block_count, SPAN, state_size)
    c_blocks = c_rows.reshape(block_count, SPAN, state_size)
    causal = jnp.arange(SPAN)[:, None] >= jnp.arange(SPAN)[None, :]

    def block_step(carry, block):
        carry_state, offset = carry
        x_block, log_block, step_block, b_block, c_block = block
        cumulative = jnp.cumsum(log_block, axis=1)
        differences = cumulative[:, :, None] - cumulative[:, None, :]
        decays = jnp.where(causal[None], jnp.exp(jnp.where(causal[None], differences, 0.0)), 0.0)
        intersection = jnp.dot(c_block, b_block.T, precision=HIGHEST)
        scores = intersection[None] * decays * step_block[:, None, :]
        within = jnp.einsum("hts,shd->thd", scores, x_block, precision=HIGHEST)
        carried = (
            jnp.einsum("tn,hnd->thd", c_block, carry_state, precision=HIGHEST)
            * jnp.exp(cumulative).T[:, :, None]
        )
        tail_weight = jnp.exp(cumulative[:, -1:] - cumulative) * step_block
        new_state = jnp.exp(cumulative[:, -1])[:, None, None] * carry_state + jnp.einsum(
            "sn,hs,shd->hnd", b_block, tail_weight, x_block, precision=HIGHEST
        )
        return (
            (new_state, offset + cumulative[:, -1]),
            (within + carried, offset[:, None] + cumulative),
        )

    start_carry = (
        jnp.zeros((head_count, state_size, head_width), jnp.float32),
        jnp.zeros((head_count,), jnp.float32),
    )
    (final_state, log_total), (outputs, cumulatives) = lax.scan(
        block_step, start_carry, (x_blocks, decay_blocks, step_blocks, b_blocks, c_blocks)
    )
    result = outputs.reshape(length, head_count, head_width) + skip[None, :, None] * x_act.reshape(
        length, head_count, head_width
    )
    cumul_all = cumulatives.transpose(1, 0, 2).reshape(head_count, length)
    return (
        result.reshape(length, head_count * head_width),
        log_total,
        final_state,
        cumul_all,
        c_rows,
    )


def add_carried(within, cumul_all, c_rows, carried):
    length = within.shape[0]
    extra = (
        jnp.einsum("tn,hnd->thd", c_rows, carried, precision=HIGHEST)
        * jnp.exp(cumul_all).T[:, :, None]
    )
    return within + extra.reshape(length, -1)


def combine(earlier, later):
    return (earlier[0] * later[0], later[0][:, None, None] * earlier[1] + later[1])


def chain_up(pair, identity):
    return prefix(pair, "seq", combine, identity, False)[1]


def chain_down(pair, identity):
    return prefix(pair, "seq", combine, identity, True)[1]


def gate_norm(values, gate):
    gated = values.astype(jnp.float32) * jax.nn.silu(gate)
    scale = lax.rsqrt(jnp.mean(gated * gated, axis=1) + EPSILON)
    return (gated, scale)


def norm_back(slope, gated, scale, gain, total):
    return (
        gain[None, :] * scale[:, None] * slope
        - (scale * scale * scale * total / INNER)[:, None] * gated
    )


def body(
    base_ids,
    embedding,
    in_weight,
    conv_weight,
    conv_bias,
    dt_bias,
    a_log,
    skip_weight,
    norm_gain,
    out_weight,
    cotangent,
):
    groups = lax.axis_size("head")
    local_heads = HEADS // groups
    local_width = local_heads * HDIM
    head_rank = lax.axis_index("head")
    seq_rank = lax.axis_index("seq")
    length = base_ids.shape[0]
    token_rows = length // groups
    vocab_size = embedding.shape[0]
    lookup_table = jnp.dot(embedding, in_weight, preferred_element_type=jnp.float32)
    symbols = base_ids + 1
    rimmed = with_halo(symbols, (("seq", 0),), KCONV - 1)
    forward_symbols = rimmed[: length + KCONV - 1]
    mirror_symbols = jnp.flip(complement_padded(rimmed))[: length + KCONV - 1]
    column_start = head_rank * local_width
    head_start = head_rank * local_heads
    params = (
        lax.dynamic_slice_in_dim(lookup_table, INNER + column_start, local_width, 1),
        lookup_table[:, 2 * INNER : 2 * INNER + 2 * STATE],
        lax.dynamic_slice_in_dim(lookup_table, 2 * INNER + 2 * STATE + head_start, local_heads, 1),
        lax.dynamic_slice_in_dim(conv_weight, column_start, local_width, 1),
        conv_weight[:, INNER:],
        lax.dynamic_slice_in_dim(conv_bias, column_start, local_width, 0),
        conv_bias[INNER:],
        lax.dynamic_slice_in_dim(dt_bias, head_start, local_heads, 0),
        lax.dynamic_slice_in_dim(a_log, head_start, local_heads, 0),
        lax.dynamic_slice_in_dim(skip_weight, head_start, local_heads, 0),
    )
    fwd_parts, fwd_backward = jax.vjp(lambda values: ssd_mixer(*values, forward_symbols), params)
    rev_parts, rev_backward = jax.vjp(lambda values: ssd_mixer(*values, mirror_symbols), params)
    fwd_within, fwd_total, fwd_state, fwd_cumul, fwd_crows = fwd_parts
    rev_within, rev_total, rev_state, rev_cumul, rev_crows = rev_parts
    fwd_decay = jnp.exp(fwd_total)
    rev_decay = jnp.exp(rev_total)
    identity = (
        jnp.ones((local_heads,), jnp.float32),
        jnp.zeros((local_heads, STATE, HDIM), jnp.float32),
    )
    fwd_carried = chain_up((fwd_decay, fwd_state), identity)
    rev_carried = chain_down((rev_decay, rev_state), identity)
    fwd_full, fwd_extra = jax.vjp(add_carried, fwd_within, fwd_cumul, fwd_crows, fwd_carried)
    rev_flipped, rev_extra = jax.vjp(add_carried, rev_within, rev_cumul, rev_crows, rev_carried)
    rev_values = jnp.flip(rev_flipped, 0)
    token_symbols = lax.dynamic_slice_in_dim(symbols, head_rank * token_rows, token_rows, 0)
    residual_rows = lookup(token_symbols, embedding.astype(jnp.float32))
    embed_grad = count_rows(token_symbols, cotangent, vocab_size)
    fwd_tokens, rev_tokens = (
        lax.all_to_all(fwd_full, "head", split_axis=0, concat_axis=1, tiled=True),
        lax.all_to_all(rev_values, "head", split_axis=0, concat_axis=1, tiled=True),
    )
    gate_table = lookup_table[:, :INNER]
    mirror_tokens = complement_padded(token_symbols)
    fwd_gate = lookup(token_symbols, gate_table)
    rev_gate = lookup(mirror_tokens, gate_table)
    fwd_gated, fwd_scale = gate_norm(fwd_tokens, fwd_gate)
    rev_gated, rev_scale = gate_norm(rev_tokens, rev_gate)
    normed = (
        fwd_gated * fwd_scale[:, None] * norm_gain[None, :]
        + rev_gated * rev_scale[:, None] * norm_gain[None, :]
    )
    mixed_sum = normed.astype(jnp.bfloat16)
    layer_out = (
        residual_rows + jnp.dot(mixed_sum, out_weight, preferred_element_type=jnp.float32)
    ).astype(jnp.bfloat16)
    slope = lax.dot_general(
        cotangent, out_weight, (((1,), (1,)), ((), ())), preferred_element_type=jnp.float32
    )
    rows_part = lax.psum_scatter(
        lax.dot_general(
            cotangent, mixed_sum, (((0,), (0,)), ((), ())), preferred_element_type=jnp.float32
        ),
        "seq",
        scatter_dimension=0,
        tiled=True,
    )
    grad_w_out = lax.psum_scatter(rows_part, "head", scatter_dimension=1, tiled=True).T
    gain_grad = jnp.sum(
        slope * (fwd_gated * fwd_scale[:, None] + rev_gated * rev_scale[:, None]), axis=0
    )
    fwd_dg = norm_back(
        slope,
        fwd_gated,
        fwd_scale,
        norm_gain,
        jnp.sum(slope * norm_gain[None, :] * fwd_gated, axis=1),
    )
    rev_dg = norm_back(
        slope,
        rev_gated,
        rev_scale,
        norm_gain,
        jnp.sum(slope * norm_gain[None, :] * rev_gated, axis=1),
    )
    fwd_dy = fwd_dg * jax.nn.silu(fwd_gate)
    rev_dy = rev_dg * jax.nn.silu(rev_gate)
    gate_grad = count_rows(
        token_symbols, fwd_dg * fwd_tokens * silu_slope(fwd_gate), vocab_size
    ) + count_rows(mirror_tokens, rev_dg * rev_tokens * silu_slope(rev_gate), vocab_size)
    fwd_back, rev_back = (
        lax.all_to_all(fwd_dy, "head", split_axis=1, concat_axis=0, tiled=True),
        lax.all_to_all(rev_dy, "head", split_axis=1, concat_axis=0, tiled=True),
    )
    rev_cot = jnp.flip(rev_back, 0)
    unused_fwd, fwd_dcumul, fwd_dcrows, fwd_pull = fwd_extra(fwd_back)
    unused_rev, rev_dcumul, rev_dcrows, rev_pull = rev_extra(rev_cot)
    fwd_ahead = chain_down((fwd_decay, fwd_pull), identity)
    rev_ahead = chain_up((rev_decay, rev_pull), identity)
    fwd_dtotal = jnp.sum(fwd_ahead * fwd_carried, axis=(1, 2)) * fwd_decay
    rev_dtotal = jnp.sum(rev_ahead * rev_carried, axis=(1, 2)) * rev_decay
    fwd_grads = fwd_backward((fwd_back, fwd_dtotal, fwd_ahead, fwd_dcumul, fwd_dcrows))[0]
    rev_grads = rev_backward((rev_cot, rev_dtotal, rev_ahead, rev_dcumul, rev_dcrows))[0]
    merged = jax.tree.map(
        lambda first_part, second_part: first_part + second_part, fwd_grads, rev_grads
    )
    (
        tab_x_grad,
        tab_bc_grad,
        tab_step_grad,
        conv_x_grad,
        conv_bc_grad,
        bias_x_grad,
        bias_bc_grad,
        step_bias_grad,
        log_rate_grad,
        skip_grad,
    ) = merged
    x_block = lax.dynamic_update_slice_in_dim(
        jnp.zeros((vocab_size, INNER), jnp.float32), tab_x_grad, column_start, 1
    )
    step_block = lax.dynamic_update_slice_in_dim(
        jnp.zeros((vocab_size, HEADS), jnp.float32), tab_step_grad, head_start, 1
    )
    table_grad = jnp.concatenate([gate_grad, x_block, tab_bc_grad, step_block], axis=1)
    conv_grad = jnp.concatenate(
        [
            lax.dynamic_update_slice_in_dim(
                jnp.zeros((KCONV, INNER), jnp.float32), conv_x_grad, column_start, 1
            ),
            conv_bc_grad,
        ],
        axis=1,
    )
    bias_grad = jnp.concatenate(
        [
            lax.dynamic_update_slice_in_dim(
                jnp.zeros((INNER,), jnp.float32), bias_x_grad, column_start, 0
            ),
            bias_bc_grad,
        ]
    )

    def place_heads(values):
        return lax.dynamic_update_slice_in_dim(
            jnp.zeros((HEADS,), jnp.float32), values, head_start, 0
        )

    totals = lax.psum(
        (
            table_grad,
            conv_grad,
            bias_grad,
            place_heads(step_bias_grad),
            place_heads(log_rate_grad),
            place_heads(skip_grad),
            gain_grad,
            embed_grad,
        ),
        ("seq", "head"),
    )
    (
        table_sum,
        grad_conv,
        grad_conv_bias,
        grad_dt_bias,
        grad_a_log,
        grad_skip,
        grad_gain,
        cot_counts,
    ) = totals
    row_count = D // lax.axis_size("seq")
    embed_columns = lax.dynamic_slice_in_dim(embedding, seq_rank * row_count, row_count, 1).astype(
        jnp.float32
    )
    grad_w_in = lax.dot_general(
        embed_columns, table_sum, (((0,), (0,)), ((), ())), precision=HIGHEST
    )
    grad_embedding = (
        lax.dot_general(
            table_sum, in_weight.astype(jnp.float32), (((1,), (1,)), ((), ())), precision=HIGHEST
        )
        + cot_counts
    )
    return (
        layer_out,
        grad_w_in,
        grad_w_out,
        grad_embedding,
        grad_conv,
        grad_conv_bias,
        grad_dt_bias,
        grad_a_log,
        grad_skip,
        grad_gain,
    )


def solution(mesh):
    return jax.shard_map(
        body,
        mesh=mesh,
        in_specs=(P("seq"), P(), P(), P(), P(), P(), P(), P(), P(), P(), P(("seq", "head"), None)),
        out_specs=(
            P(("seq", "head"), None),
            P("seq", None),
            P("head", "seq"),
            P(),
            P(),
            P(),
            P(),
            P(),
            P(),
            P(),
        ),
        check_vma=False,
    )
```

profile of v0, /device:TPU:0, one launch (start us, length us, event | category | flops | bytes accessed | tf_op | source)
XLA Modules:
  0.0 1649.6 jit_solution(7303677710969053059)
XLA Ops:
  13.6 6.0 fusion.440
  72.9 104.6 %while.229 = (s32[]{:T(128)}, f32[4,128,64]{1,2,0:T(8,128)}, f32[4]{0:T(128)}, f32[4,256,4,64]{1,3,2,0:T(8,128)}, f32[4,4,256]{2,1,0:T(4,128)}, /*index=5*/f32[4...) while((s32[]{:T(128)}, f32[4,128,64]{1,2,0:T(8,128)}, ...), condition=%wide.region_10.12_spmd.clone.clone, body=%wide.region_7.11_spmd.clone.clone.sunk | while | flops 506435616 | bytes 10521084 | solution.py:131
  198.1 105.1 %while.228 = (s32[]{:T(128)}, f32[4,128,64]{1,2,0:T(8,128)}, f32[4]{0:T(128)}, f32[4,256,4,64]{1,3,2,0:T(8,128)}, f32[4,4,256]{2,1,0:T(4,128)}, /*index=5*/f32[4...) while((s32[]{:T(128)}, f32[4,128,64]{1,2,0:T(8,128)}, ...), condition=%wide.region_3.5_spmd.clone.clone, body=%wide.region_0.4_spmd.clone.clone.sunk | while | flops 506435616 | bytes 10521084 | solution.py:131
  304.6 33.5 %all-reduce.45 = (f32[64]{0:T(128)S(1)}, f32[64]{0:T(128)S(1)}) all-reduce(f32[64]{0:T(128)S(1)} %exponential_dynamic-update-slice_fusion, f32[64]{0:T(128)S(1)} %exponential_dynamic-update-slice_fusion.1), channel_id=4, replica_groups=mesh['seq'=16,'head'=8] {'seq'}, use_global_device_ids=true, to_apply=%add.43 | all-reduce | flops 128 | bytes 1024
  353.4 93.4 %while.225 = (s32[]{:T(128)}, f32[4,128,64]{2,1,0:T(8,128)}, s32[]{:T(128)}, f32[16,4]{1,0:T(8,128)}, f32[16,4,128,64]{2,3,1,0:T(8,128)}, /*index=5*/s32[]{:T(128)}, s32[]{:T(128)}, s32[]{:T(128)}, s32[]{:T(128)}) while((s32[]{:T(128)}, f32[4,128,64]{2,1,0:T(8,128)}, s32[]{:T(128)}, f32[16,4]{1,0:T(8,128)}, ...), condition=%wide.region_12.14_spmd.clone, body=%wide.region_11.13_spmd.clone.sunk | while | flops 131080 | bytes 917719 | solution.py:34
  455.3 93.3 %while.224 = (s32[]{:T(128)}, f32[4,128,64]{2,1,0:T(8,128)}, s32[]{:T(128)}, f32[16,4]{1,0:T(8,128)}, f32[16,4,128,64]{2,3,1,0:T(8,128)}, /*index=5*/s32[]{:T(128)}, s32[]{:T(128)}) while((s32[]{:T(128)}, f32[4,128,64]{2,1,0:T(8,128)}, s32[]{:T(128)}, f32[16,4]{1,0:T(8,128)}, f32[16,4,128,64]{2,3,1,0:T(8,128)}, ...), condition=%wide.region_5.7_spmd.clone, body=%wide.region_4.6_spmd.clone.sunk | while | flops 131076 | bytes 917657 | solution.py:34
  562.7 8.9 rev.9
  571.5 22.0 %all_to_all.73 = f32[8,128,256]{2,1,0:T(8,128)} all-to-all(f32[8,128,256]{2,1,0:T(8,128)} %bitcast.1071), channel_id=1, replica_groups=mesh['seq'=16,'head'=8] {'head'}, dimensions={0} | all-to-all | bytes 2097152 | tf_op jit(solution)/shard_map/all_to_all | solution.py:241
  606.7 5.5 all-to-all-done
  613.5 5.4 multiply_reduce_fusion.21
  622.4 16.9 %all_to_all.74 = f32[128,8,256]{2,0,1:T(8,128)} all-to-all(f32[128,8,256]{2,0,1:T(8,128)S(1)} %bitcast.1072), channel_id=1, replica_groups=mesh['seq'=16,'head'=8] {'head'}, dimensions={1} | all-to-all | bytes 2097152 | tf_op jit(solution)/shard_map/all_to_all | solution.py:293
  639.3 8.9 rev.10
  656.3 18.2 %all_to_all.75 = f32[128,8,256]{0,2,1:T(8,128)S(1)} all-to-all(f32[128,8,256]{0,2,1:T(8,128)} %bitcast.1074), channel_id=1, replica_groups=mesh['seq'=16,'head'=8] {'head'}, dimensions={1} | all-to-all | bytes 2097152 | tf_op jit(solution)/shard_map/all_to_all | solution.py:292
  686.8 5.7 convolution_bitcast_fusion.12
  692.6 9.2 copy.296
  725.3 80.3 %while.227 = (s32[]{:T(128)}, f32[4,128,64]{2,1,0:T(8,128)}, s32[]{:T(128)}, f32[16,4]{1,0:T(8,128)}, f32[16,4,128,64]{2,3,1,0:T(8,128)}, /*index=5*/s32[]{:T(128)}, s32[]{:T(128)}) while((s32[]{:T(128)}, f32[4,128,64]{2,1,0:T(8,128)}, s32[]{:T(128)}, f32[16,4]{1,0:T(8,128)}, f32[16,4,128,64]{2,3,1,0:T(8,128)}, ...), condition=%wide.region_33.35_spmd.clone, body=%wide.region_32.34_spmd.clone.sunk | while | flops 131076 | bytes 917657 | solution.py:34
  808.5 79.8 %while.226 = (s32[]{:T(128)}, f32[4,128,64]{2,1,0:T(8,128)}, s32[]{:T(128)}, f32[16,4]{1,0:T(8,128)}, f32[16,4,128,64]{2,3,1,0:T(8,128)}, /*index=5*/s32[]{:T(128)}, s32[]{:T(128)}, s32[]{:T(128)}, s32[]{:T(128)}) while((s32[]{:T(128)}, f32[4,128,64]{2,1,0:T(8,128)}, s32[]{:T(128)}, f32[16,4]{1,0:T(8,128)}, ...), condition=%wide.region_17.19_spmd.clone, body=%wide.region_16.18_spmd.clone.sunk | while | flops 131080 | bytes 917719 | solution.py:34
  896.2 154.7 %while.223 = (s32[]{:T(128)}, f32[4,128,64]{1,2,0:T(8,128)}, f32[4]{0:T(128)}, f32[4,256,4,64]{1,3,2,0:T(8,128)}, f32[4,4,256]{2,1,0:T(4,128)}, /*index=5*/f32[4...) while((s32[]{:T(128)}, f32[4,128,64]{1,2,0:T(8,128)}, ...), condition=%wide.region_47.49_spmd.clone.clone, body=%wide.region_36.48_spmd.clone.clone.sunk | while | flops 1010316288 | bytes 11387949 | solution.py:131
  912.0 5.0 reduce-window.98
  950.8 5.0 reduce-window.98
  989.4 5.0 reduce-window.98
  1028.0 5.0 reduce-window.98
  1061.5 166.4 %while.222 = (s32[]{:T(128)}, f32[4,128,64]{1,2,0:T(8,128)}, f32[4]{0:T(128)}, f32[4,256,4,64]{1,3,2,0:T(8,128)}, f32[4,4,256]{2,1,0:T(4,128)}, /*index=5*/f32[4...) while((s32[]{:T(128)}, f32[4,128,64]{1,2,0:T(8,128)}, ...), condition=%wide.region_31.33_spmd.clone.clone, body=%wide.region_20.32_spmd.clone.clone.sunk | while | flops 1010316288 | bytes 13482125 | solution.py:131
  1081.3 5.0 reduce-window.96
  1122.9 5.0 reduce-window.96
  1164.4 5.0 reduce-window.96
  1205.9 5.0 reduce-window.96
  1233.9 6.3 multiply_reduce_fusion.14
  1272.5 145.0 %all-reduce.49.cloned.1.call-done = f32[5,4384]{1,0:T(8,128)} async-done(((f32[5,4384]{1,0:T(8,128)}), f32[5,4384]{1,0:T(8,128)}) %all-reduce.49.cloned.1.call-update) | async-done | bytes 87696 | tf_op jit(solution)/shard_map/psum | solution.py:349
  1420.2 143.7 %all-reduce.51.cloned.1.call-done = (f32[5,1024]{1,0:T(8,128)}, f32[4,2304]{1,0:T(4,128)}, f32[2304]{0:T(1024)}, f32[32]{0:T(128)}, f32[32]{0:T(128)}, /*index=5*/f32[32]{0:T(128)}, f32[2048]{0:T(1024)}) async-done(((f32[5,1024]{1,0:T(8,128)}, f32[4,2304]{1,0:T(4,128)}, f32[2304]{0:T(1024)}, f32[32]{0:T(128)}, f32[32]{0:T(128)}, /*index=5*/f32[32]{0:T(128)}, f32[2048]{0:T(1024)}), (f32[5,1024]{1,0:T(8,128)}, ...) | async-done | bytes 75152 | tf_op jit(solution)/shard_map/psum | solution.py:349
  1563.9 7.8 convolution_add_fusion.6
  1571.7 65.7 %reduce-scatter.5.cloned.1.call-done = f32[64,256]{0,1:T(8,128)} async-done(((f32[64,2048]{0,1:T(8,128)}), f32[64,256]{0,1:T(8,128)}) %reduce-scatter.5.cloned.1.call-update) | async-done | bytes 65552 | tf_op jit(solution)/shard_map/reduce_scatter | solution.py:268
  (1232 shorter events, 1083.0 us)
Async XLA Ops:
  7.2 606.3 %copy-start = (bf16[128,1024]{1,0:T(8,128)(2,1)S(1)}, bf16[128,1024]{1,0:T(8,128)(2,1)}, u32[]{:S(2)}) copy-start(bf16[128,1024]{1,0:T(8,128)(2,1)} %param.38) | copy-start | bytes 786436
  7.2 346.2 %all-gather.13.cloned.1.call-start = ((), (), s32[]{:S(2)}) async-start(), calls=%async_computation.9 | async-start | bytes 2228224 | tf_op jit(solution)/shard_map/all_gather | solution.py:21
  8.0 18.7 %copy-start.51 = (s32[1024]{0:T(1024)}, s32[1024]{0:T(1024)S(1)}, u32[]{:S(2)}) copy-start(s32[1024]{0:T(1024)S(1)} %broadcast_add_fusion.4) | copy-start | bytes 12292
  8.0 16.9 %collective-permute-start = (s32[3]{0:T(128)S(1)}, s32[3]{0:T(128)S(1)}, u32[]{:S(2)}, u32[]{:S(2)}) collective-permute-start(s32[3]{0:T(128)S(1)} %get-tuple-element.4155), channel_id=1, source_target_pairs={{0,8},{8,16},{16,24},{24,32},{32,40},{40,48},{48,56},{56,64},{64,7... | collective-permute-start | bytes 44 | tf_op jit(solution)/shard_map/ppermute | solution.py:44
  9.3 15.6 collective-permute-start.1
  10.6 39.9 %copy-start.43 = (s32[5]{0:T(128)}, s32[5]{0:T(128)S(1)}, u32[]{:S(2)}) copy-start(s32[5]{0:T(128)S(1)} %iota_add_fusion) | copy-start | bytes 64
  23.8 13.9 copy-start.59
  23.8 13.9 copy-start.61
  23.8 13.9 copy-start.63
  23.8 13.9 copy-start.65
  177.5 277.8 %all-gather.11.cloned.1.call-start = ((), (), s32[]{:S(2)}) async-start(), calls=%async_computation.8 | async-start | bytes 2228224 | tf_op jit(solution)/shard_map/all_gather | solution.py:21
  339.5 384.0 %copy-start.29 = (f32[4,4,256]{2,1,0:T(4,128)}, f32[4,4,256]{2,1,0:T(4,128)S(1)}, u32[]{:S(2)}) copy-start(f32[4,4,256]{2,1,0:T(4,128)S(1)} %exp.285) | copy-start | bytes 49156
  593.5 20.0 %copy-start.40 = (f32[2048]{0:T(1024)S(1)}, f32[2048]{0:T(1024)}, u32[]{:S(2)}) copy-start(f32[2048]{0:T(1024)} %param.36) | copy-start | bytes 24580
  593.5 18.6 %all-to-all-start = ((f32[8,128,256]{2,1,0:T(8,128)}), f32[8,128,256]{2,1,0:T(8,128)}, u32[]{:S(2)}, u32[]{:S(2)}) async-start(f32[8,128,256]{2,1,0:T(8,128)} %bitcast.1068), calls=%async_computation | async-start | bytes 2097152 | tf_op jit(solution)/shard_map/all_to_all | solution.py:240
  597.9 127.5 %all-gather.17.cloned.1.call-start = ((), (), s32[]{:S(2)}) async-start(), calls=%async_computation.11 | async-start | bytes 2228224 | tf_op jit(solution)/shard_map/all_gather | solution.py:21
  653.7 154.8 %all-gather.15.cloned.1.call-start = ((), (), s32[]{:S(2)}) async-start(), calls=%async_computation.10 | async-start | bytes 2228224 | tf_op jit(solution)/shard_map/all_gather | solution.py:21
  682.7 583.8 %reduce-scatter.7.cloned.1.call-start = ((), (), s32[]{:S(2)}) async-start(), calls=%async_computation.12 | async-start | bytes 8912896
  706.6 710.9 %all-reduce.49.cloned.1.call-start = ((), (), s32[]{:S(2)}) async-start(), calls=%async_computation.6 | async-start | bytes 286720 | tf_op jit(solution)/shard_map/psum | solution.py:349
  808.5 83.1 %copy-start.57 = (f32[4]{0:T(128)S(1)}, f32[4]{0:T(128)}, u32[]{:S(2)}) copy-start(f32[4]{0:T(128)} %get-tuple-element.2454) | copy-start | bytes 52
  1086.7 12.7 copy-start.4
  1128.3 12.7 copy-start.4
  1169.8 12.6 copy-start.4
  1211.3 12.7 copy-start.4
  1264.9 298.9 %all-reduce.51.cloned.1.call-start = ((), (), s32[]{:S(2)}) async-start(), calls=%async_computation.13 | async-start | bytes 183296 | tf_op jit(solution)/shard_map/psum | solution.py:349
  1266.1 371.2 %reduce-scatter.5.cloned.1.call-start = ((), (), s32[]{:S(2)}) async-start(), calls=%async_computation.7 | async-start | bytes 1179648 | tf_op jit(solution)/shard_map/reduce_scatter | solution.py:268
  1563.8 75.1 %copy-start.53 = (f32[4,2304]{1,0:T(4,128)S(1)}, f32[4,2304]{1,0:T(4,128)}, u32[]{:S(2)}) copy-start(f32[4,2304]{1,0:T(4,128)} %get-tuple-element.5608) | copy-start | bytes 110596
  1563.8 75.8 %copy-start.58 = (f32[2304]{0:T(1024)S(1)}, f32[2304]{0:T(1024)}, u32[]{:S(2)}) copy-start(f32[2304]{0:T(1024)} %get-tuple-element.5609) | copy-start | bytes 27652
  1563.8 76.4 %copy-start.107 = (f32[32]{0:T(128)S(1)}, f32[32]{0:T(128)}, u32[]{:S(2)}) copy-start(f32[32]{0:T(128)} %get-tuple-element.5610) | copy-start | bytes 388
  1563.8 76.9 %copy-start.106 = (f32[32]{0:T(128)S(1)}, f32[32]{0:T(128)}, u32[]{:S(2)}) copy-start(f32[32]{0:T(128)} %get-tuple-element.5611) | copy-start | bytes 388
  1563.8 77.4 %copy-start.105 = (f32[32]{0:T(128)S(1)}, f32[32]{0:T(128)}, u32[]{:S(2)}) copy-start(f32[32]{0:T(128)} %get-tuple-element.5612) | copy-start | bytes 388
  1563.8 77.9 %copy-start.80 = (f32[2048]{0:T(1024)S(1)}, f32[2048]{0:T(1024)}, u32[]{:S(2)}) copy-start(f32[2048]{0:T(1024)} %get-tuple-element.5613) | copy-start | bytes 24580
  1563.8 78.5 %copy-start.1 = (bf16[128,1024]{1,0:T(8,128)(2,1)S(1)}, bf16[128,1024]{1,0:T(8,128)(2,1)}, u32[]{:S(2)}) copy-start(bf16[128,1024]{1,0:T(8,128)(2,1)} %param.38) | copy-start | bytes 786436
  (111 other events, 458.3 us)
Sparse Core Ops, SparseCore 0:
  177.7 39.6 all-gather.12
  353.5 32.8 all-gather.10
  653.9 37.7 all-gather.16
  693.2 35.6 all-gather.14
  731.2 74.8 reduce-scatter.6
  1265.0 152.4 all-reduce.48
  1425.7 138.0 all-reduce.50
  1567.4 69.8 reduce-scatter.4
where the time goes:
time: 1670 us; the launch traced here: 1650 us
  local copies, waits for them, and re-layouts  550 us (33%)
  waiting for transfers between devices  360 us (22%)
  other arithmetic  339 us (20%)
  matrix products  284 us (17%)
  blocking collectives  90.6 us (5%)
    psum x2, waiting for transfers between devices, body(): lax.psum((table_grad, conv_grad, bias_grad, place_heads(step_bias_grad),...  289 us
    dynamic_slice x128, local copies, waits for them, and re-layouts, step(): new = combine(before, jax.tree.map(lambda part: part[at], everything))  189 us
    select_n x64, other arithmetic, step(): return jax.tree.map(lambda a, b: jnp.where(reached, a, b), new, before)  113 us
    dot_general x24, matrix products, block_step(): within = jnp.einsum('hts,shd->thd', scores, x_block, precision=HIGHEST)  78.5 us
    reduce_scatter x1, waiting for transfers between devices, body(): lax.psum_scatter(rows_part, 'head', scatter_dimension=1, tiled=True)  65.7 us
    dynamic_update_slice x40, other arithmetic, ssd_mixer(): lax.scan(block_step, start_carry, (x_blocks, decay_blocks, step_blocks, b...  62.5 us
    another operation x137, local copies, waits for them, and re-layouts  53.4 us
    another operation x48, other arithmetic  51.8 us
  transfers between devices with their start and end apart: 11, of which 4 were waited for; matrix products, arithmetic and copies ran while one was open for 52% of the time, Pallas kernels for 0%

commit v1 on v0

v1 whole, which is shorter than its diff:
```python
import jax
import jax.numpy as jnp
import numpy as np
from jax import lax
from jax.experimental import pallas as pl
from jax.experimental.pallas import tpu as pltpu
from jax.sharding import PartitionSpec as P

D = 1024
HEADS = 32
HDIM = 64
STATE = 128
BLOCK = 256
KCONV = 4
INNER = 2048
EPSILON = 1e-05

f32 = jnp.float32
bf16 = jnp.bfloat16
NN = (((1,), (0,)), ((), ()))
NT = (((1,), (1,)), ((), ()))
TN = (((0,), (0,)), ((), ()))

CODES = 32


def _decode_codes():
    first = np.zeros((CODES,), np.int32)
    second = np.zeros((CODES,), np.int32)
    for code in range(25):
        first[code], second[code] = code // 5 + 1, code % 5 + 1
    for code in range(25, 30):
        second[code] = code - 24
    return first, second


def _gram_onehot():
    first, second = _decode_codes()
    early, late = np.divmod(np.arange(CODES * CODES), CODES)
    symbols = (first[early], second[early], first[late], second[late])
    rows = np.zeros((CODES * CODES, 128), np.float32)
    for tap, symbol in enumerate(symbols):
        valid = symbol > 0
        rows[np.arange(CODES * CODES)[valid], (8 * tap + symbol)[valid]] = 1.0
    rows[:, 6] = 1.0
    rows[:, 64:96] = rows[:, :32]
    return rows


def encode(earlier, later):
    return jnp.where(
        earlier > 0, (earlier - 1) * 5 + later - 1, jnp.where(later > 0, 24 + later, 30)
    )


def complement_padded(symbols):
    return jnp.where((symbols >= 1) & (symbols <= 4), 5 - symbols, symbols)


def halves(values):
    high = values.astype(bf16)
    return high, (values - high.astype(f32)).astype(bf16)


def dot1(a, b, dims=NN):
    return lax.dot_general(a.astype(bf16), b.astype(bf16), dims, preferred_element_type=f32)


def dot2(a, b, dims=NN):
    high, low = halves(b)
    a = a.astype(bf16)
    return dot1(a, high, dims) + dot1(a, low, dims)


def dot2l(a, b, dims=NN):
    high, low = halves(a)
    b = b.astype(bf16)
    return dot1(high, b, dims) + dot1(low, b, dims)


def dot3(a, b, dims=NN):
    a_high, a_low = halves(a)
    b_high, b_low = halves(b)
    return dot1(a_high, b_high, dims) + (dot1(a_high, b_low, dims) + dot1(a_low, b_high, dims))


def iota(shape, axis):
    return lax.broadcasted_iota(jnp.int32, shape, axis)


def ones_where(condition):
    return jnp.where(condition, 1.0, 0.0).astype(bf16)


def expand_grams(sums):
    grams = CODES * CODES
    early = ones_where(iota((grams, CODES), 0) // CODES == iota((grams, CODES), 1))
    spread = dot2(early, sums, NT)
    mine = iota((grams, 128), 0) % CODES == iota((grams, 128), 1) % CODES
    spread = jnp.where(mine, spread, 0.0)
    widen = ones_where(iota((128, 256), 0) // CODES == iota((128, 256), 1) // HDIM)
    return dot2l(spread, widen)


def gather_grams(values):
    grams = CODES * CODES
    narrow = ones_where(iota((256, 128), 0) // HDIM == iota((256, 128), 1) // CODES)
    spread = dot2l(values, narrow)
    mine = iota((grams, 128), 0) % CODES == iota((grams, 128), 1) % CODES
    spread = jnp.where(mine, spread, 0.0)
    early = ones_where(iota((CODES, grams), 1) // CODES == iota((CODES, grams), 0))
    return dot2(early, spread)


def sigmoid(values):
    return 1.0 / (1.0 + jnp.exp(-values))


def scan_inputs(oh_ref, oht_ref, tt_ref, lx_ref, lrow_ref, rows, branch):
    onehot = oh_ref[rows, :]
    onehot_t = oht_ref[:, rows]
    before = branch * 512
    pre = dot1(onehot, tt_ref[:, before : before + 512])
    step = dot1(onehot, tt_ref[:, 1024 + branch * 256 : 1280 + branch * 256])
    row = iota((BLOCK, BLOCK), 0)
    col = iota((BLOCK, BLOCK), 1)
    lower = ones_where(row >= col)
    upper = ones_where(row <= col)
    counts = dot1(lower if branch == 0 else upper, onehot).astype(bf16)
    counts_t = dot1(onehot_t, upper if branch == 0 else lower)
    log_wide = dot1(counts, lx_ref[:, branch * 256 : branch * 256 + 256])
    log_cols = dot1(counts, lx_ref[:, 512:640])
    log_rows = dot1(lrow_ref[...], counts_t)
    return onehot_t, pre, step, counts_t, log_wide, log_cols, log_rows


def forward_kernel(
    seq_ref, ltab_ref, qs_ref, ca_ref, cb_ref, oh_ref, oht_ref, goh_ref, tt_ref, lx_ref, lrow_ref,
    skip_ref,
    y_ref, states_ref, sums_ref, decay_ref, after_ref,
    high_ref, low_ref, lhs_ref, rhs_ref, carry_ref,
):
    seq = seq_ref[0]
    first = seq * 8
    symbols = qs_ref[...]
    row = iota((128, 128), 0)
    col = iota((128, 128), 1)
    upto = ones_where(row <= col)
    every = jnp.ones((128, 128), bf16)
    signs = (jnp.where(col < row, 1.0, 0.0) - jnp.where(col < first, 1.0, 0.0)).astype(bf16)
    is_before = row < first
    logs = [jnp.zeros((128, 128), f32) for _ in range(4)]
    for symbol in range(1, 6):
        here = symbols == symbol
        found = ones_where(here)
        within = dot1(found, upto)
        total = dot1(found, every)
        upper = within + dot1(signs, total)
        after = jnp.where(is_before, -upper, upper - jnp.where(here, 1.0, 0.0))
        after_ref[symbol - 1] = after
        for h in range(4):
            logs[h] = logs[h] + after * ltab_ref[h, symbol]
    for h in range(4):
        decay = jnp.where(symbols > 0, jnp.exp(logs[h]), 0.0)
        decay_ref[h] = decay
        high = decay.astype(bf16).astype(f32)
        high_ref[h] = high
        low_ref[h] = decay - high
    codes = iota((CODES, 128), 0)

    def add_shard(shard, total):
        at = pl.ds(pl.multiple_of(shard * 8, 8), 8)
        early = ca_ref[at, :]
        late = cb_ref[at, :]
        for j in range(8):
            cols = slice(128 * j, 128 * j + 128)
            rhs_ref[:, cols] = ones_where(early[j : j + 1] == codes)
            mine = late[j : j + 1] == codes
            for h in range(4):
                lhs_ref[32 * h : 32 * h + 32, cols] = jnp.where(
                    mine, high_ref[h, at, :][j : j + 1], 0.0
                ).astype(bf16)
                lhs_ref[128 + 32 * h : 160 + 32 * h, cols] = jnp.where(
                    mine, low_ref[h, at, :][j : j + 1], 0.0
                ).astype(bf16)
        return total + dot1(lhs_ref[...], rhs_ref[...], NT)

    zero = jnp.zeros((256, CODES), f32)
    both = (
        lax.fori_loop(0, seq, add_shard, zero),
        lax.fori_loop(seq + 1, 16, add_shard, zero),
    )
    gram_pre = dot1(goh_ref[...], tt_ref[:, :512])
    gram_act = gram_pre * sigmoid(gram_pre)
    gram_x = gram_act[:, :256]
    gram_b = gram_act[:, 256:384]
    gram_xs = gram_x * dot1(goh_ref[...], tt_ref[:, 1024:1280])
    skip = skip_ref[...]
    row = iota((BLOCK, BLOCK), 0)
    col = iota((BLOCK, BLOCK), 1)
    for branch in range(2):
        sums = both[branch][:128] + both[branch][128:]
        sums_ref[branch] = sums
        weights = expand_grams(sums)
        carry_ref[...] = dot3(gram_b, weights * gram_xs, TN)
        causal = row >= col if branch == 0 else row <= col

        def block_step(k, unused, branch=branch, causal=causal):
            block = k if branch == 0 else 3 - k
            rows = pl.ds(pl.multiple_of(block * BLOCK, BLOCK), BLOCK)
            onehot_t, pre, step, counts_t, log_wide, log_cols, log_rows = scan_inputs(
                oh_ref, oht_ref, tt_ref, lx_ref, lrow_ref, rows, branch
            )
            act = pre * sigmoid(pre)
            x = act[:, :256]
            b = act[:, 256:384]
            c = act[:, 384:]
            xs = x * step
            state = carry_ref[...]
            states_ref[branch * 4 + block] = state
            inner = dot3(c, b, NT)
            parts = []
            for h in range(4):
                lane = branch * 4 + h
                decays = jnp.exp(
                    jnp.where(
                        causal,
                        log_cols[:, lane : lane + 1]
                        - log_rows[branch * 8 + h : branch * 8 + h + 1, :],
                        -1e30,
                    )
                )
                parts.append(dot1(inner * decays, xs[:, h * HDIM : (h + 1) * HDIM]))
            within = jnp.concatenate(parts, axis=1)
            y = within + dot3(c, state) * jnp.exp(log_wide)
            y_ref[branch, rows, :] = y + skip * x
            edge = log_wide[BLOCK - 1 :] if branch == 0 else log_wide[:1]
            carry_ref[...] = jnp.exp(edge) * state + dot3(b, jnp.exp(edge - log_wide) * xs, TN)
            return unused

        lax.fori_loop(0, 4, block_step, 0)


def slope_kernel(y_ref, oh_ref, tt_ref, cot_ref, ow_ref, gain_ref, slope_ref, sums_ref):
    slope = lax.dot_general(cot_ref[...], ow_ref[...], NT, preferred_element_type=f32)
    slope_ref[...] = slope
    weighted = slope * gain_ref[...]
    every = jnp.ones((8, 256), bf16)
    for branch in range(2):
        gate = dot1(oh_ref[...], tt_ref[:, 1536 + 256 * branch : 1792 + 256 * branch])
        g = y_ref[branch] * gate
        for kind, product in enumerate((g * g, weighted * g)):
            at = 2 * branch + kind
            sums_ref[at : at + 1, :] = dot2(every, product, NT)[:1]
    sums_ref[4:, :] = jnp.zeros((4, sums_ref.shape[1]), f32)


def mix_kernel(
    y_ref, oh_ref, oht_ref, tt_ref, slope_ref, gain_ref, cols_ref,
    mixed_ref, dy_ref, dgate_ref, dgain_ref,
):
    gain = gain_ref[...]
    slope = slope_ref[...]
    cols = cols_ref[...]
    sloped = slope * gain
    total = None
    for branch in range(2):
        gate = dot1(oh_ref[...], tt_ref[:, 1536 + 256 * branch : 1792 + 256 * branch])
        y = y_ref[branch]
        g = y * gate
        scale = cols[:, 2 * branch : 2 * branch + 1]
        weight = cols[:, 2 * branch + 1 : 2 * branch + 2]
        normed = g * scale
        total = normed if total is None else total + normed
        dg = scale * sloped - weight * g
        dy_ref[branch] = dg * gate
        lanes = oht_ref[32 * branch : 32 * branch + 32, :]
        dgate_ref[branch] = dot2(lanes, dg * y)
    mixed_ref[...] = (total * gain).astype(bf16)
    dgain_ref[...] = jnp.sum(slope * total, axis=0, keepdims=True)


def backward_kernel(
    seq_ref, ca_ref, cb_ref, oh_ref, oht_ref, goh_ref, goht_ref, tt_ref, lx_ref, lrow_ref, skip_ref,
    y_ref, states_ref, sums_ref, decay_ref, after_ref, dy_ref,
    tables_ref, steps_ref, logs_ref, skips_ref, far_ref,
    carry_ref, pulls_ref, mark_ref, found_ref,
):
    skip = skip_ref[...]
    row = iota((BLOCK, BLOCK), 0)
    col = iota((BLOCK, BLOCK), 1)
    tables_ref[...] = jnp.zeros_like(tables_ref)
    steps_ref[...] = jnp.zeros_like(steps_ref)
    logs_ref[...] = jnp.zeros_like(logs_ref)
    skips_ref[...] = jnp.zeros_like(skips_ref)
    for branch in range(2):
        causal = row <= col if branch == 0 else row >= col
        carry_ref[...] = jnp.zeros_like(carry_ref)

        def block_step(k, unused, branch=branch, causal=causal):
            block = 3 - k if branch == 0 else k
            later = jnp.minimum(block + 1, 3) if branch == 0 else jnp.maximum(block - 1, 0)
            rows = pl.ds(pl.multiple_of(block * BLOCK, BLOCK), BLOCK)
            onehot_t, pre, step, counts_t, log_wide, log_cols, log_rows = scan_inputs(
                oh_ref, oht_ref, tt_ref, lx_ref, lrow_ref, rows, branch
            )
            lanes = slice(32 * branch, 32 * branch + 32)
            onehot_t = onehot_t[lanes]
            counts_t = counts_t[lanes]
            logistic = sigmoid(pre)
            act = pre * logistic
            bend = logistic * (1.0 + pre * (1.0 - logistic))
            x = act[:, :256]
            b = act[:, 256:384]
            c = act[:, 384:]
            xs = x * step
            dy = dy_ref[branch, rows, :]
            own = y_ref[branch, rows, :] - skip * x
            state = states_ref[branch * 4 + block]
            pull = carry_ref[...]
            xs_low = xs.astype(bf16)
            dy_low = dy.astype(bf16)
            inner = dot3(b, c, NT)
            parts = []
            slopes = jnp.zeros((BLOCK, BLOCK), f32)
            for h in range(4):
                lane = branch * 4 + h
                wide = slice(h * HDIM, (h + 1) * HDIM)
                decays = jnp.exp(
                    jnp.where(
                        causal,
                        log_rows[branch * 8 + h : branch * 8 + h + 1, :]
                        - log_cols[:, lane : lane + 1],
                        -1e30,
                    )
                )
                parts.append(dot1(inner * decays, dy_low[:, wide]))
                slopes = slopes + dot1(xs_low[:, wide], dy_low[:, wide], NT) * decays
            within = jnp.concatenate(parts, axis=1)
            faded = jnp.exp(log_wide) * dy
            edge = log_wide[BLOCK - 1 :] if branch == 0 else log_wide[:1]
            tail = jnp.exp(edge - log_wide)
            db = dot1(slopes, c) + dot1(tail * xs, pull, NT)
            dc = dot1(slopes, b, TN) + dot1(faded, state, NT)
            dxs = within + tail * dot1(b, pull)
            dlog = dy_low.astype(f32) * own - xs_low.astype(f32) * dxs
            edge_count = counts_t[:, BLOCK - 1 :] if branch == 0 else counts_t[:, :1]
            ahead = jnp.sum(states_ref[branch * 4 + later] * pull, axis=0, keepdims=True)
            logs_ref[...] += dot2(counts_t, dlog) + edge_count * ahead
            carry_ref[...] = dot1(c, faded, TN) + jnp.exp(edge) * pull
            dpre = jnp.concatenate([step * dxs + skip * dy, db, dc], axis=1) * bend
            tables_ref[...] += dot2(onehot_t, dpre)
            steps_ref[...] += dot2(onehot_t, x * dxs)
            skips_ref[...] += jnp.sum(dy * x, axis=0, keepdims=True)
            return unused

        lax.fori_loop(0, 4, block_step, 0)
        pulls_ref[branch] = carry_ref[...]

    seq = seq_ref[0]
    gram_pre = dot1(goh_ref[...], tt_ref[:, :512])
    logistic = sigmoid(gram_pre)
    gram_act = gram_pre * logistic
    bend = logistic * (1.0 + gram_pre * (1.0 - logistic))
    gram_x = gram_act[:, :256]
    gram_b = gram_act[:, 256:384]
    gram_step = dot1(goh_ref[...], tt_ref[:, 1024:1280])
    gram_xs = gram_x * gram_step
    dxs = jnp.zeros((CODES * CODES, 256), f32)
    db = jnp.zeros((CODES * CODES, 128), f32)
    found = []
    for branch in range(2):
        pull = pulls_ref[branch]
        weights = expand_grams(sums_ref[branch])
        met = dot1(gram_b, pull)
        dxs = dxs + weights * met
        db = db + dot1(weights * gram_xs, pull, NT)
        found.append(gather_grams(gram_xs * met))
    dpre = jnp.concatenate([gram_step * dxs, db], axis=1) * bend[:, :384]
    gram_t = goht_ref[...]
    tables_ref[:, :384] += dot2(gram_t, dpre)
    steps_ref[...] += dot2(gram_t, gram_x * dxs)
    codes = iota((CODES, 128), 0)

    def look_up(branch):
        table_high, table_low = halves(found[branch])

        def one_shard(shard, unused):
            at = pl.ds(pl.multiple_of(shard * 8, 8), 8)
            early = ca_ref[at, :]
            late = cb_ref[at, :]
            for j in range(8):
                mark_ref[:, 128 * j : 128 * j + 128] = ones_where(early[j : j + 1] == codes)
            marks = mark_ref[...]
            looked = dot1(table_high, marks, TN) + dot1(table_low, marks, TN)
            for h in range(4):
                rows = []
                for j in range(8):
                    part = looked[32 * h : 32 * h + 32, 128 * j : 128 * j + 128]
                    mine = late[j : j + 1] == codes
                    rows.append(jnp.sum(jnp.where(mine, part, 0.0), axis=0, keepdims=True))
                found_ref[h, at, :] = jnp.concatenate(rows, axis=0)
            return unused

        return one_shard

    found_ref[...] = jnp.zeros_like(found_ref)
    lax.fori_loop(0, seq, look_up(0), 0)
    lax.fori_loop(seq + 1, 16, look_up(1), 0)
    for h in range(4):
        weighted = found_ref[h] * decay_ref[h]
        for symbol in range(5):
            far_ref[5 * h + symbol : 5 * h + symbol + 1, :] = jnp.sum(
                weighted * after_ref[symbol], axis=0, keepdims=True
            )


VMEM = pl.BlockSpec(memory_space=pltpu.VMEM)
SMEM = pl.BlockSpec(memory_space=pltpu.SMEM)


def call(kernel, outs, in_specs, scratch=()):
    return pl.pallas_call(
        kernel,
        out_shape=[jax.ShapeDtypeStruct(shape, kind) for shape, kind in outs],
        in_specs=in_specs,
        out_specs=[VMEM] * len(outs),
        scratch_shapes=list(scratch),
        compiler_params=pltpu.CompilerParams(vmem_limit_bytes=56 * 1024 * 1024),
    )


def gather(shard, axis):
    devices = lax.axis_size(axis)
    spread = jnp.broadcast_to(shard[None], (devices,) + shard.shape)
    return lax.all_to_all(spread, axis, split_axis=0, concat_axis=0, tiled=True)


def split_two(values):
    high = lax.reduce_precision(values, 8, 7)
    return high.astype(bf16), (values - high).astype(bf16)


def two_halves(table):
    high, low = split_two(table)
    return jnp.concatenate([high, low], axis=0)


def silu_slope(values):
    logistic = jax.nn.sigmoid(values)
    return logistic * (1.0 + values * (1.0 - logistic))


def body(
    base_ids, embedding, in_weight, conv_weight, conv_bias, dt_bias, a_log, skip_weight, norm_gain,
    out_weight, cotangent,
):
    groups = lax.axis_size("head")
    shards = lax.axis_size("seq")
    local_heads = HEADS // groups
    width = local_heads * HDIM
    head_rank = lax.axis_index("head")
    seq_rank = lax.axis_index("seq")
    length = base_ids.shape[0]
    token_rows = length // groups
    column_start = head_rank * width
    head_start = head_rank * local_heads

    everyone = gather(base_ids.reshape(8, 128), "seq").reshape(shards * length)
    cot_all = gather(cotangent, "head").reshape(length, D)

    def cols(array, start, size):
        return lax.dynamic_slice_in_dim(array, start, size, array.ndim - 1)

    weight_own = jnp.concatenate(
        [
            cols(in_weight, column_start, width),
            cols(in_weight, INNER + column_start, width),
            in_weight[:, 2 * INNER :],
        ],
        axis=1,
    )
    table = jnp.dot(embedding, weight_own, preferred_element_type=f32)
    tab_gate = table[:, :width]
    tab_conv = table[:, width : 2 * width + 2 * STATE]
    tab_step = cols(table[:, 2 * width + 2 * STATE :], head_start, local_heads)
    conv = jnp.concatenate([cols(conv_weight, column_start, width), conv_weight[:, INNER:]], axis=1)
    bias = jnp.concatenate([cols(conv_bias, column_start, width), conv_bias[INNER:]])
    rate = jnp.exp(cols(a_log, head_start, local_heads))
    pre_step = tab_step + cols(dt_bias, head_start, local_heads)[None, :]
    step_tab = jax.nn.softplus(pre_step)
    log_tab = -(rate[None, :] * step_tab)
    gain_own = cols(norm_gain, column_start, width)[None, :]
    skip_own = jnp.repeat(cols(skip_weight, head_start, local_heads), HDIM)[None, :]
    ow_own = lax.dynamic_slice_in_dim(out_weight, column_start, width, 0)

    def own_symbol(values, branch):
        start = 32 * branch + 25
        return jnp.pad(values, ((start, 64 - start - 5), (0, 0)))

    taps = jnp.pad(conv[:, None, :] * tab_conv[None, :, :], ((0, 0), (1, 2), (0, 0)))
    taps = taps.reshape(32, width + 2 * STATE)
    taps = taps + jnp.pad(bias[None, :], ((6, 25), (0, 0)))
    step_wide = jnp.repeat(step_tab, HDIM, axis=1)
    log_wide = jnp.repeat(log_tab, HDIM, axis=1)
    gate_act = jax.nn.silu(tab_gate)
    big = jnp.concatenate(
        [
            jnp.pad(taps, ((0, 32), (0, 0))),
            jnp.pad(taps, ((32, 0), (0, 0))),
            own_symbol(step_wide, 0),
            own_symbol(step_wide, 1),
            own_symbol(gate_act, 0),
            own_symbol(gate_act, 1),
        ],
        axis=1,
    )
    big = two_halves(big)
    log_cols = jnp.concatenate([own_symbol(log_tab, 0), own_symbol(log_tab, 1)], axis=1)
    log_cols = jnp.pad(log_cols, ((0, 0), (0, 120)))
    logs = two_halves(
        jnp.concatenate([own_symbol(log_wide, 0), own_symbol(log_wide, 1), log_cols], axis=1)
    )
    log_rows = jnp.concatenate(
        [
            jnp.pad(own_symbol(log_tab, 0).T, ((0, 4), (0, 0))),
            jnp.pad(own_symbol(log_tab, 1).T, ((0, 4), (0, 0))),
        ],
        axis=0,
    )
    log_rows = jnp.concatenate(split_two(log_rows), axis=1)
    log_small = jnp.pad(log_tab.T, ((0, 0), (1, 2)))

    total = shards * length
    symbols = everyone + 1
    padded = jnp.pad(symbols, (3, 3))
    mirrored = complement_padded(padded)
    ahead = [padded[k : k + total] for k in range(4)]
    behind = [mirrored[6 - k : 6 - k + total] for k in range(4)]
    shard_of = jnp.arange(total, dtype=jnp.int32) // length
    is_before = shard_of < seq_rank
    far = [jnp.where(is_before, a, b) for a, b in zip(ahead, behind)]
    early = encode(far[0], far[1]).reshape(128, 128)
    late = encode(far[2], far[3]).reshape(128, 128)
    own = jnp.where(shard_of == seq_rank, 0, far[3]).reshape(128, 128)
    window = lax.dynamic_slice_in_dim(padded, seq_rank * length, length + 6, 0)
    turned = complement_padded(window)
    lane = jnp.arange(128, dtype=jnp.int32)

    def onehot_of(axis):
        at = jnp.expand_dims(lane, 1 - axis)
        at = at % 64
        tap = (at % 32) // 8
        symbol = at % 8
        value = jnp.zeros(at.shape, jnp.int32)
        for k in range(4):
            first = jnp.expand_dims(window[k : k + length], axis)
            second = jnp.expand_dims(turned[6 - k : 6 - k + length], axis)
            value = jnp.where(tap == k, jnp.where(at < 32, first, second), value)
        hit = (value == symbol) & (symbol > 0) | (at % 32 == 6)
        return hit.astype(bf16)

    onehot = onehot_of(1)
    onehot_t = onehot_of(0)
    grams = _gram_onehot()
    gram_rows = jnp.asarray(grams, bf16)
    gram_cols = jnp.asarray(np.ascontiguousarray(grams[:, :32].T), bf16)
    seq_at = jnp.reshape(seq_rank, (1,)).astype(jnp.int32)

    y, states, sums, decays, after = call(
        forward_kernel,
        [
            ((2, length, width), f32),
            ((8, STATE, width), f32),
            ((2, 128, CODES), f32),
            ((4, 128, 128), f32),
            ((5, 128, 128), f32),
        ],
        [SMEM, SMEM] + [VMEM] * 10,
        [
            pltpu.VMEM((4, 128, 128), f32),
            pltpu.VMEM((4, 128, 128), f32),
            pltpu.VMEM((256, 1024), bf16),
            pltpu.VMEM((32, 1024), bf16),
            pltpu.VMEM((STATE, width), f32),
        ],
    )(
        seq_at, log_small, own, early, late, onehot, onehot_t, gram_rows, big, logs, log_rows,
        skip_own,
    )

    slope, row_sums = call(
        slope_kernel, [((length, width), f32), ((8, length), f32)], [VMEM] * 6
    )(y, onehot, big, cot_all, ow_own, gain_own)
    row_sums = jnp.sum(gather(row_sums, "head").reshape(groups, 8, length), axis=0)
    squares = jnp.stack([row_sums[0], row_sums[2]])
    crossed = jnp.stack([row_sums[1], row_sums[3]])
    scale = lax.rsqrt(squares / INNER + EPSILON)
    weight = scale * scale * scale * crossed / INNER
    scalars = jnp.stack([scale[0], weight[0], scale[1], weight[1]] + [scale[0]] * 4, axis=1)

    mixed, dy, dgate, dgain = call(
        mix_kernel,
        [
            ((length, width), bf16),
            ((2, length, width), f32),
            ((2, 32, width), f32),
            ((1, width), f32),
        ],
        [VMEM] * 7,
    )(y, onehot, onehot_t, big, slope, gain_own, scalars)

    mixed_all = lax.all_to_all(
        mixed.reshape(groups, token_rows, width), "head", split_axis=0, concat_axis=0, tiled=True
    )
    partial = lax.dot_general(cot_all, mixed, TN, preferred_element_type=f32)
    partial = lax.all_to_all(
        partial.reshape(shards, D // shards, width), "seq", split_axis=0, concat_axis=0, tiled=True
    )

    tables, steps, logs_back, skips, far_logs = call(
        backward_kernel,
        [
            ((32, 512), f32),
            ((32, width), f32),
            ((32, width), f32),
            ((1, width), f32),
            ((20, 128), f32),
        ],
        [SMEM] + [VMEM] * 16,
        [
            pltpu.VMEM((STATE, width), f32),
            pltpu.VMEM((2, STATE, width), f32),
            pltpu.VMEM((32, 1024), bf16),
            pltpu.VMEM((4, 128, 128), f32),
        ],
    )(
        seq_at, early, late, onehot, onehot_t, gram_rows, gram_cols, big, logs, log_rows, skip_own,
        y, states, sums, decays, after, dy,
    )

    grad_w_out = jnp.sum(partial, axis=0).T
    token_ids = lax.dynamic_slice_in_dim(base_ids, head_rank * token_rows, token_rows, 0)
    alphabet = jnp.arange(5, dtype=jnp.int32)
    token_hot = (token_ids[:, None] == alphabet[None, :]).astype(bf16)
    residual = jnp.dot(token_hot, embedding, preferred_element_type=f32)
    mixed_rows = mixed_all.transpose(1, 0, 2).reshape(token_rows, INNER)
    layer_out = (
        residual + jnp.dot(mixed_rows, out_weight, preferred_element_type=f32)
    ).astype(bf16)

    def own_rows(values):
        return jnp.sum(values[25:30].reshape(5, local_heads, HDIM), axis=2)

    by_tap = tables.reshape(KCONV, 8, width + 2 * STATE)
    grad_bias = tables[6]
    by_tap = by_tap[:, 1:6]
    conv_part = jnp.sum(by_tap * tab_conv[None], axis=1)
    tab_part = jnp.sum(by_tap * conv[:, None, :], axis=0)
    far_part = jnp.sum(far_logs, axis=1).reshape(local_heads, 5).T
    log_part = own_rows(logs_back) + far_part
    rate_part = jnp.sum(log_part * log_tab, axis=0)
    step_part = own_rows(steps) - rate[None, :] * log_part
    step_part = step_part * jax.nn.sigmoid(pre_step)
    skip_part = jnp.sum(skips.reshape(local_heads, HDIM), axis=1)
    gate_part = (dgate[0, 25:30] + dgate[1, 25:30]) * silu_slope(tab_gate)
    counts = lax.dot_general(token_hot, cotangent, TN, preferred_element_type=f32)
    step_cols = lax.dynamic_update_slice_in_dim(
        jnp.zeros((5, HEADS), f32), step_part, head_start, 1
    )
    table_part = jnp.concatenate([gate_part, tab_part, step_cols], axis=1)
    embed_part = counts + lax.dot_general(
        table_part, weight_own.astype(f32), NT, precision=lax.Precision.HIGHEST
    )
    heads_row = jnp.concatenate(
        [step_part, jnp.sum(step_part, axis=0)[None], rate_part[None], skip_part[None]], axis=0
    )
    heads_row = jnp.pad(heads_row.reshape(1, 8 * local_heads), ((0, 0), (0, width - 32)))
    packed = jnp.concatenate(
        [
            gate_part,
            tab_part[:, :width],
            conv_part[:, :width],
            grad_bias[None, :width],
            dgain,
            heads_row,
            tab_part[:, width:],
            conv_part[:, width:],
            grad_bias[None, width:],
            embed_part.reshape(20, width),
            jnp.zeros((1, width), f32),
        ],
        axis=0,
    )
    rows = packed.shape[0]
    pieces = lax.all_to_all(
        packed.reshape(shards, rows // shards, width), "seq", split_axis=0, concat_axis=0, tiled=True
    )
    piece = jnp.sum(pieces, axis=0)
    whole = gather(piece, ("seq", "head")).reshape(shards, groups, rows // shards, width)
    whole = whole.transpose(1, 0, 2, 3).reshape(groups, rows, width)
    mine = whole[:, :17]
    shared = jnp.sum(whole[:, 17:], axis=0)

    def lay(rows_of):
        return rows_of.transpose(1, 0, 2).reshape(rows_of.shape[1], INNER)

    heads_all = mine[:, 16, :32].reshape(groups, 8, local_heads)
    heads_all = heads_all.transpose(1, 0, 2).reshape(8, HEADS)
    table_sum = jnp.concatenate(
        [lay(mine[:, :5]), lay(mine[:, 5:10]), shared[:5], heads_all[:5]], axis=1
    )
    grad_conv = jnp.concatenate([lay(mine[:, 10:14]), shared[5:9]], axis=1)
    grad_conv_bias = jnp.concatenate([mine[:, 14].reshape(INNER), shared[9]])
    grad_gain = mine[:, 15].reshape(INNER)
    grad_embedding = shared[10:30].reshape(5, D)
    row_count = D // shards
    embed_columns = lax.dynamic_slice_in_dim(embedding, seq_rank * row_count, row_count, 1)
    grad_w_in = lax.dot_general(
        embed_columns.astype(f32), table_sum, TN, precision=lax.Precision.HIGHEST
    )
    return (
        layer_out,
        grad_w_in,
        grad_w_out,
        grad_embedding,
        grad_conv,
        grad_conv_bias,
        heads_all[5],
        heads_all[6],
        heads_all[7],
        grad_gain,
    )


def solution(mesh):
    return jax.shard_map(
        body,
        mesh=mesh,
        in_specs=(P("seq"), P(), P(), P(), P(), P(), P(), P(), P(), P(), P(("seq", "head"), None)),
        out_specs=(
            P(("seq", "head"), None),
            P("seq", None),
            P("head", "seq"),
            P(),
            P(),
            P(),
            P(),
            P(),
            P(),
            P(),
        ),
        check_vma=False,
    )
```

time: 1670 us -> 191 us (0.11); the launches traced: 1650 us -> 189 us
  local copies, waits for them, and re-layouts: 550 us -> 30.3 us
  waiting for transfers between devices: 360 us -> 32.8 us
  other arithmetic: 339 us -> 12.8 us
  matrix products: 284 us -> 9.79 us
  blocking collectives: 90.6 us -> 11 us
  Pallas kernels: 0 us -> 58 us
  starting transfers between devices: 7.87 us -> 33 us
    psum x2 -> x0, waiting for transfers between devices: 289 us -> none  [body(): lax.psum((table_grad, conv_grad, bias_grad, place_heads(step_bias_grad),...]
    dot_general x116 -> x7, matrix products: 270 us -> 9.79 us  [the longest x1 3.64 us: body(): jnp.dot(mixed_rows, out_weight, preferred_element_type=f32)]
    dynamic_slice x142 -> x8, local copies, waits for them, and re-layouts: 202 us -> 6.92 us  [the longest x6 4.29 us: cols(): return lax.dynamic_slice_in_dim(array, start, size, array.ndim - 1)]
    select_n x64 -> x2, other arithmetic: 113 us -> 0.87 us  [the longest x1 0.86 us: encode(): jnp.where(earlier > 0, (earlier - 1) * 5 + later - 1, jnp.where(later > 0...]
    mul x98 -> x2, local copies, waits for them, and re-layouts: 68.9 us -> 0.17 us  [the longest x1 0.09 us: body(): step_part = step_part * jax.nn.sigmoid(pre_step)]
    reduce_scatter x1 -> x0, waiting for transfers between devices: 65.7 us -> none  [body(): lax.psum_scatter(rows_part, 'head', scatter_dimension=1, tiled=True)]
    dynamic_update_slice x45 -> x0, other arithmetic: 63 us -> none  [the longest x40 62.5 us: ssd_mixer(): lax.scan(block_step, start_carry, (x_blocks, decay_blocks, step_blocks, b...]
    pallas_call x0 -> x4, Pallas kernels: none -> 58 us  [the longest x1 27.1 us: body(): call(backward_kernel, [((32, 512), f32), ((32, width), f32), ((32, width)...]
  transfers between devices with their start and end apart: 11 -> 6, of which waited for: 4 -> 5; matrix products, arithmetic and copies ran while one was open for 52% -> 18% of each run, Pallas kernels for 0% -> 11%
where the time goes in v1:
time: 191 us; the launch traced here: 189 us
  Pallas kernels  58 us (30%)
  starting transfers between devices  33 us (17%)
  waiting for transfers between devices  32.8 us (17%)
  local copies, waits for them, and re-layouts  30.3 us (16%)
  other arithmetic  12.8 us (7%)
  blocking collectives  11 us (6%)
  matrix products  9.79 us (5%)
    pallas_call x1, Pallas kernels, body(): call(backward_kernel, [((32, 512), f32), ((32, width), f32), ((32, width)...  27.1 us
    all_to_all x4, starting transfers between devices, gather(): return lax.all_to_all(spread, axis, split_axis=0, concat_axis=0, tiled=True)  25.8 us
    pallas_call x1, Pallas kernels, body(): call(forward_kernel, [((2, length, width), f32), ((8, STATE, width), f32)...  20.5 us
    all_to_all x4, waiting for transfers between devices, gather(): return lax.all_to_all(spread, axis, split_axis=0, concat_axis=0, tiled=True)  16.7 us
    all_to_all x1, blocking collectives, body(): lax.all_to_all(packed.reshape(shards, rows // shards, width), 'seq', spli...  11 us
    all_to_all x1, waiting for transfers between devices, body(): lax.all_to_all(mixed.reshape(groups, token_rows, width), 'head', split_ax...  9.85 us
    all_to_all x1, waiting for transfers between devices, body(): lax.all_to_all(partial.reshape(shards, D // shards, width), 'seq', split_...  6.29 us
    pallas_call x1, Pallas kernels, body(): call(slope_kernel, [((length, width), f32), ((8, length), f32)], [VMEM] * 6)  5.38 us
  transfers between devices with their start and end apart: 6, of which 5 were waited for; matrix products, arithmetic and copies ran while one was open for 18% of the time, Pallas kernels for 11%

profile of v1, /device:TPU:0, one launch (start us, length us, event | category | flops | bytes accessed | tf_op | source)
XLA Modules:
  0.0 188.9 jit_solution(3280007829972932655)
XLA Ops:
  0.7 1.3 broadcast_in_dim.298
  2.0 6.4 %all-to-all-start = ((s32[16,8,128]{2,1,0:T(8,128)}), s32[16,8,128]{2,1,0:T(8,128)S(1)}, u32[]{:S(2)}, u32[]{:S(2)}) async-start(s32[16,8,128]{2,1,0:T(8,128)} %broadcast_in_dim.298), calls=%async_computation | async-start | bytes 131072 | tf_op jit(solution)/shard_map/all_to_all | solution.py:436
  8.4 1.1 slice.207
  9.5 1.3 constant_dynamic-slice_fusion.3
  17.2 1.9 constant_dynamic-slice_fusion.ow_ref
  19.0 1.6 broadcast_in_dim.332
  20.7 6.7 %all-to-all-start.1 = ((bf16[8,128,1024]{2,1,0:T(8,128)(2,1)}), bf16[8,128,1024]{2,1,0:T(8,128)(2,1)S(1)}, u32[]{:S(2)}, u32[]{:S(2)}) async-start(bf16[8,128,1024]{2,1,0:T(8,128)(2,1)} %broadcast_in_dim.332), calls=%async_computation.1 | async-start | bytes 4194304 | tf_op jit(solution)/shard_map/all_to_all | solution.py:436
  28.2 1.3 dynamic_slice.50
  31.1 2.3 %fusion.4.oh_ref = bf16[1024,128]{1,0:T(8,128)(2,1)} fusion(s32[128]{0:T(128)S(1)} %and_select_fusion, s32[1024]{0:T(1024)S(1)} %get-tuple-element.107, s32[1024]{0:T(1024)S(1)} %get-tuple-element.63, s32[1024]{0:T(1024)S(1)} %get-tuple-element.106, s32[1024]{0:T(1024)S(1)} %get-tuple-element.62, s32[1024]{0:T(1024)S(1)} %get-tuple-element.105, ...), kind=kLoop, calls=%fused_computation.14 | loop fusion | flops 1572864 | bytes 296320 | tf_op jit(solution)/shard_map/convert_element_type | solution.py:561
  33.4 1.0 fusion.7.oht_ref
  35.4 20.5 %shard_map.204 = (f32[2,1024,256]{2,1,0:T(8,128)}, f32[8,128,256]{2,1,0:T(8,128)}, f32[2,128,32]{2,1,0:T(8,128)}, f32[4,128,128]{2,1,0:T(8,128)}, f32[5,128,128]{2,1,0:T(8,128)}) custom-call(s32[1]{0:T(128)} %bitcast.seq_ref, f32[4,8]{1,0:T(4,128)} %pad.69.ltab_ref, s32[128,128]{1,0:T(8,128)} %get-tuple-element.58.qs_ref, ...), custom_call_target="tpu_custom_call" | custom-call | tf_op jit(solution)/shard_map/pallas_call | solution.py:570
  56.5 1.3 copy-done.1
  57.8 5.4 %shard_map.205 = (f32[1024,256]{1,0:T(8,128)}, f32[8,1024]{1,0:T(8,128)}) custom-call(f32[2,1024,256]{2,1,0:T(8,128)} %get-tuple-element.26.y_ref, bf16[1024,128]{1,0:T(8,128)(2,1)} %fusion.4.oh_ref, bf16[128,2048]{1,0:T(8,128)(2,1)} %pad_maximum_fusion.3.tt_ref, bf16[1024,1024]{1,0:T(8,128)(2,1)} %bitcast.126, ...), custom_call_target="tpu_custom_call" | custom-call | tf_op jit(solution)/shard_map/pallas_call | solution.py:592
  63.2 1.5 broadcast_in_dim.334
  64.7 6.7 %all-to-all-start.2 = ((f32[8,8,1024]{2,1,0:T(8,128)}), f32[8,8,1024]{2,1,0:T(8,128)S(1)}, u32[]{:S(2)}, u32[]{:S(2)}) async-start(f32[8,8,1024]{2,1,0:T(8,128)} %broadcast_in_dim.334), calls=%async_computation.2 | async-start | bytes 524288 | tf_op jit(solution)/shard_map/all_to_all | solution.py:436
  71.6 8.5 %all-to-all-done.2 = f32[8,8,1024]{2,1,0:T(8,128)S(1)} async-done(((f32[8,8,1024]{2,1,0:T(8,128)}), f32[8,8,1024]{2,1,0:T(8,128)S(1)}, u32[]{:S(2)}, u32[]{:S(2)}) %all-to-all-start.2) | async-done | bytes 262176 | tf_op jit(solution)/shard_map/all_to_all | solution.py:436
  80.3 1.0 copy.166.cols_ref
  81.3 5.1 %shard_map.206 = (bf16[1024,256]{1,0:T(8,128)(2,1)}, f32[2,1024,256]{2,1,0:T(8,128)}, f32[2,32,256]{2,1,0:T(8,128)}, f32[1,256]{1,0:T(1,128)}) custom-call(f32[2,1024,256]{2,1,0:T(8,128)} %get-tuple-element.26.y_ref, bf16[1024,128]{1,0:T(8,128)(2,1)} %fusion.4.oh_ref, bf16[128,1024]{1,0:T(8,128)(2,1)} %fusion.7.oht_ref, ...), custom_call_target="tpu_custom_call" | custom-call | tf_op jit(solution)/shard_map/pallas_call | solution.py:602
  86.4 27.1 %shard_map.207 = (f32[32,512]{1,0:T(8,128)}, f32[32,256]{1,0:T(8,128)}, f32[32,256]{1,0:T(8,128)}, f32[1,256]{1,0:T(1,128)}, f32[20,128]{1,0:T(8,128)}) custom-call(s32[1]{0:T(128)} %bitcast.seq_ref, s32[128,128]{1,0:T(8,128)} %get-tuple-element.57.ca_ref, s32[128,128]{1,0:T(8,128)} %get-tuple-element.56.cb_ref, bf16[1024,128]{1,0:T(8,128)(2,1)} %fusion.4.oh_ref, ...), custom_call_target="tpu_custom_call" | custom-call | tf_op jit(solution)/shard_map/pallas_call | solution.py:621
  122.6 11.0 %all_to_all.35 = f32[16,3,256]{2,1,0:T(4,128)S(1)} all-to-all(f32[16,3,256]{2,1,0:T(4,128)S(1)} %reshape.383), channel_id=1, replica_groups=mesh['seq'=16,'head'=8] {'seq'}, dimensions={0} | all-to-all | bytes 98304 | tf_op jit(solution)/shard_map/all_to_all | solution.py:696
  134.5 6.0 %all-to-all-start.5 = ((f32[128,3,256]{2,1,0:T(4,128)}), f32[128,3,256]{2,1,0:T(4,128)}, u32[]{:S(2)}, u32[]{:S(2)}) async-start(f32[128,3,256]{2,1,0:T(4,128)} %broadcast_in_dim.340), calls=%async_computation.5 | async-start | bytes 1048576 | tf_op jit(solution)/shard_map/all_to_all | solution.py:436
  140.5 1.1 fusion.26
  141.6 1.8 convolution_bitcast_fusion
  143.4 1.3 copy.184
  145.7 7.6 %all-to-all-done.5 = f32[128,3,256]{2,1,0:T(4,128)} async-done(((f32[128,3,256]{2,1,0:T(4,128)}), f32[128,3,256]{2,1,0:T(4,128)}, u32[]{:S(2)}, u32[]{:S(2)}) %all-to-all-start.5) | async-done | bytes 393248 | tf_op jit(solution)/shard_map/all_to_all | solution.py:436
  153.2 3.5 %all-to-all-start.3 = ((bf16[8,128,256]{1,2,0:T(8,128)(2,1)}), bf16[8,128,256]{1,2,0:T(8,128)(2,1)S(1)}, u32[]{:S(2)}, u32[]{:S(2)}) async-start(bf16[8,128,256]{1,2,0:T(8,128)(2,1)} %copy.167), calls=%async_computation.3 | async-start | bytes 1048576 | tf_op jit(solution)/shard_map/all_to_all | solution.py:613
  156.7 1.1 copy.198
  158.0 9.9 %all-to-all-done.3 = bf16[8,128,256]{1,2,0:T(8,128)(2,1)S(1)} async-done(((bf16[8,128,256]{1,2,0:T(8,128)(2,1)}), bf16[8,128,256]{1,2,0:T(8,128)(2,1)S(1)}, u32[]{:S(2)}, u32[]{:S(2)}) %all-to-all-start.3) | async-done | bytes 524320 | tf_op jit(solution)/shard_map/all_to_all | solution.py:613
  167.9 3.8 %all-to-all-start.6 = ((f32[16,64,256]{2,1,0:T(8,128)}), f32[16,64,256]{2,1,0:T(8,128)S(1)}, u32[]{:S(2)}, u32[]{:S(2)}) async-start(f32[16,64,256]{2,1,0:T(8,128)} %bitcast.40), calls=%async_computation.6 | async-start | bytes 2097152 | tf_op jit(solution)/shard_map/all_to_all | solution.py:617
  175.9 1.7 fusion.10
  178.3 3.6 %fusion = bf16[128,1024]{1,0:T(8,128)(2,1)} fusion(f32[128,1024]{1,0:T(8,128)S(1)} %copy-done.4, bf16[128,2048]{0,1:T(8,128)(2,1)S(1)} %bitcast.129, bf16[2048,1024]{1,0:T(8,128)(2,1)} %param.22), kind=kOutput, calls=%fused_computation.4 | convolution fusion | flops 537133056 | bytes 5505024 | tf_op jit(solution)/shard_map/dot_general | solution.py:649
  181.9 6.3 %all-to-all-done.6 = f32[16,64,256]{2,1,0:T(8,128)S(1)} async-done(((f32[16,64,256]{2,1,0:T(8,128)}), f32[16,64,256]{2,1,0:T(8,128)S(1)}, u32[]{:S(2)}, u32[]{:S(2)}) %all-to-all-start.6) | async-done | bytes 1048608 | tf_op jit(solution)/shard_map/all_to_all | solution.py:617
  (160 shorter events, 27.1 us)
Async XLA Ops:
  0.6 10.2 %copy-start = (bf16[5,1024]{1,0:T(8,128)(2,1)S(1)}, bf16[5,1024]{1,0:T(8,128)(2,1)}, u32[]{:S(2)}) copy-start(bf16[5,1024]{1,0:T(8,128)(2,1)} %param.14) | copy-start | bytes 30724
  2.0 17.1 %all-to-all-start = ((s32[16,8,128]{2,1,0:T(8,128)}), s32[16,8,128]{2,1,0:T(8,128)S(1)}, u32[]{:S(2)}, u32[]{:S(2)}) async-start(s32[16,8,128]{2,1,0:T(8,128)} %broadcast_in_dim.298), calls=%async_computation | async-start | bytes 131072 | tf_op jit(solution)/shard_map/all_to_all | solution.py:436
  10.9 0.8 copy-start.6
  10.9 1.0 copy-start.8
  10.9 1.0 copy-start.12
  10.9 1.1 copy-start.13
  14.4 4.6 %copy-start.5 = (bf16[128,1024]{1,0:T(8,128)(2,1)S(1)}, bf16[128,1024]{1,0:T(8,128)(2,1)}, u32[]{:S(2)}) copy-start(bf16[128,1024]{1,0:T(8,128)(2,1)} %param.23) | copy-start | bytes 786436
  20.7 6.7 %copy-start.14 = (f32[32]{0:T(128)S(1)}, f32[32]{0:T(128)}, u32[]{:S(2)}) copy-start(f32[32]{0:T(128)} %param.20) | copy-start | bytes 388
  20.7 35.8 %all-to-all-start.1 = ((bf16[8,128,1024]{2,1,0:T(8,128)(2,1)}), bf16[8,128,1024]{2,1,0:T(8,128)(2,1)S(1)}, u32[]{:S(2)}, u32[]{:S(2)}) async-start(bf16[8,128,1024]{2,1,0:T(8,128)(2,1)} %broadcast_in_dim.332), calls=%async_computation.1 | async-start | bytes 4194304 | tf_op jit(solution)/shard_map/all_to_all | solution.py:436
  56.5 1.3 copy-start.1
  64.7 15.5 %all-to-all-start.2 = ((f32[8,8,1024]{2,1,0:T(8,128)}), f32[8,8,1024]{2,1,0:T(8,128)S(1)}, u32[]{:S(2)}, u32[]{:S(2)}) async-start(f32[8,8,1024]{2,1,0:T(8,128)} %broadcast_in_dim.334), calls=%async_computation.2 | async-start | bytes 524288 | tf_op jit(solution)/shard_map/all_to_all | solution.py:436
  86.4 33.1 %copy-start.7 = (bf16[1024,256]{0,1:T(8,128)(2,1)S(1)}, bf16[1024,256]{0,1:T(8,128)(2,1)}, u32[]{:S(2)}) copy-start(bf16[1024,256]{0,1:T(8,128)(2,1)} %copy-done.6) | copy-start | bytes 1572868
  86.4 33.1 %copy-start.9 = (bf16[1024,256]{0,1:T(8,128)(2,1)S(1)}, bf16[1024,256]{0,1:T(8,128)(2,1)}, u32[]{:S(2)}) copy-start(bf16[1024,256]{0,1:T(8,128)(2,1)} %copy-done.8) | copy-start | bytes 1572868
  119.2 1.8 copy-start.11
  119.2 3.0 %copy-start.10 = (f32[1,256]{1,0:T(1,128)S(1)}, f32[1,256]{1,0:T(1,128)}, u32[]{:S(2)}) copy-start(f32[1,256]{1,0:T(1,128)} %get-tuple-element.37) | copy-start | bytes 3076
  120.3 21.3 %copy-start.2 = (bf16[8,128,1024]{2,1,0:T(8,128)(2,1)S(1)}, bf16[8,128,1024]{2,1,0:T(8,128)(2,1)}, u32[]{:S(2)}) copy-start(bf16[8,128,1024]{2,1,0:T(8,128)(2,1)} %copy-done.1) | copy-start | bytes 6291460
  134.5 18.7 %all-to-all-start.5 = ((f32[128,3,256]{2,1,0:T(4,128)}), f32[128,3,256]{2,1,0:T(4,128)}, u32[]{:S(2)}, u32[]{:S(2)}) async-start(f32[128,3,256]{2,1,0:T(4,128)} %broadcast_in_dim.340), calls=%async_computation.5 | async-start | bytes 1048576 | tf_op jit(solution)/shard_map/all_to_all | solution.py:436
  143.3 1.3 copy-start.3
  153.2 14.6 %all-to-all-start.3 = ((bf16[8,128,256]{1,2,0:T(8,128)(2,1)}), bf16[8,128,256]{1,2,0:T(8,128)(2,1)S(1)}, u32[]{:S(2)}, u32[]{:S(2)}) async-start(bf16[8,128,256]{1,2,0:T(8,128)(2,1)} %copy.167), calls=%async_computation.3 | async-start | bytes 1048576 | tf_op jit(solution)/shard_map/all_to_all | solution.py:613
  167.9 10.4 %copy-start.4 = (f32[128,1024]{1,0:T(8,128)S(1)}, f32[128,1024]{1,0:T(8,128)}, u32[]{:S(2)}) copy-start(f32[128,1024]{1,0:T(8,128)} %fusion.26) | copy-start | bytes 1572868
  167.9 20.4 %all-to-all-start.6 = ((f32[16,64,256]{2,1,0:T(8,128)}), f32[16,64,256]{2,1,0:T(8,128)S(1)}, u32[]{:S(2)}, u32[]{:S(2)}) async-start(f32[16,64,256]{2,1,0:T(8,128)} %bitcast.40), calls=%async_computation.6 | async-start | bytes 2097152 | tf_op jit(solution)/shard_map/all_to_all | solution.py:617

commit v2 on v1

v2 whole, which is shorter than its diff:
```python
import jax
import jax.numpy as jnp
import numpy as np
from jax import lax
from jax.experimental import pallas as pl
from jax.experimental.pallas import tpu as pltpu
from jax.sharding import PartitionSpec as P

D = 1024
HEADS = 32
HDIM = 64
STATE = 128
BLOCK = 256
KCONV = 4
INNER = 2048
EPSILON = 1e-05

f32 = jnp.float32
bf16 = jnp.bfloat16
NN = (((1,), (0,)), ((), ()))
NT = (((1,), (1,)), ((), ()))
TN = (((0,), (0,)), ((), ()))

CODES = 32


def _decode_codes():
    first = np.zeros((CODES,), np.int32)
    second = np.zeros((CODES,), np.int32)
    for code in range(25):
        first[code], second[code] = code // 5 + 1, code % 5 + 1
    for code in range(25, 30):
        second[code] = code - 24
    return first, second


def _gram_onehot():
    first, second = _decode_codes()
    early, late = np.divmod(np.arange(CODES * CODES), CODES)
    symbols = (first[early], second[early], first[late], second[late])
    rows = np.zeros((CODES * CODES, 128), np.float32)
    for tap, symbol in enumerate(symbols):
        valid = symbol > 0
        rows[np.arange(CODES * CODES)[valid], (8 * tap + symbol)[valid]] = 1.0
    rows[:, 6] = 1.0
    rows[:, 64:96] = rows[:, :32]
    return rows


def encode(earlier, later):
    return jnp.where(
        earlier > 0, (earlier - 1) * 5 + later - 1, jnp.where(later > 0, 24 + later, 30)
    )


def complement_padded(symbols):
    return jnp.where((symbols >= 1) & (symbols <= 4), 5 - symbols, symbols)


def halves(values):
    high = values.astype(bf16)
    return high, (values - high.astype(f32)).astype(bf16)


def dot1(a, b, dims=NN):
    return lax.dot_general(a.astype(bf16), b.astype(bf16), dims, preferred_element_type=f32)


def doubled(values, axis):
    return jnp.concatenate([values, values], axis=axis)


def dot2(a, b, dims=NN):
    high, low = halves(b)
    a = a.astype(bf16)
    if a.shape[dims[0][0][0]] <= 128:
        pieces = jnp.concatenate([high, low], axis=dims[0][1][0])
        return dot1(doubled(a, dims[0][0][0]), pieces, dims)
    return dot1(a, high, dims) + dot1(a, low, dims)


def dot2l(a, b, dims=NN):
    high, low = halves(a)
    b = b.astype(bf16)
    if b.shape[dims[0][1][0]] <= 128:
        pieces = jnp.concatenate([high, low], axis=dims[0][0][0])
        return dot1(pieces, doubled(b, dims[0][1][0]), dims)
    return dot1(high, b, dims) + dot1(low, b, dims)


def dot3(a, b, dims=NN):
    a_high, a_low = halves(a)
    b_high, b_low = halves(b)
    if a.shape[dims[0][0][0]] <= 128:
        pieces = jnp.concatenate([a_high, a_low], axis=dims[0][0][0])
        return dot1(pieces, doubled(b_high, dims[0][1][0]), dims) + dot1(a_high, b_low, dims)
    return dot1(a_high, b_high, dims) + (dot1(a_high, b_low, dims) + dot1(a_low, b_high, dims))


def dot_exact(a, b, dims=NN):
    first = a.astype(bf16)
    rest = a - first.astype(f32)
    second = rest.astype(bf16)
    third = rest - second.astype(f32)
    b = b.astype(bf16)
    return dot1(first, b, dims) + (dot1(second, b, dims) + dot1(third, b, dims))


def iota(shape, axis):
    return lax.broadcasted_iota(jnp.int32, shape, axis)


def ones_where(condition):
    return jnp.where(condition, 1.0, 0.0).astype(bf16)


def expand_grams(sums):
    grams = CODES * CODES
    early = ones_where(iota((grams, CODES), 0) // CODES == iota((grams, CODES), 1))
    spread = dot2(early, sums)
    mine = iota((grams, 128), 0) % CODES == iota((grams, 128), 1) % CODES
    spread = jnp.where(mine, spread, 0.0)
    widen = ones_where(iota((128, 256), 0) // CODES == iota((128, 256), 1) // HDIM)
    return dot2l(spread, widen)


def gather_grams(values):
    grams = CODES * CODES
    narrow = ones_where(iota((256, 128), 0) // HDIM == iota((256, 128), 1) // CODES)
    spread = dot2l(values, narrow)
    mine = iota((grams, 128), 0) % CODES == iota((grams, 128), 1) % CODES
    spread = jnp.where(mine, spread, 0.0)
    early = ones_where(iota((CODES, grams), 1) // CODES == iota((CODES, grams), 0))
    return dot2(early, spread)


def sigmoid(values):
    return 0.5 * jnp.tanh(0.5 * values) + 0.5


def scan_inputs(oh_ref, oht_ref, tt_ref, lx_ref, lrow_ref, rows, branch):
    onehot = oh_ref[rows, :]
    onehot_t = oht_ref[:, rows]
    before = branch * 512
    pre = dot1(onehot, tt_ref[:, before : before + 512])
    step = dot1(onehot, tt_ref[:, 1024 + branch * 256 : 1280 + branch * 256])
    row = iota((BLOCK, BLOCK), 0)
    col = iota((BLOCK, BLOCK), 1)
    lower = ones_where(row >= col)
    upper = ones_where(row <= col)
    counts = dot1(lower if branch == 0 else upper, onehot).astype(bf16)
    counts_t = dot1(onehot_t, upper if branch == 0 else lower)
    log_wide = dot1(counts, lx_ref[:, branch * 256 : branch * 256 + 256])
    log_rows = dot1(lrow_ref[...].astype(bf16), counts_t)
    return onehot_t, pre, step, counts_t, log_wide, log_rows


def prep_kernel(
    at_ref, embed_ref, gate_w_ref, x_w_ref, bc_w_ref, step_w_ref, conv_x_ref, conv_bc_ref,
    bias_x_ref, bias_bc_ref, heads_ref, goh_ref,
    big_ref, logs_ref, lrow_ref, tab_ref, wide_ref, weight_ref, gact_ref, gbend_ref, gstep_ref,
):
    rank = at_ref[1]
    place = ones_where(iota((8, 5), 0) == iota((8, 5), 1) + 1)
    embed = dot1(place, embed_ref[...]).astype(bf16)
    gate_w = gate_w_ref[...]
    x_w = x_w_ref[...]
    bc_w = bc_w_ref[...]
    step_w = step_w_ref[...]
    weight_ref[:256, :] = gate_w
    weight_ref[256:512, :] = x_w
    weight_ref[512:768, :] = bc_w
    step_w = jnp.where(iota((128, D), 0) < HEADS, step_w.astype(f32), 0.0).astype(bf16)
    weight_ref[768:896, :] = step_w
    gate = dot1(embed, gate_w, NT)
    x = dot1(embed, x_w, NT)
    bc = dot1(embed, bc_w, NT)
    tab_ref[:, :256] = gate
    tab_ref[:, 256:512] = x
    tab_ref[:, 512:768] = bc
    row = iota((8, 128), 0)
    lane = iota((8, 128), 1)
    valid = (row >= 1) & (row <= 5)
    pre = dot1(embed, step_w, NT) + heads_ref[0:1, :]
    valid = valid & (lane < HEADS)
    step = jnp.maximum(pre, 0.0) + jnp.log1p(jnp.exp(-jnp.abs(pre)))
    rate = jnp.exp(heads_ref[1:2, :])
    logs = jnp.where(valid, -(rate * step), 0.0)
    step = jnp.where(valid, step, 0.0)
    bent = jnp.where(valid, sigmoid(pre), 0.0)
    widen = ones_where(iota((128, 256), 0) == rank * 4 + iota((128, 256), 1) // HDIM)
    step_wide = dot_exact(step, widen)
    logs_wide = dot_exact(logs, widen)
    wide_ref[0:8, :] = dot_exact(bent, widen)
    wide_ref[8:16, :] = logs_wide
    others = jnp.where(row == 0, rate, jnp.where(row == 1, heads_ref[2:3, :], 0.0))
    others = jnp.where(lane < HEADS, others, 0.0)
    wide_ref[16:24, :] = dot_exact(others, widen)
    one_row = iota((8, 256), 0) == 6
    conv_x = conv_x_ref[...]
    conv_bc = conv_bc_ref[...]
    taps = []
    for k in range(4):
        tap_x = conv_x[k : k + 1] * x
        tap_bc = conv_bc[k : k + 1] * bc
        if k == 0:
            tap_x = jnp.where(one_row, bias_x_ref[...], tap_x)
            tap_bc = jnp.where(one_row, bias_bc_ref[...], tap_bc)
        taps.append(jnp.concatenate([tap_x, tap_bc], axis=1))
    silu_gate = gate * sigmoid(gate)

    def put(ref, start, pieces):
        nothing = jnp.zeros(pieces[0][1].shape, f32)
        pieces = dict(pieces)
        table = jnp.concatenate([pieces.get(k, nothing) for k in range(8)], axis=0)
        high, low = halves(table)
        ref[0:64, start : start + table.shape[1]] = high
        ref[64:128, start : start + table.shape[1]] = low
        return high, low

    first_high, first_low = put(big_ref, 0, list(enumerate(taps)))
    put(big_ref, 512, [(4 + k, tap) for k, tap in enumerate(taps)])
    step_high, step_low = put(big_ref, 1024, [(3, step_wide)])
    put(big_ref, 1280, [(7, step_wide)])
    put(big_ref, 1536, [(3, silu_gate)])
    put(big_ref, 1792, [(7, silu_gate)])
    put(logs_ref, 0, [(3, logs_wide)])
    put(logs_ref, 256, [(7, logs_wide)])
    pick = ones_where((iota((8, 128), 1) == rank * 4 + row) & (row < 4))
    nothing = jnp.zeros((8, 128), f32)
    for branch in range(2):
        spot = 3 + 4 * branch
        rows = jnp.concatenate([logs if k % 8 == spot else nothing for k in range(16)], axis=0)
        first = rows.astype(bf16)
        rest = rows - first.astype(f32)
        second = rest.astype(bf16)
        third = rest - second.astype(f32)
        values = dot1(pick, first, NT) + (dot1(pick, second, NT) + dot1(pick, third, NT))
        high = values.astype(bf16).astype(f32)
        lrow_ref[8 * branch : 8 * branch + 8, :] = jnp.where(lane < 64, high, values - high)
    grams = goh_ref[...]
    pre = dot1(grams, big_ref[:, :384])
    logistic = sigmoid(pre)
    gact_ref[...] = pre * logistic
    gbend_ref[...] = logistic * (1.0 + pre * (1.0 - logistic))
    gstep_ref[...] = dot1(grams, big_ref[:, 1024:1280])


def shifted(symbols, by):
    row = iota((128, 128), 0)
    col = iota((128, 128), 1)
    if by > 0:
        rolled = pltpu.roll(symbols, by, axis=1)
        other = jnp.where(row == 0, 0, pltpu.roll(rolled, 1, axis=0))
        return jnp.where(col < by, other, rolled)
    rolled = pltpu.roll(symbols, 128 + by, axis=1)
    other = jnp.where(row == 127, 0, pltpu.roll(rolled, 127, axis=0))
    return jnp.where(col >= 128 + by, other, rolled)


def read_symbols(
    seq, ids_ref, ca_ref, cb_ref, taps_ref, oh_ref, oht_ref
):
    symbols = ids_ref[...] + 1
    taps = [shifted(symbols, 3 - k) if k < 3 else symbols for k in range(4)]
    turned = [complement_padded(shifted(symbols, k - 3) if k < 3 else symbols) for k in range(4)]
    row = iota((128, 128), 0)
    is_before = row < seq * 8
    far = [jnp.where(is_before, a, b) for a, b in zip(taps, turned)]
    ca_ref[...] = encode(far[0], far[1])
    cb_ref[...] = encode(far[2], far[3])
    for k in range(4):
        taps_ref[k] = taps[k]
        taps_ref[4 + k] = turned[k]
    at = pl.ds(pl.multiple_of(seq * 8, 8), 8)
    own = [taps_ref[k, at, :] for k in range(8)]
    sub = iota((8, 128), 0)
    for j in range(8):
        groups = []
        for k in range(8):
            hit = (own[k][j : j + 1] == sub) & (sub > 0)
            if k % 4 == 0:
                hit = hit | (sub == 6)
            groups.append(jnp.where(hit, 1.0, 0.0))
        rows = jnp.concatenate(groups + groups, axis=0)
        cols = slice(128 * j, 128 * j + 128)
        oht_ref[:, cols] = rows.astype(bf16)
        oh_ref[cols, :] = jnp.transpose(rows).astype(bf16)
    is_own = (row >= seq * 8) & (row < seq * 8 + 8)
    return jnp.where(is_own, 0, far[3])


def forward_kernel(
    at_ref, ids_ref, tt_ref, lx_ref, lrow_ref, wide_ref, gact_ref, gstep_ref,
    y_ref, states_ref, sums_ref, decay_ref, after_ref, oh_ref, oht_ref, ca_ref, cb_ref,
    taps_ref, lhs_ref, rhs_ref, carry_ref,
):
    seq = at_ref[0]
    first = seq * 8
    symbols = read_symbols(seq, ids_ref, ca_ref, cb_ref, taps_ref, oh_ref, oht_ref)
    log_small = lrow_ref[0:8, :] + pltpu.roll(lrow_ref[0:8, :], 64, axis=1)
    row = iota((128, 128), 0)
    col = iota((128, 128), 1)
    upto = ones_where(row <= col)
    every = jnp.ones((128, 128), bf16)
    signs = (jnp.where(col < row, 1.0, 0.0) - jnp.where(col < first, 1.0, 0.0)).astype(bf16)
    is_before = row < first
    logs = [jnp.zeros((128, 128), f32) for _ in range(4)]
    for symbol in range(1, 6):
        here = symbols == symbol
        found = ones_where(here)
        within = dot1(found, upto)
        total = dot1(found, every)
        upper = within + dot1(signs, total)
        after = jnp.where(is_before, -upper, upper - jnp.where(here, 1.0, 0.0))
        after_ref[symbol - 1] = after
        for h in range(4):
            logs[h] = logs[h] + after * log_small[h : h + 1, 24 + symbol : 25 + symbol]
    for h in range(4):
        decay = jnp.where(symbols > 0, jnp.exp(logs[h]), 0.0)
        decay_ref[h] = decay
    codes = iota((CODES, 128), 0)

    def add_shard(shard, total):
        at = pl.ds(pl.multiple_of(shard * 8, 8), 8)
        early = ca_ref[at, :]
        late = cb_ref[at, :]
        for j in range(8):
            cols = slice(128 * j, 128 * j + 128)
            rhs_ref[:, cols] = ones_where(early[j : j + 1] == codes)
            mine = late[j : j + 1] == codes
            for h in range(4):
                lhs_ref[32 * h : 32 * h + 32, cols] = jnp.where(
                    mine, decay_ref[h, at, :][j : j + 1], 0.0
                ).astype(bf16)
        return total + dot1(rhs_ref[...], lhs_ref[...], NT)

    zero = jnp.zeros((CODES, 128), f32)
    both = (
        lax.fori_loop(0, seq, add_shard, zero),
        lax.fori_loop(seq + 1, 16, add_shard, zero),
    )
    gram_b = gact_ref[:, 256:384]
    gram_xs = gact_ref[:, :256] * gstep_ref[...]
    skip = wide_ref[17:18, :]
    row = iota((BLOCK, BLOCK), 0)
    col = iota((BLOCK, BLOCK), 1)
    for branch in range(2):
        sums = both[branch]
        sums_ref[branch] = sums
        weights = expand_grams(sums)
        carry_ref[...] = dot3(gram_b, weights * gram_xs, TN)
        causal = row >= col if branch == 0 else row <= col

        def block_step(k, unused, branch=branch, causal=causal):
            block = k if branch == 0 else 3 - k
            rows = pl.ds(pl.multiple_of(block * BLOCK, BLOCK), BLOCK)
            onehot_t, pre, step, counts_t, log_wide, log_rows = scan_inputs(
                oh_ref, oht_ref, tt_ref, lx_ref, lrow_ref, rows, branch
            )
            act = pre * sigmoid(pre)
            x = act[:, :256]
            b = act[:, 256:384]
            c = act[:, 384:]
            xs = x * step
            state = carry_ref[...]
            states_ref[branch * 4 + block] = state
            inner = dot3(c, b, NT)
            parts = []
            for h in range(4):
                decays = jnp.exp(
                    jnp.where(
                        causal,
                        log_wide[:, h * HDIM : h * HDIM + 1]
                        - log_rows[branch * 8 + h : branch * 8 + h + 1, :],
                        -1e30,
                    )
                )
                parts.append(dot1(inner * decays, xs[:, h * HDIM : (h + 1) * HDIM]))
            within = jnp.concatenate(parts, axis=1)
            y = within + dot3(c, state) * jnp.exp(log_wide)
            y_ref[branch, rows, :] = y + skip * x
            edge = log_wide[BLOCK - 1 :] if branch == 0 else log_wide[:1]
            carry_ref[...] = jnp.exp(edge) * state + dot3(b, jnp.exp(edge - log_wide) * xs, TN)
            return unused

        lax.fori_loop(0, 4, block_step, 0)


def slope_kernel(at_ref, y_ref, oh_ref, tt_ref, cot_ref, ow_ref, gain_ref, slope_ref, sums_ref):
    slope = lax.dot_general(cot_ref[...], ow_ref[...], NT, preferred_element_type=f32)
    slope_ref[...] = slope
    weighted = slope * gain_ref[...]
    for branch in range(2):
        gate = dot1(oh_ref[...], tt_ref[:, 1536 + 256 * branch : 1792 + 256 * branch])
        g = y_ref[branch] * gate
        for kind, product in enumerate((g * g, weighted * g)):
            at = 2 * branch + kind
            product = product[:, :128] + product[:, 128:]
            for j in range(8):
                cols = slice(128 * j, 128 * j + 128)
                total = jnp.sum(jnp.transpose(product[cols]), axis=0, keepdims=True)
                for peer in range(sums_ref.shape[0]):
                    sums_ref[peer, at : at + 1, cols] = total


def mix_kernel(
    at_ref, y_ref, oh_ref, oht_ref, tt_ref, slope_ref, gain_ref, sums_ref,
    mixed_ref, dy_ref, dgate_ref, dgain_ref,
    cols_ref,
):
    gain = gain_ref[...]
    slope = slope_ref[...]
    sums = sums_ref[0]
    for peer in range(1, sums_ref.shape[0]):
        sums = sums + sums_ref[peer]
    scale = lax.rsqrt(sums / INNER + EPSILON)
    crossed = jnp.concatenate([sums[1:2], sums[1:2], sums[3:4], sums[3:4]], axis=0)
    weight = scale * scale * scale * crossed / INNER
    kind = iota(sums.shape, 0)
    weight = jnp.concatenate([weight[0:1], weight[0:1], weight[2:3], weight[2:3]], axis=0)
    rows = jnp.where(kind % 2 == 0, scale, weight)
    rows = jnp.concatenate([rows, rows] * 16, axis=0)
    for j in range(8):
        cols = slice(128 * j, 128 * j + 128)
        cols_ref[cols, :] = jnp.transpose(rows[:, cols])
    sloped = slope * gain
    total = None
    for branch in range(2):
        gate = dot1(oh_ref[...], tt_ref[:, 1536 + 256 * branch : 1792 + 256 * branch])
        y = y_ref[branch]
        g = y * gate
        scale = cols_ref[:, 2 * branch : 2 * branch + 1]
        weight = cols_ref[:, 2 * branch + 1 : 2 * branch + 2]
        normed = g * scale
        total = normed if total is None else total + normed
        dg = scale * sloped - weight * g
        dy_ref[branch] = dg * gate
        lanes = oht_ref[32 * branch : 32 * branch + 32, :]
        dgate_ref[branch] = dot2(lanes, dg * y)
    mixed_ref[...] = (total * gain).astype(bf16)
    dgain_ref[...] = jnp.sum(slope * total, axis=0, keepdims=True)


def backward_scan(
    branch, oh_ref, oht_ref, tt_ref, lx_ref, lrow_ref, wide_ref, y_ref, states_ref, dy_ref,
    tables_ref, steps_ref, logs_ref, skips_ref, carry_ref,
):
    skip = wide_ref[17:18, :]
    row = iota((BLOCK, BLOCK), 0)
    col = iota((BLOCK, BLOCK), 1)
    causal = row <= col if branch == 0 else row >= col
    carry_ref[...] = jnp.zeros_like(carry_ref)

    def block_step(k, unused):
        block = 3 - k if branch == 0 else k
        later = jnp.minimum(block + 1, 3) if branch == 0 else jnp.maximum(block - 1, 0)
        rows = pl.ds(pl.multiple_of(block * BLOCK, BLOCK), BLOCK)
        onehot_t, pre, step, counts_t, log_wide, log_rows = scan_inputs(
            oh_ref, oht_ref, tt_ref, lx_ref, lrow_ref, rows, branch
        )
        lanes = slice(32 * branch, 32 * branch + 32)
        onehot_t = onehot_t[lanes]
        counts_t = counts_t[lanes]
        logistic = sigmoid(pre)
        act = pre * logistic
        bend = logistic * (1.0 + pre * (1.0 - logistic))
        x = act[:, :256]
        b = act[:, 256:384]
        c = act[:, 384:]
        xs = x * step
        dy = dy_ref[branch, rows, :]
        own = y_ref[branch, rows, :] - skip * x
        state = states_ref[branch * 4 + block]
        pull = carry_ref[...]
        xs_low = xs.astype(bf16)
        dy_low = dy.astype(bf16)
        inner = dot3(b, c, NT)
        parts = []
        slopes = jnp.zeros((BLOCK, BLOCK), f32)
        for h in range(4):
            wide = slice(h * HDIM, (h + 1) * HDIM)
            decays = jnp.exp(
                jnp.where(
                    causal,
                    log_rows[branch * 8 + h : branch * 8 + h + 1, :]
                    - log_wide[:, h * HDIM : h * HDIM + 1],
                    -1e30,
                )
            )
            parts.append(dot1(inner * decays, dy_low[:, wide]))
            slopes = slopes + dot1(xs_low[:, wide], dy_low[:, wide], NT) * decays
        within = jnp.concatenate(parts, axis=1)
        faded = jnp.exp(log_wide) * dy
        edge = log_wide[BLOCK - 1 :] if branch == 0 else log_wide[:1]
        tail = jnp.exp(edge - log_wide)
        db = dot1(slopes, c) + dot1(tail * xs, pull, NT)
        dc = dot1(slopes, b, TN) + dot1(faded, state, NT)
        dxs = within + tail * dot1(b, pull)
        dlog = dy_low.astype(f32) * own - xs_low.astype(f32) * dxs
        edge_count = counts_t[:, BLOCK - 1 :] if branch == 0 else counts_t[:, :1]
        ahead = jnp.sum(states_ref[branch * 4 + later] * pull, axis=0, keepdims=True)
        logs_ref[...] += dot2(counts_t, dlog) + edge_count * ahead
        carry_ref[...] = dot1(c, faded, TN) + jnp.exp(edge) * pull
        dpre = jnp.concatenate([step * dxs + skip * dy, db, dc], axis=1) * bend
        tables_ref[...] += dot2(onehot_t, dpre)
        steps_ref[...] += dot2(onehot_t, x * dxs)
        skips_ref[...] += jnp.sum(dy * x, axis=0, keepdims=True)
        return unused

    lax.fori_loop(0, 4, block_step, 0)


def first_backward_kernel(
    at_ref, oh_ref, oht_ref, tt_ref, lx_ref, lrow_ref, wide_ref, y_ref, states_ref, dy_ref,
    cot_ref, mixed_ref,
    tables_ref, steps_ref, logs_ref, skips_ref, pull_ref, outer_ref,
):
    for ref in (tables_ref, steps_ref, logs_ref, skips_ref):
        ref[...] = jnp.zeros_like(ref)
    backward_scan(
        0, oh_ref, oht_ref, tt_ref, lx_ref, lrow_ref, wide_ref, y_ref, states_ref, dy_ref,
        tables_ref, steps_ref, logs_ref, skips_ref, pull_ref,
    )
    outer_ref[...] = lax.dot_general(cot_ref[...], mixed_ref[...], TN, preferred_element_type=f32)


def second_backward_kernel(
    at_ref, ca_ref, cb_ref, oh_ref, oht_ref, goht_ref, tt_ref, lx_ref, lrow_ref, wide_ref,
    y_ref, states_ref, sums_ref, decay_ref, after_ref, dy_ref, gact_ref, gbend_ref, gstep_ref,
    tab_ref, weight_ref, cot_ref, conv_x_ref, conv_bc_ref, dgate_ref, dgain_ref,
    tables_in_ref, steps_in_ref, logs_in_ref, skips_in_ref, pull_in_ref,
    packed_ref,
    pull_ref, mark_ref, found_ref, tables_ref, steps_ref, logs_ref, skips_ref,
):
    tables_ref[...] = tables_in_ref[...]
    steps_ref[...] = steps_in_ref[...]
    logs_ref[...] = logs_in_ref[...]
    skips_ref[...] = skips_in_ref[...]
    backward_scan(
        1, oh_ref, oht_ref, tt_ref, lx_ref, lrow_ref, wide_ref, y_ref, states_ref, dy_ref,
        tables_ref, steps_ref, logs_ref, skips_ref, pull_ref,
    )
    seq = at_ref[0]
    gram_x = gact_ref[:, :256]
    gram_b = gact_ref[:, 256:]
    gram_step = gstep_ref[...]
    gram_xs = gram_x * gram_step
    dxs = jnp.zeros((CODES * CODES, 256), f32)
    db = jnp.zeros((CODES * CODES, 128), f32)
    found = []
    for branch in range(2):
        pull = (pull_in_ref, pull_ref)[branch][...]
        weights = expand_grams(sums_ref[branch])
        met = dot1(gram_b, pull)
        dxs = dxs + weights * met
        db = db + dot1(weights * gram_xs, pull, NT)
        found.append(gather_grams(gram_xs * met))
    dpre = jnp.concatenate([gram_step * dxs, db], axis=1) * gbend_ref[...]
    gram_t = goht_ref[...]
    tables_ref[:, :384] += dot2(gram_t, dpre)
    steps_ref[...] += dot2(gram_t, gram_x * dxs)
    codes = iota((CODES, 128), 0)

    def look_up(branch):
        table = found[branch].astype(bf16)

        def one_shard(shard, unused):
            at = pl.ds(pl.multiple_of(shard * 8, 8), 8)
            early = ca_ref[at, :]
            late = cb_ref[at, :]
            for j in range(8):
                mark_ref[:, 128 * j : 128 * j + 128] = ones_where(early[j : j + 1] == codes)
            marks = mark_ref[...]
            looked = dot1(table, marks, TN)
            for h in range(4):
                rows = []
                for j in range(8):
                    part = looked[32 * h : 32 * h + 32, 128 * j : 128 * j + 128]
                    mine = late[j : j + 1] == codes
                    rows.append(jnp.sum(jnp.where(mine, part, 0.0), axis=0, keepdims=True))
                found_ref[h, at, :] = jnp.concatenate(rows, axis=0)
            return unused

        return one_shard

    found_ref[...] = jnp.zeros_like(found_ref)
    lax.fori_loop(0, seq, look_up(0), 0)
    lax.fori_loop(seq + 1, 16, look_up(1), 0)
    lane_head = iota((1, 256), 1) // HDIM
    sub = iota((8, 256), 0)
    far = jnp.zeros((8, 256), f32)
    for h in range(4):
        weighted = found_ref[h] * decay_ref[h]
        for symbol in range(5):
            total = jnp.sum(weighted * after_ref[symbol], axis=0, keepdims=True)
            total = jnp.sum(total, axis=1, keepdims=True)
            far = far + jnp.where((lane_head == h) & (sub == symbol + 1), total, 0.0)

    gate_tab = tab_ref[:, :256]
    x_tab = tab_ref[:, 256:512]
    bc_tab = tab_ref[:, 512:768]
    logistic = sigmoid(gate_tab)
    gate_part = (dgate_ref[0, 24:32, :] + dgate_ref[1, 24:32, :]) * (
        logistic * (1.0 + gate_tab * (1.0 - logistic))
    )
    conv_x = conv_x_ref[...]
    conv_bc = conv_bc_ref[...]
    x_part = jnp.zeros((8, 256), f32)
    bc_part = jnp.zeros((8, 256), f32)
    x_taps = []
    bc_taps = []
    for k in range(KCONV):
        dtap_x = tables_ref[8 * k : 8 * k + 8, :256]
        dtap_bc = tables_ref[8 * k : 8 * k + 8, 256:]
        x_part = x_part + conv_x[k : k + 1] * dtap_x
        bc_part = bc_part + conv_bc[k : k + 1] * dtap_bc
        x_taps.append(jnp.sum(dtap_x * x_tab, axis=0, keepdims=True))
        bc_taps.append(jnp.sum(dtap_bc * bc_tab, axis=0, keepdims=True))
    bias = tables_ref[6:7, :]
    same = ones_where(iota((256, 256), 0) // HDIM == iota((256, 256), 1) // HDIM)
    log_part = dot_exact(logs_ref[24:32, :], same) + far
    step_part = dot_exact(steps_ref[24:32, :], same) - wide_ref[16:17, :] * log_part
    step_part = step_part * wide_ref[0:8, :]
    rate_part = jnp.sum(log_part * wide_ref[8:16, :], axis=0, keepdims=True)
    skip_part = dot_exact(jnp.broadcast_to(skips_ref[...], (8, 256)), same)
    valid = (sub >= 1) & (sub <= 5)
    step_part = jnp.where(valid, step_part, 0.0)
    step_rows = jnp.where(
        sub == 0,
        jnp.sum(step_part, axis=0, keepdims=True),
        jnp.where(sub == 6, rate_part, jnp.where(sub == 7, skip_part, step_part)),
    )
    rank = at_ref[1]
    spread = iota((256, 128), 1)
    narrow = ones_where(
        (iota((256, 128), 0) % HDIM == 0)
        & (rank * 4 + iota((256, 128), 0) // HDIM == spread)
    )
    step_heads = dot_exact(step_rows, narrow)

    def against(part, first, last):
        first_piece = part.astype(bf16)
        rest = part - first_piece.astype(f32)
        second_piece = rest.astype(bf16)
        third_piece = rest - second_piece.astype(f32)
        weights = weight_ref[first:last, :]
        return dot1(first_piece, weights) + (
            dot1(second_piece, weights) + dot1(third_piece, weights)
        )

    tokens = oht_ref[16:32, pl.ds(pl.multiple_of(rank * 128, 128), 128)]
    embed_part = (
        dot1(tokens, cot_ref[...])[8:]
        + against(jnp.where(valid, gate_part, 0.0), 0, 256)
        + against(jnp.where(valid, x_part, 0.0), 256, 512)
        + against(jnp.where(valid, bc_part, 0.0), 512, 768)
        + against(jnp.where(valid[:, :128], step_heads, 0.0), 768, 896)
    )

    def rows_of(part, zero, six, seven):
        return jnp.where(
            sub == 0, zero, jnp.where(sub == 6, six, jnp.where(sub == 7, seven, part))
        )

    gate_rows = rows_of(gate_part, x_taps[0], x_taps[1], x_taps[2])
    x_rows = rows_of(x_part, x_taps[3], bias[:, :256], dgain_ref[...])
    bc_rows = rows_of(bc_part, bc_taps[0], bc_taps[1], bc_taps[2])
    embed_first = rows_of(embed_part[:, :256], bc_taps[3], bias[:, 256:], 0.0)
    for half in range(2):
        cols = slice(128 * half, 128 * half + 128)
        packed_ref[half] = gate_rows[:, cols]
        packed_ref[2 + half] = x_rows[:, cols]
        packed_ref[4 + half] = bc_rows[:, cols]
        packed_ref[7 + half] = embed_first[:, cols]
    packed_ref[6] = step_heads
    for piece in range(2, 8):
        packed_ref[7 + piece] = embed_part[:, 128 * piece : 128 * piece + 128]
    packed_ref[15] = jnp.zeros((8, 128), f32)


def out_kernel(mixed_ref, ow_ref, token_ref, embed_ref, out_ref):
    total = dot1(token_ref[...], embed_ref[...])
    for peer in range(mixed_ref.shape[0]):
        total = total + dot1(mixed_ref[peer], ow_ref[256 * peer : 256 * peer + 256, :])
    out_ref[...] = total.astype(bf16)


def sum_kernel(pieces_ref, spread_ref):
    total = pieces_ref[0]
    for k in range(1, pieces_ref.shape[0]):
        total = total + pieces_ref[k]
    spread_ref[...] = jnp.broadcast_to(total[None], spread_ref.shape)


def final_kernel(
    whole_ref, embed_ref,
    w_in_ref, embedding_ref, conv_ref, bias_ref, dt_ref, rate_ref, skip_ref, gain_ref,
):
    def summed(piece):
        total = whole_ref[8 * piece]
        for k in range(1, 8):
            total = total + whole_ref[8 * piece + k]
        return total

    embed = embed_ref[...]

    def outer(table, first):
        one = table.astype(bf16)
        rest = table - one.astype(f32)
        two = rest.astype(bf16)
        three = rest - two.astype(f32)
        pieces = jnp.concatenate([one.astype(f32), two.astype(f32), three], axis=0)
        value = dot1(embed, pieces)
        w_in_ref[:, first : first + table.shape[1]] = value

    for rank in range(8):
        for half in range(2):
            gate = whole_ref[8 * half + rank]
            x = whole_ref[8 * (2 + half) + rank]
            at = 256 * rank + 128 * half
            cols = slice(at, at + 128)
            outer(gate, at)
            outer(x, INNER + at)
            conv_ref[0:1, cols] = gate[0:1]
            conv_ref[1:2, cols] = gate[6:7]
            conv_ref[2:3, cols] = gate[7:8]
            conv_ref[3:4, cols] = x[0:1]
            bias_ref[:, cols] = x[6:7]
            gain_ref[:, cols] = x[7:8]
    for half in range(2):
        bc = summed(4 + half)
        at = INNER + 128 * half
        cols = slice(at, at + 128)
        outer(bc, INNER + at)
        rest = summed(7 + half)
        conv_ref[0:1, cols] = bc[0:1]
        conv_ref[1:2, cols] = bc[6:7]
        conv_ref[2:3, cols] = bc[7:8]
        conv_ref[3:4, cols] = rest[0:1]
        bias_ref[:, cols] = rest[6:7]
    steps = summed(6)[:, :HEADS]
    outer(steps, 2 * INNER + 2 * STATE)
    dt_ref[...] = steps[0:1]
    rate_ref[...] = steps[6:7]
    skip_ref[...] = steps[7:8]
    for piece in range(8):
        embedding_ref[:, 128 * piece : 128 * piece + 128] = summed(7 + piece)[1:6]


VMEM = pl.BlockSpec(memory_space=pltpu.VMEM)


def whole(array):
    zeros = (0,) * array.ndim
    return pl.BlockSpec(array.shape, lambda i, at: zeros)


def own(shape, index):
    return pl.BlockSpec(shape, index)


def call(kernel, at, operands, outs, scratch=(), cost=5e9):
    arrays = [item[0] if isinstance(item, tuple) else item for item in operands]
    specs = [
        own(item[1], item[2]) if isinstance(item, tuple) else whole(item) for item in operands
    ]
    shapes = [jax.ShapeDtypeStruct(shape, kind) for shape, kind in outs]
    return pl.pallas_call(
        kernel,
        out_shape=shapes,
        grid_spec=pltpu.PrefetchScalarGridSpec(
            num_scalar_prefetch=1,
            grid=(1,),
            in_specs=specs,
            out_specs=[whole(shape) for shape in shapes],
            scratch_shapes=list(scratch),
        ),
        compiler_params=pltpu.CompilerParams(vmem_limit_bytes=58 * 1024 * 1024),
        cost_estimate=pl.CostEstimate(flops=int(cost), bytes_accessed=4000000, transcendentals=0),
    )(at, *arrays)


def call_plain(kernel, operands, outs, cost=1e9):
    return pl.pallas_call(
        kernel,
        out_shape=[jax.ShapeDtypeStruct(shape, kind) for shape, kind in outs],
        in_specs=[VMEM] * len(operands),
        out_specs=[VMEM] * len(outs),
        compiler_params=pltpu.CompilerParams(vmem_limit_bytes=48 * 1024 * 1024),
        cost_estimate=pl.CostEstimate(flops=int(cost), bytes_accessed=1000000, transcendentals=0),
    )(*operands)


def gather(shard, axis):
    devices = lax.axis_size(axis)
    spread = jnp.broadcast_to(shard[None], (devices,) + shard.shape)
    return lax.all_to_all(spread, axis, split_axis=0, concat_axis=0, tiled=True)


def exchange(array, axis):
    return lax.all_to_all(array, axis, split_axis=0, concat_axis=0, tiled=True)


def body(
    base_ids, embedding, in_weight, conv_weight, conv_bias, dt_bias, a_log, skip_weight, norm_gain,
    out_weight, cotangent,
):
    groups = lax.axis_size("head")
    shards = lax.axis_size("seq")
    width = HEADS // groups * HDIM
    head_rank = lax.axis_index("head")
    seq_rank = lax.axis_index("seq")
    length = base_ids.shape[0]
    token_rows = length // groups
    at = jnp.stack([seq_rank, head_rank]).astype(jnp.int32)

    ids = gather(base_ids.reshape(8, 128), "seq").reshape(128, 128)
    cot_spread = jnp.broadcast_to(cotangent[None], (groups,) + cotangent.shape)

    weight_t = in_weight.T
    heads = jnp.pad(jnp.stack([dt_bias, a_log, skip_weight]), ((0, 5), (0, 128 - HEADS)))
    bias_row = conv_bias[None, :]
    gain_row = norm_gain[None, :]
    grams = _gram_onehot()
    gram_rows = jnp.asarray(grams, bf16)
    gram_cols = jnp.asarray(np.ascontiguousarray(grams[:, :32].T), bf16)
    conv_x = (conv_weight, (KCONV, width), lambda i, at: (0, at[1]))
    conv_bc = (conv_weight, (KCONV, width), lambda i, at: (0, INNER // width))
    count = CODES * CODES
    big, logs, log_rows, tab, wide, weight_own, gact, gbend, gstep = call(
        prep_kernel,
        at,
        [
            embedding,
            (weight_t, (width, D), lambda i, at: (at[1], 0)),
            (weight_t, (width, D), lambda i, at: (INNER // width + at[1], 0)),
            (weight_t, (256, D), lambda i, at: (16, 0)),
            (weight_t, (128, D), lambda i, at: (34, 0)),
            conv_x,
            conv_bc,
            (bias_row, (1, width), lambda i, at: (0, at[1])),
            (bias_row, (1, width), lambda i, at: (0, INNER // width)),
            heads,
            gram_rows,
        ],
        [
            ((128, 2048), bf16),
            ((128, 512), bf16),
            ((16, 128), f32),
            ((8, 768), f32),
            ((24, width), f32),
            ((896, D), bf16),
            ((count, 384), f32),
            ((count, 384), f32),
            ((count, width), f32),
        ],
        cost=3e9,
    )

    ids, cot_spread, big = lax.optimization_barrier((ids, cot_spread, big))
    cot_all = exchange(cot_spread, "head").reshape(length, D)
    y, states, sums, decays, after, onehot, onehot_t, early, late = call(
        forward_kernel,
        at,
        [ids, big, logs, log_rows, wide, gact, gstep],
        [
            ((2, length, width), f32),
            ((8, STATE, width), f32),
            ((2, CODES, 128), f32),
            ((4, 128, 128), f32),
            ((5, 128, 128), f32),
            ((length, 128), bf16),
            ((128, length), bf16),
            ((128, 128), jnp.int32),
            ((128, 128), jnp.int32),
        ],
        [
            pltpu.VMEM((8, 128, 128), jnp.int32),
            pltpu.VMEM((128, 1024), bf16),
            pltpu.VMEM((32, 1024), bf16),
            pltpu.VMEM((STATE, width), f32),
        ],
        cost=1.5e10,
    )

    gain_own = (gain_row, (1, width), lambda i, at: (0, at[1]))
    slope, row_sums = call(
        slope_kernel,
        at,
        [y, onehot, big, cot_all, (out_weight, (width, D), lambda i, at: (at[1], 0)), gain_own],
        [((length, width), f32), ((groups, 4, length), f32)],
        cost=4e9,
    )
    row_sums = exchange(row_sums, "head")
    mixed, dy, dgate, dgain = call(
        mix_kernel,
        at,
        [y, onehot, onehot_t, big, slope, gain_own, row_sums],
        [
            ((length, width), bf16),
            ((2, length, width), f32),
            ((2, 32, width), f32),
            ((1, width), f32),
        ],
        [pltpu.VMEM((length, 128), f32)],
        cost=4e9,
    )

    mixed_all = exchange(mixed.reshape(groups, token_rows, width), "head")
    shared = [onehot, onehot_t, big, logs, log_rows, wide, y, states]
    accumulators = [((32, 512), f32), ((32, width), f32), ((32, width), f32), ((1, width), f32)]
    *grads, pull, partial = call(
        first_backward_kernel,
        at,
        shared + [dy, cot_all, mixed],
        accumulators + [((STATE, width), f32), ((D, width), f32)],
        cost=1.5e10,
    )
    mixed_all, partial, pull = lax.optimization_barrier((mixed_all, partial, pull))
    partial = exchange(partial.reshape(shards, D // shards, width), "seq")
    (packed,) = call(
        second_backward_kernel,
        at,
        [
            early, late, onehot, onehot_t, gram_cols, big, logs, log_rows, wide, y, states, sums,
            decays, after, dy, gact, gbend, gstep, tab, weight_own, cotangent, conv_x, conv_bc,
            dgate, dgain, *grads, pull,
        ],
        [((shards, 8, 128), f32)],
        [
            pltpu.VMEM((STATE, width), f32),
            pltpu.VMEM((32, 1024), bf16),
            pltpu.VMEM((4, 128, 128), f32),
            *[pltpu.VMEM(shape, kind) for shape, kind in accumulators],
        ],
        cost=2e10,
    )
    packed, partial = lax.optimization_barrier((packed, partial))

    grad_w_out = jnp.sum(partial, axis=0).T
    token_ids = lax.dynamic_slice_in_dim(base_ids, head_rank * token_rows, token_rows, 0)
    alphabet = jnp.arange(5, dtype=jnp.int32)
    token_hot = (token_ids[:, None] == alphabet[None, :]).astype(bf16)
    (layer_out,) = call_plain(
        out_kernel,
        [mixed_all, out_weight, token_hot, embedding],
        [((token_rows, D), bf16)],
        4e9,
    )

    pieces = exchange(packed, "seq")
    (spread,) = call_plain(sum_kernel, [pieces], [((shards * groups, 8, 128), f32)], 1e8)
    everything = exchange(spread, ("seq", "head"))
    row_count = D // shards
    columns = lax.dynamic_slice_in_dim(embedding, seq_rank * row_count, row_count, 1)
    columns = jnp.pad(columns, ((1, 2), (0, 0)))
    columns = jnp.concatenate([columns] * 3, axis=0).T
    w_in, embed, conv, bias, dt, rate, skip, gain = call_plain(
        final_kernel,
        [everything, columns],
        [
            ((row_count, in_weight.shape[1]), f32),
            (embedding.shape, f32),
            (conv_weight.shape, f32),
            ((1, conv_bias.shape[0]), f32),
            ((1, HEADS), f32),
            ((1, HEADS), f32),
            ((1, HEADS), f32),
            ((1, INNER), f32),
        ],
    )
    return (
        layer_out, w_in, grad_w_out, embed, conv, bias[0], dt[0], rate[0], skip[0], gain[0],
    )


def solution(mesh):
    return jax.shard_map(
        body,
        mesh=mesh,
        in_specs=(P("seq"), P(), P(), P(), P(), P(), P(), P(), P(), P(), P(("seq", "head"), None)),
        out_specs=(
            P(("seq", "head"), None),
            P("seq", None),
            P("head", "seq"),
            P(),
            P(),
            P(),
            P(),
            P(),
            P(),
            P(),
        ),
        check_vma=False,
    )
```

time: 191 us -> 160 us (0.84)
  local copies, waits for them, and re-layouts: 30.3 us -> 9.36 us
  Pallas kernels: 58 us -> 72.8 us
  blocking collectives: 11 us -> 0 us
  matrix products: 9.79 us -> 0 us
  other arithmetic: 12.8 us -> 3.28 us
  starting transfers between devices: 33 us -> 39.5 us
    all_to_all x2 -> x6, starting transfers between devices: 7.28 us -> 33.1 us  [exchange(): return lax.all_to_all(array, axis, split_axis=0, concat_axis=0, tiled=True)]
    all_to_all x4 -> x1, starting transfers between devices: 25.8 us -> 6.43 us  [gather(): return lax.all_to_all(spread, axis, split_axis=0, concat_axis=0, tiled=True)]
    all_to_all x2 -> x6, waiting for transfers between devices: 16.1 us -> 33.2 us  [exchange(): return lax.all_to_all(array, axis, split_axis=0, concat_axis=0, tiled=True)]
    all_to_all x4 -> x1, waiting for transfers between devices: 16.7 us -> 0.01 us  [gather(): return lax.all_to_all(spread, axis, split_axis=0, concat_axis=0, tiled=True)]
    pallas_call x4 -> x9, Pallas kernels: 58 us -> 72.8 us  [the longest x6 69.1 us: call(): pl.pallas_call(kernel, out_shape=shapes, grid_spec=pltpu.PrefetchScalarGr...]
    all_to_all x1 -> x0, blocking collectives: 11 us -> none  [body(): lax.all_to_all(packed.reshape(shards, rows // shards, width), 'seq', spli...]
    dot_general x7 -> x0, matrix products: 9.79 us -> none  [the longest x1 3.64 us: body(): jnp.dot(mixed_rows, out_weight, preferred_element_type=f32)]
    dynamic_slice x7 -> x1, local copies, waits for them, and re-layouts: 6.16 us -> 0.08 us  [body(): lax.dynamic_slice_in_dim(embedding, seq_rank * row_count, row_count, 1)]
  transfers between devices with their start and end apart: 6 -> 7, of which waited for: 5 -> 4; matrix products, arithmetic and copies ran while one was open for 18% -> 3% of each run, Pallas kernels for 11% -> 37%
where the time goes in v2:
time: 160 us; the launch traced here: 159 us
  Pallas kernels  72.8 us (46%)
  starting transfers between devices  39.5 us (25%)
  waiting for transfers between devices  33.2 us (21%)
  local copies, waits for them, and re-layouts  9.36 us (6%)
  other arithmetic  3.28 us (2%)
    pallas_call x6, Pallas kernels, call(): pl.pallas_call(kernel, out_shape=shapes, grid_spec=pltpu.PrefetchScalarGr...  69.1 us
    all_to_all x6, waiting for transfers between devices, exchange(): return lax.all_to_all(array, axis, split_axis=0, concat_axis=0, tiled=True)  33.2 us
    all_to_all x6, starting transfers between devices, exchange(): return lax.all_to_all(array, axis, split_axis=0, concat_axis=0, tiled=True)  33.1 us
    all_to_all x1, starting transfers between devices, gather(): return lax.all_to_all(spread, axis, split_axis=0, concat_axis=0, tiled=True)  6.43 us
    unnamed x12, local copies, waits for them, and re-layouts  4.2 us
    pallas_call x3, Pallas kernels, call_plain(): pl.pallas_call(kernel, out_shape=[jax.ShapeDtypeStruct(shape, kind) for s...  3.63 us
  transfers between devices with their start and end apart: 7, of which 4 were waited for; matrix products, arithmetic and copies ran while one was open for 3% of the time, Pallas kernels for 37%

profile of v2, /device:TPU:0, one launch (start us, length us, event | category | flops | bytes accessed | tf_op | source)
XLA Modules:
  0.0 158.9 jit_solution(4056662543960718551)
XLA Ops:
  0.6 1.3 broadcast_in_dim.22
  2.0 6.4 %all-to-all-start = ((s32[16,8,128]{2,1,0:T(8,128)}), s32[16,8,128]{2,1,0:T(8,128)S(1)}, u32[]{:S(2)}, u32[]{:S(2)}) async-start(s32[16,8,128]{2,1,0:T(8,128)} %broadcast_in_dim.22), calls=%async_computation | async-start | bytes 131072 | tf_op jit(solution)/shard_map/all_to_all | solution.py:798
  8.4 1.3 broadcast_in_dim.24.bias_x_ref.bias_bc_ref
  9.7 0.6 pad_add_fusion.at_ref
  10.3 1.3 select_maximum_fusion.heads_ref
  11.6 5.8 %shard_map.204 = (bf16[128,2048]{1,0:T(8,128)(2,1)}, bf16[128,512]{1,0:T(8,128)(2,1)}, f32[16,128]{1,0:T(8,128)}, f32[8,768]{1,0:T(8,128)}, f32[24,256]{1,0:T(8,...) custom-call(s32[2]{0:T(128)} %pad_add_fusion.at_ref, ...), custom_call_target="tpu_custom_call" | custom-call | flops 3000000000 | bytes 4000000 | tf_op jit(solution)/shard_map/pallas_call | solution.py:769
  17.4 1.6 broadcast_in_dim.23
  19.0 6.6 %all-to-all-start.1 = ((bf16[8,128,1024]{2,1,0:T(8,128)(2,1)}), bf16[8,128,1024]{2,1,0:T(8,128)(2,1)S(1)}, u32[]{:S(2)}, u32[]{:S(2)}) async-start(bf16[8,128,1024]{2,1,0:T(8,128)(2,1)} %broadcast_in_dim.23), calls=%async_computation.1 | async-start | bytes 4194304 | tf_op jit(solution)/shard_map/all_to_all | solution.py:802
  25.6 18.2 %shard_map.205 = (f32[2,1024,256]{2,1,0:T(8,128)}, f32[8,128,256]{2,1,0:T(8,128)}, f32[2,32,128]{2,1,0:T(8,128)}, f32[4,128,128]{2,1,0:T(8,128)}, f32[5,128,128]...) custom-call(s32[2]{0:T(128)} %pad_add_fusion.at_ref, ...), custom_call_target="tpu_custom_call" | custom-call | flops 15000000512 | bytes 4000000 | tf_op jit(solution)/shard_map/pallas_call | solution.py:769
  43.8 10.9 %all-to-all-done.1 = bf16[8,128,1024]{2,1,0:T(8,128)(2,1)S(1)} async-done(((bf16[8,128,1024]{2,1,0:T(8,128)(2,1)}), bf16[8,128,1024]{2,1,0:T(8,128)(2,1)S(1)}, u32[]{:S(2)}, u32[]{:S(2)}) %all-to-all-start.1) | async-done | bytes 2097184 | tf_op jit(solution)/shard_map/all_to_all | solution.py:802
  54.7 1.4 copy-done.2
  56.1 5.5 %shard_map.206 = (f32[1024,256]{1,0:T(8,128)}, f32[8,4,1024]{2,1,0:T(4,128)}) custom-call(s32[2]{0:T(128)} %pad_add_fusion.at_ref, f32[2,1024,256]{2,1,0:T(8,128)} %get-tuple-element.64.y_ref, bf16[1024,128]{1,0:T(8,128)(2,1)} %get-tuple-element.65.oh_ref, bf16[128,2048]{1,0:T(8,128)(2,1)} %get-tuple-element.58.tt_ref, bf16[1024,1024]{1,0:T(8,128)(2,1)} %bitcast.23, ...), custom_call_target="tpu_custom_call" | custom-call | flops 4000000000 | bytes 4000000 | tf_op jit(solution)/shard_map/pallas_call | solution.py:769
  61.6 3.4 %all-to-all-start.2 = ((f32[8,4,1024]{2,1,0:T(4,128)}), f32[8,4,1024]{2,1,0:T(4,128)S(1)}, u32[]{:S(2)}, u32[]{:S(2)}) async-start(f32[8,4,1024]{2,1,0:T(4,128)} %get-tuple-element.69), calls=%async_computation.2 | async-start | bytes 262144 | tf_op jit(solution)/shard_map/all_to_all | solution.py:802
  65.1 8.0 %all-to-all-done.2.sums_ref = f32[8,4,1024]{2,1,0:T(4,128)S(1)} async-done(((f32[8,4,1024]{2,1,0:T(4,128)}), f32[8,4,1024]{2,1,0:T(4,128)S(1)}, u32[]{:S(2)}, u32[]{:S(2)}) %all-to-all-start.2) | async-done | bytes 131104 | tf_op jit(solution)/shard_map/all_to_all | solution.py:802
  73.1 0.6 copy-done.4
  73.8 5.8 %shard_map.207 = (bf16[1024,256]{1,0:T(8,128)(2,1)}, f32[2,1024,256]{2,1,0:T(8,128)}, f32[2,32,256]{2,1,0:T(8,128)}, f32[1,256]{1,0:T(1,128)}) custom-call(s32[2]{0:T(128)} %pad_add_fusion.at_ref, f32[2,1024,256]{2,1,0:T(8,128)} %get-tuple-element.64.y_ref, bf16[1024,128]{1,0:T(8,128)(2,1)} %get-tuple-element.65.oh_ref, ...), custom_call_target="tpu_custom_call" | custom-call | flops 4000000000 | bytes 4000000 | tf_op jit(solution)/shard_map/pallas_call | solution.py:769
  79.6 3.7 %all-to-all-start.3 = ((bf16[8,128,256]{2,1,0:T(8,128)(2,1)}), bf16[8,128,256]{2,1,0:T(8,128)(2,1)S(1)}, u32[]{:S(2)}, u32[]{:S(2)}) async-start(bf16[8,128,256]{2,1,0:T(8,128)(2,1)} %bitcast.26), calls=%async_computation.3 | async-start | bytes 1048576 | tf_op jit(solution)/shard_map/all_to_all | solution.py:802
  83.3 12.8 %shard_map.208 = (f32[32,512]{1,0:T(8,128)}, f32[32,256]{1,0:T(8,128)}, f32[32,256]{1,0:T(8,128)}, f32[1,256]{1,0:T(1,128)}, f32[128,256]{1,0:T(8,128)}, /*index=5*/f32[1024,256]{1,0:T(8,128)}) custom-call(s32[2]{0:T(128)} %pad_add_fusion.at_ref, bf16[1024,128]{1,0:T(8,128)(2,1)} %get-tuple-element.65.oh_ref, bf16[128,1024]{1,0:T(8,128)(2,1)} %get-tuple-element.66.oht_ref, ...), custom_call_target="tpu_custom_call" | custom-call | flops 15000000512 | bytes 4000000 | tf_op jit(solution)/shard_map/pallas_call | solution.py:769
  96.0 4.8 %all-to-all-start.4 = ((f32[16,64,256]{2,1,0:T(8,128)}), f32[16,64,256]{2,1,0:T(8,128)S(1)}, u32[]{:S(2)}, u32[]{:S(2)}) async-start(f32[16,64,256]{2,1,0:T(8,128)} %bitcast.25), calls=%async_computation.4 | async-start | bytes 2097152 | tf_op jit(solution)/shard_map/all_to_all | solution.py:802
  100.9 21.1 %shard_map.210 = f32[16,8,128]{2,1,0:T(8,128)} custom-call(s32[2]{0:T(128)} %pad_add_fusion.at_ref, s32[128,128]{1,0:T(8,128)} %get-tuple-element.76.ca_ref, s32[128,128]{1,0:T(8,128)} %get-tuple-element.77.cb_ref, bf16[1024,128]{1,0:T(8,128)(2,1)} %get-tuple-element.65.oh_ref, bf16[128,1024]{1,0:T(8,128)(2,1)} %get-tuple-element.66.oht_ref, ...), custom_call_target="tpu_custom_call" | custom-call | flops 20000000000 | bytes 4000000 | tf_op jit(solution)/shard_map/pallas_call | solution.py:769
  122.0 5.7 %all-to-all-start.5 = ((f32[16,8,128]{2,1,0:T(8,128)}), f32[16,8,128]{2,1,0:T(8,128)S(1)}, u32[]{:S(2)}, u32[]{:S(2)}) async-start(f32[16,8,128]{2,1,0:T(8,128)} %shard_map.210), calls=%async_computation.5 | async-start | bytes 131072 | tf_op jit(solution)/shard_map/all_to_all | solution.py:802
  127.6 0.1 copy.24
  127.7 0.8 dynamic_slice.6
  128.5 5.3 %all-to-all-done.5.pieces_ref = f32[16,8,128]{2,1,0:T(8,128)S(1)} async-done(((f32[16,8,128]{2,1,0:T(8,128)}), f32[16,8,128]{2,1,0:T(8,128)S(1)}, u32[]{:S(2)}, u32[]{:S(2)}) %all-to-all-start.5) | async-done | bytes 65568 | tf_op jit(solution)/shard_map/all_to_all | solution.py:802
  133.8 0.8 shard_map.211
  134.6 8.9 %all-to-all-start.6 = ((f32[128,8,128]{2,1,0:T(8,128)}), f32[128,8,128]{2,1,0:T(8,128)S(1)}, u32[]{:S(2)}, u32[]{:S(2)}) async-start(f32[128,8,128]{2,1,0:T(8,128)} %shard_map.211), calls=%async_computation.6 | async-start | bytes 1048576 | tf_op jit(solution)/shard_map/all_to_all | solution.py:802
  143.6 2.2 %copy-done.1 = bf16[2048,1024]{1,0:T(8,128)(2,1)S(1)} copy-done((bf16[2048,1024]{1,0:T(8,128)(2,1)S(1)}, bf16[2048,1024]{1,0:T(8,128)(2,1)}, u32[]{:S(2)}) %copy-start.1) | copy-done | bytes 4194328
  145.8 1.5 shard_map.209
  147.3 0.7 reduce_sum.9
  148.0 8.9 %all-to-all-done.6.whole_ref = f32[128,8,128]{2,1,0:T(8,128)S(1)} async-done(((f32[128,8,128]{2,1,0:T(8,128)}), f32[128,8,128]{2,1,0:T(8,128)S(1)}, u32[]{:S(2)}, u32[]{:S(2)}) %all-to-all-start.6) | async-done | bytes 524320 | tf_op jit(solution)/shard_map/all_to_all | solution.py:802
  156.9 1.3 shard_map.212
  158.2 0.6 reduce
  (16 shorter events, 0.2 us)
Async XLA Ops:
  2.0 15.4 %all-to-all-start = ((s32[16,8,128]{2,1,0:T(8,128)}), s32[16,8,128]{2,1,0:T(8,128)S(1)}, u32[]{:S(2)}, u32[]{:S(2)}) async-start(s32[16,8,128]{2,1,0:T(8,128)} %broadcast_in_dim.22), calls=%async_computation | async-start | bytes 131072 | tf_op jit(solution)/shard_map/all_to_all | solution.py:798
  11.6 5.8 %copy-start.3 = (bf16[128,1024]{1,0:T(8,128)(2,1)S(1)}, bf16[128,1024]{1,0:T(8,128)(2,1)}, u32[]{:S(2)}) copy-start(bf16[128,1024]{1,0:T(8,128)(2,1)} %cot_ref.1) | copy-start | bytes 786436
  17.4 1.6 %copy-start.5 = (s32[16,8,128]{2,1,0:T(8,128)}, s32[16,8,128]{2,1,0:T(8,128)S(1)}, u32[]{:S(2)}) copy-start(s32[16,8,128]{2,1,0:T(8,128)S(1)} %all-to-all-done) | copy-start | bytes 196612
  19.0 35.7 %all-to-all-start.1 = ((bf16[8,128,1024]{2,1,0:T(8,128)(2,1)}), bf16[8,128,1024]{2,1,0:T(8,128)(2,1)S(1)}, u32[]{:S(2)}, u32[]{:S(2)}) async-start(bf16[8,128,1024]{2,1,0:T(8,128)(2,1)} %broadcast_in_dim.23), calls=%async_computation.1 | async-start | bytes 4194304 | tf_op jit(solution)/shard_map/all_to_all | solution.py:802
  54.7 1.4 copy-start.2
  56.1 8.9 %copy-start = (bf16[5,1024]{1,0:T(8,128)(2,1)S(1)}, bf16[5,1024]{1,0:T(8,128)(2,1)}, u32[]{:S(2)}) copy-start(bf16[5,1024]{1,0:T(8,128)(2,1)} %embed_ref.3) | copy-start | bytes 30724
  61.6 11.5 %all-to-all-start.2 = ((f32[8,4,1024]{2,1,0:T(4,128)}), f32[8,4,1024]{2,1,0:T(4,128)S(1)}, u32[]{:S(2)}, u32[]{:S(2)}) async-start(f32[8,4,1024]{2,1,0:T(4,128)} %get-tuple-element.69), calls=%async_computation.2 | async-start | bytes 262144 | tf_op jit(solution)/shard_map/all_to_all | solution.py:802
  73.1 0.7 copy-start.4
  79.6 16.4 %all-to-all-start.3 = ((bf16[8,128,256]{2,1,0:T(8,128)(2,1)}), bf16[8,128,256]{2,1,0:T(8,128)(2,1)S(1)}, u32[]{:S(2)}, u32[]{:S(2)}) async-start(bf16[8,128,256]{2,1,0:T(8,128)(2,1)} %bitcast.26), calls=%async_computation.3 | async-start | bytes 1048576 | tf_op jit(solution)/shard_map/all_to_all | solution.py:802
  96.0 25.9 %all-to-all-start.4 = ((f32[16,64,256]{2,1,0:T(8,128)}), f32[16,64,256]{2,1,0:T(8,128)S(1)}, u32[]{:S(2)}, u32[]{:S(2)}) async-start(f32[16,64,256]{2,1,0:T(8,128)} %bitcast.25), calls=%async_computation.4 | async-start | bytes 2097152 | tf_op jit(solution)/shard_map/all_to_all | solution.py:802
  122.0 11.8 %all-to-all-start.5 = ((f32[16,8,128]{2,1,0:T(8,128)}), f32[16,8,128]{2,1,0:T(8,128)S(1)}, u32[]{:S(2)}, u32[]{:S(2)}) async-start(f32[16,8,128]{2,1,0:T(8,128)} %shard_map.210), calls=%async_computation.5 | async-start | bytes 131072 | tf_op jit(solution)/shard_map/all_to_all | solution.py:802
  134.6 22.3 %all-to-all-start.6 = ((f32[128,8,128]{2,1,0:T(8,128)}), f32[128,8,128]{2,1,0:T(8,128)S(1)}, u32[]{:S(2)}, u32[]{:S(2)}) async-start(f32[128,8,128]{2,1,0:T(8,128)} %shard_map.211), calls=%async_computation.6 | async-start | bytes 1048576 | tf_op jit(solution)/shard_map/all_to_all | solution.py:802
  143.6 2.2 %copy-start.1 = (bf16[2048,1024]{1,0:T(8,128)(2,1)S(1)}, bf16[2048,1024]{1,0:T(8,128)(2,1)}, u32[]{:S(2)}) copy-start(bf16[2048,1024]{1,0:T(8,128)(2,1)} %ow_ref.3) | copy-start | bytes 12582916

commit v3 on v2

v3 whole, which is shorter than its diff:
```python
import jax
import jax.numpy as jnp
import numpy as np
from jax import lax
from jax.experimental import pallas as pl
from jax.experimental.pallas import tpu as pltpu
from jax.sharding import PartitionSpec as P

D = 1024
HEADS = 32
HDIM = 64
STATE = 128
BLOCK = 256
KCONV = 4
INNER = 2048
EPSILON = 1e-05
LOG2E = 1.4426950408889634

f32 = jnp.float32
bf16 = jnp.bfloat16
NN = (((1,), (0,)), ((), ()))
NT = (((1,), (1,)), ((), ()))
TN = (((0,), (0,)), ((), ()))

CODES = 32


def _decode_codes():
    first = np.zeros((CODES,), np.int32)
    second = np.zeros((CODES,), np.int32)
    for code in range(25):
        first[code], second[code] = code // 5 + 1, code % 5 + 1
    for code in range(25, 30):
        second[code] = code - 24
    return first, second


def _gram_onehot():
    first, second = _decode_codes()
    early, late = np.divmod(np.arange(CODES * CODES), CODES)
    symbols = (first[early], second[early], first[late], second[late])
    rows = np.zeros((CODES * CODES, 128), np.float32)
    for tap, symbol in enumerate(symbols):
        valid = symbol > 0
        rows[np.arange(CODES * CODES)[valid], (8 * tap + symbol)[valid]] = 1.0
    rows[:, 6] = 1.0
    rows[:, 64:96] = rows[:, :32]
    return rows


def encode(earlier, later):
    return jnp.where(
        earlier > 0, (earlier - 1) * 5 + later - 1, jnp.where(later > 0, 24 + later, 30)
    )


def complement_padded(symbols):
    return jnp.where((symbols >= 1) & (symbols <= 4), 5 - symbols, symbols)


def halves(values):
    high = values.astype(bf16)
    return high, (values - high.astype(f32)).astype(bf16)


def dot1(a, b, dims=NN):
    return lax.dot_general(a.astype(bf16), b.astype(bf16), dims, preferred_element_type=f32)


def doubled(values, axis):
    return jnp.concatenate([values, values], axis=axis)


def dot2(a, b, dims=NN):
    high, low = halves(b)
    a = a.astype(bf16)
    if a.shape[dims[0][0][0]] <= 128:
        pieces = jnp.concatenate([high, low], axis=dims[0][1][0])
        return dot1(doubled(a, dims[0][0][0]), pieces, dims)
    return dot1(a, high, dims) + dot1(a, low, dims)


def dot2l(a, b, dims=NN):
    high, low = halves(a)
    b = b.astype(bf16)
    if b.shape[dims[0][1][0]] <= 128:
        pieces = jnp.concatenate([high, low], axis=dims[0][0][0])
        return dot1(pieces, doubled(b, dims[0][1][0]), dims)
    return dot1(high, b, dims) + dot1(low, b, dims)


def dot3(a, b, dims=NN):
    a_high, a_low = halves(a)
    b_high, b_low = halves(b)
    if a.shape[dims[0][0][0]] <= 128:
        pieces = jnp.concatenate([a_high, a_low], axis=dims[0][0][0])
        return dot1(pieces, doubled(b_high, dims[0][1][0]), dims) + dot1(a_high, b_low, dims)
    return dot1(a_high, b_high, dims) + (dot1(a_high, b_low, dims) + dot1(a_low, b_high, dims))


def dot_exact(a, b, dims=NN):
    first = a.astype(bf16)
    rest = a - first.astype(f32)
    second = rest.astype(bf16)
    third = rest - second.astype(f32)
    b = b.astype(bf16)
    return dot1(first, b, dims) + (dot1(second, b, dims) + dot1(third, b, dims))


def iota(shape, axis):
    return lax.broadcasted_iota(jnp.int32, shape, axis)


def ones_where(condition):
    return jnp.where(condition, 1.0, 0.0).astype(bf16)


def expand_grams(sums):
    grams = CODES * CODES
    early = ones_where(iota((grams, CODES), 0) // CODES == iota((grams, CODES), 1))
    both = dot2(early, jnp.concatenate([sums[:CODES], sums[CODES:]], axis=1))
    mine = iota((grams, 128), 0) % CODES == iota((grams, 128), 1) % CODES
    widen = ones_where(iota((128, 256), 0) // CODES == iota((128, 256), 1) // HDIM)
    return [
        dot2l(jnp.where(mine, both[:, 128 * k : 128 * k + 128], 0.0), widen) for k in range(2)
    ]


def gather_grams(values):
    grams = CODES * CODES
    narrow = ones_where(iota((256, 128), 0) // HDIM == iota((256, 128), 1) // CODES)
    mine = iota((grams, 128), 0) % CODES == iota((grams, 128), 1) % CODES
    spread = [jnp.where(mine, dot1(value, narrow), 0.0) for value in values]
    early = ones_where(iota((CODES, grams), 1) // CODES == iota((CODES, grams), 0))
    both = dot1(early, jnp.concatenate(spread, axis=1))
    return jnp.concatenate([both[:, :128], both[:, 128:]], axis=0)


def sigmoid(values):
    return 0.5 * jnp.tanh(0.5 * values) + 0.5


def scan_inputs(onehot, onehot_t, pre_tab, step_tab, log_tab, log_rows, ahead, behind):
    pre = dot1(onehot, pre_tab)
    step = dot1(onehot, step_tab)
    counts = dot1(ones_where(behind), onehot).astype(bf16)
    counts_t = dot1(onehot_t, ones_where(ahead))
    log_wide = dot1(counts, log_tab)
    log_rows = dot1(log_rows.astype(bf16), counts_t)
    return pre, step, counts_t, log_wide, log_rows


def prep_kernel(
    at_ref, embed_ref, gate_w_ref, x_w_ref, bc_w_ref, step_w_ref, conv_x_ref, conv_bc_ref,
    bias_ref, dt_ref, rate_ref, skip_ref, goh_ref,
    big_ref, logs_ref, lrow_ref, tab_ref, wide_ref, gxs_ref, gbt_ref,
):
    rank = at_ref[1]
    place = ones_where(iota((8, 5), 0) == iota((8, 5), 1) + 1)
    embed = dot1(place, embed_ref[...]).astype(bf16)
    gate_w = gate_w_ref[...]
    x_w = x_w_ref[...]
    bc_w = bc_w_ref[...]
    step_w = step_w_ref[...]
    step_w = jnp.where(iota((128, D), 0) < HEADS, step_w.astype(f32), 0.0).astype(bf16)

    def heads_row(ref):
        return jnp.concatenate([ref[...], jnp.zeros((1, 128 - HEADS), f32)], axis=1)

    bias_x = jnp.concatenate(
        [bias_ref[pl.ds(2 * rank, 1), :], bias_ref[pl.ds(2 * rank + 1, 1), :]], axis=1
    )
    bias_bc = jnp.concatenate([bias_ref[16:17, :], bias_ref[17:18, :]], axis=1)
    gate = dot1(embed, gate_w, NT)
    x = dot1(embed, x_w, NT)
    bc = dot1(embed, bc_w, NT)
    tab_ref[:, :256] = gate
    tab_ref[:, 256:512] = x
    tab_ref[:, 512:768] = bc
    row = iota((8, 128), 0)
    lane = iota((8, 128), 1)
    valid = (row >= 1) & (row <= 5)
    pre = dot1(embed, step_w, NT) + heads_row(dt_ref)
    valid = valid & (lane < HEADS)
    step = jnp.maximum(pre, 0.0) + jnp.log1p(jnp.exp(-jnp.abs(pre)))
    rate = jnp.exp(heads_row(rate_ref))
    logs = jnp.where(valid, -(rate * step), 0.0)
    step = jnp.where(valid, step, 0.0)
    bent = jnp.where(valid, sigmoid(pre), 0.0)
    widen = ones_where(iota((128, 256), 0) == rank * 4 + iota((128, 256), 1) // HDIM)
    step_wide = dot_exact(step, widen)
    logs_wide = dot_exact(logs, widen)
    logs = logs * LOG2E
    wide_ref[0:8, :] = dot_exact(bent, widen)
    wide_ref[8:16, :] = logs_wide
    others = jnp.where(row == 0, rate, jnp.where(row == 1, heads_row(skip_ref), 0.0))
    others = jnp.where(lane < HEADS, others, 0.0)
    wide_ref[16:24, :] = dot_exact(others, widen)
    one_row = iota((8, 256), 0) == 6
    conv_x = conv_x_ref[...]
    conv_bc = conv_bc_ref[...]
    taps = []
    for k in range(4):
        tap_x = conv_x[k : k + 1] * x
        tap_bc = conv_bc[k : k + 1] * bc
        if k == 0:
            tap_x = jnp.where(one_row, bias_x, tap_x)
            tap_bc = jnp.where(one_row, bias_bc, tap_bc)
        taps.append(jnp.concatenate([tap_x, tap_bc], axis=1))
    silu_gate = gate * sigmoid(gate)

    def put(ref, start, pieces):
        nothing = jnp.zeros(pieces[0][1].shape, f32)
        pieces = dict(pieces)
        table = jnp.concatenate([pieces.get(k, nothing) for k in range(8)], axis=0)
        high, low = halves(table)
        ref[0:64, start : start + table.shape[1]] = high
        ref[64:128, start : start + table.shape[1]] = low
        return high, low

    first_high, first_low = put(big_ref, 0, list(enumerate(taps)))
    put(big_ref, 512, [(4 + k, tap) for k, tap in enumerate(taps)])
    step_high, step_low = put(big_ref, 1024, [(3, step_wide)])
    put(big_ref, 1280, [(7, step_wide)])
    put(big_ref, 1536, [(3, silu_gate)])
    put(big_ref, 1792, [(7, silu_gate)])
    put(logs_ref, 0, [(3, logs_wide * LOG2E)])
    put(logs_ref, 256, [(7, logs_wide * LOG2E)])
    pick = ones_where((iota((8, 128), 1) == rank * 4 + row) & (row < 4))
    nothing = jnp.zeros((8, 128), f32)
    for branch in range(2):
        spot = 3 + 4 * branch
        rows = jnp.concatenate([logs if k % 8 == spot else nothing for k in range(16)], axis=0)
        first = rows.astype(bf16)
        rest = rows - first.astype(f32)
        second = rest.astype(bf16)
        third = rest - second.astype(f32)
        values = dot1(pick, first, NT) + (dot1(pick, second, NT) + dot1(pick, third, NT))
        high = values.astype(bf16).astype(f32)
        lrow_ref[8 * branch : 8 * branch + 8, :] = jnp.where(lane < 64, high, values - high)
    grams = goh_ref[...]
    pre = dot1(grams, big_ref[:, :384])
    act = pre * sigmoid(pre)
    for j in range(8):
        cols = slice(128 * j, 128 * j + 128)
        gbt_ref[:, cols] = jnp.transpose(act[cols, 256:])
    gxs_ref[...] = act[:, :256] * dot1(grams, big_ref[:, 1024:1280])


def gram_kernel(at_ref, goh_ref, pre_ref, step_ref, gact_ref, gbend_ref, gstep_ref):
    pre = dot1(goh_ref[...], pre_ref[:, :384])
    logistic = sigmoid(pre)
    gact_ref[...] = pre * logistic
    gbend_ref[...] = logistic * (1.0 + pre * (1.0 - logistic))
    gstep_ref[...] = dot1(goh_ref[...], step_ref[...])


def shifted(symbols, by):
    row = iota((128, 128), 0)
    col = iota((128, 128), 1)
    if by > 0:
        rolled = pltpu.roll(symbols, by, axis=1)
        other = jnp.where(row == 0, 0, pltpu.roll(rolled, 1, axis=0))
        return jnp.where(col < by, other, rolled)
    rolled = pltpu.roll(symbols, 128 + by, axis=1)
    other = jnp.where(row == 127, 0, pltpu.roll(rolled, 127, axis=0))
    return jnp.where(col >= 128 + by, other, rolled)


def read_symbols(
    seq, ids_ref, ca_ref, cb_ref, taps_ref, oh_ref, oht_ref
):
    symbols = []
    for shard in range(16):
        mask = jnp.bitwise_xor(seq, shard)
        near = jnp.bitwise_and(mask, 1) + 2 * jnp.bitwise_and(mask // 8, 1)
        symbols.append(ids_ref[jnp.bitwise_and(mask // 2, 3) * 4 + near])
    symbols = jnp.concatenate(symbols, axis=0) + 1
    taps = [shifted(symbols, 3 - k) if k < 3 else symbols for k in range(4)]
    turned = [complement_padded(shifted(symbols, k - 3) if k < 3 else symbols) for k in range(4)]
    row = iota((128, 128), 0)
    is_before = row < seq * 8
    far = [jnp.where(is_before, a, b) for a, b in zip(taps, turned)]
    ca_ref[...] = encode(far[0], far[1]) + jnp.where(is_before, 0, CODES)
    cb_ref[...] = encode(far[2], far[3])
    for k in range(4):
        taps_ref[k] = taps[k]
        taps_ref[4 + k] = turned[k]
    at = pl.ds(pl.multiple_of(seq * 8, 8), 8)
    own = [taps_ref[k, at, :] for k in range(8)]
    sub = iota((8, 128), 0)
    for j in range(8):
        groups = []
        for k in range(8):
            hit = (own[k][j : j + 1] == sub) & (sub > 0)
            if k % 4 == 0:
                hit = hit | (sub == 6)
            groups.append(jnp.where(hit, 1.0, 0.0))
        rows = jnp.concatenate(groups + groups, axis=0)
        cols = slice(128 * j, 128 * j + 128)
        oht_ref[:, cols] = rows.astype(bf16)
        oh_ref[cols, :] = jnp.transpose(rows).astype(bf16)
    is_own = (row >= seq * 8) & (row < seq * 8 + 8)
    return jnp.where(is_own, 0, far[3])


def triangle(lower, column, row, inner, sign=1.0):
    half = BLOCK // 2
    apart = iota((half, half), 0) - iota((half, half), 1)
    keep = apart >= 0 if lower else apart <= 0
    parts = []
    for i in range(2):
        rows = slice(half * i, half * i + half)
        line = []
        for j in range(2):
            cols = slice(half * j, half * j + half)
            if (i < j) if lower else (i > j):
                line.append(jnp.zeros((half, half), f32))
                continue
            apart = column[rows] - row[:, cols] if sign > 0 else row[:, cols] - column[rows]
            if i == j:
                apart = jnp.where(keep, apart, -1e30)
            value = jnp.exp2(apart)
            line.append(value if inner is None else value * inner[rows, cols])
        parts.append(jnp.concatenate(line, axis=1))
    return jnp.concatenate(parts, axis=0)


def gram_sums(ca_ref, cb_ref, decay_ref, lhs_ref, rhs_ref):
    early_codes = iota((2 * CODES, 128), 0)
    late_codes = iota((CODES, 128), 0)

    def add(k, total):
        for j in range(32):
            if j % 8 == 0:
                at = pl.ds(pl.multiple_of(k * 32 + j, 8), 8)
                early = ca_ref[at, :]
                late = cb_ref[at, :]
                decays = [decay_ref[h, at, :] for h in range(4)]
            cols = slice(128 * j, 128 * j + 128)
            one = slice(j % 8, j % 8 + 1)
            rhs_ref[:, cols] = ones_where(early[one] == early_codes)
            mine = late[one] == late_codes
            for h in range(4):
                lhs_ref[32 * h : 32 * h + 32, cols] = jnp.where(mine, decays[h][one], 0.0).astype(
                    bf16
                )
        return total + dot1(rhs_ref[...], lhs_ref[...], NT)

    return lax.fori_loop(0, 4, add, jnp.zeros((2 * CODES, 128), f32), unroll=2)


def forward_kernel(
    at_ref, ids_ref, pre_ref, step_ref, lx_ref, lrow_ref, wide_ref, gxs_ref, gbt_ref,
    y_first_ref, y_second_ref, states_ref, sums_ref, decay_ref, after_ref, oh_ref, oht_ref,
    ca_ref, cb_ref,
    taps_ref, lhs_ref, rhs_ref, carry_ref,
):
    step_at = pl.program_id(0)
    y_refs = (y_first_ref, y_second_ref)

    @pl.when(step_at == 0)
    def _():
        seq = at_ref[0]
        first = seq * 8
        symbols = read_symbols(seq, ids_ref, ca_ref, cb_ref, taps_ref, oh_ref, oht_ref)
        log_small = lrow_ref[0:8, :] + pltpu.roll(lrow_ref[0:8, :], 64, axis=1)
        row = iota((128, 128), 0)
        col = iota((128, 128), 1)
        upto = ones_where(row <= col)
        every = jnp.ones((128, 128), bf16)
        signs = (jnp.where(col < row, 1.0, 0.0) - jnp.where(col < first, 1.0, 0.0)).astype(bf16)
        is_before = row < first
        logs = [jnp.zeros((128, 128), f32) for _ in range(4)]
        for symbol in range(1, 6):
            here = symbols == symbol
            found = ones_where(here)
            upper = dot1(found, upto) + dot1(signs, dot1(found, every))
            after = jnp.where(is_before, -upper, upper - jnp.where(here, 1.0, 0.0))
            after_ref[symbol - 1] = after
            for h in range(4):
                logs[h] = logs[h] + after * log_small[h : h + 1, 24 + symbol : 25 + symbol]
        for h in range(4):
            decay_ref[h] = jnp.where(symbols > 0, jnp.exp2(logs[h]), 0.0)
        sums = gram_sums(ca_ref, cb_ref, decay_ref, lhs_ref, rhs_ref)
        sums_ref[...] = sums
        gram_xs = gxs_ref[...]
        both = jnp.concatenate([weights * gram_xs for weights in expand_grams(sums)], axis=1)
        states = dot3(gbt_ref[...], both)
        carry_ref[0] = states[:, :256]
        carry_ref[1] = states[:, 256:]

    for branch in range(2):
        block = step_at if branch == 0 else 3 - step_at
        rows = pl.ds(pl.multiple_of(block * BLOCK, BLOCK), BLOCK)
        apart = iota((BLOCK, BLOCK), 0) - iota((BLOCK, BLOCK), 1)
        lower = branch == 0
        behind = apart >= 0 if lower else apart <= 0
        ahead = apart <= 0 if lower else apart >= 0
        pre, step, counts_t, log_wide, log_rows = scan_inputs(
            oh_ref[rows, :], oht_ref[:, rows], pre_ref[:, 512 * branch : 512 * branch + 512],
            step_ref[:, 256 * branch : 256 * branch + 256],
            lx_ref[:, 256 * branch : 256 * branch + 256],
            lrow_ref[8 * branch : 8 * branch + 8, :], ahead, behind,
        )
        act = pre * sigmoid(pre)
        x = act[:, :256]
        b = act[:, 256:384]
        c = act[:, 384:]
        xs = x * step
        state = carry_ref[branch]
        states_ref[branch, 0] = state
        inner = dot3(c, b, NT)
        parts = []
        for h in range(4):
            decays = triangle(
                lower, log_wide[:, h * HDIM : h * HDIM + 1], log_rows[h : h + 1, :], inner
            )
            parts.append(dot1(decays, xs[:, h * HDIM : (h + 1) * HDIM]))
        within = jnp.concatenate(parts, axis=1)
        y = within + dot3(c, state) * jnp.exp2(log_wide)
        y_refs[branch][...] = y + wide_ref[17:18, :] * x
        edge = log_wide[BLOCK - 1 :] if lower else log_wide[:1]
        carry_ref[branch] = jnp.exp2(edge) * state + dot3(b, jnp.exp2(edge - log_wide) * xs, TN)


def own_row(ref, rank):
    return jnp.concatenate([ref[pl.ds(2 * rank, 1), :], ref[pl.ds(2 * rank + 1, 1), :]], axis=1)


def slope_kernel(
    at_ref, y_first_ref, y_second_ref, oh_ref, gate_ref, cot_ref, ow_ref, gain_ref,
    slope_ref, sums_ref,
):
    slope = lax.dot_general(cot_ref[...], ow_ref[...], NT, preferred_element_type=f32)
    slope_ref[...] = slope
    weighted = slope * own_row(gain_ref, at_ref[1])
    gates = dot1(oh_ref[...], gate_ref[...])
    for branch in range(2):
        g = (y_first_ref, y_second_ref)[branch][...] * gates[:, 256 * branch : 256 * branch + 256]
        for kind, product in enumerate((g * g, weighted * g)):
            at = 2 * branch + kind
            product = product[:, :128] + product[:, 128:]
            for j in range(product.shape[0] // 128):
                cols = slice(128 * j, 128 * j + 128)
                total = jnp.sum(jnp.transpose(product[cols]), axis=0, keepdims=True)
                for peer in range(sums_ref.shape[0]):
                    sums_ref[peer, at : at + 1, cols] = total


def mix_kernel(
    at_ref, y_first_ref, y_second_ref, oh_ref, oht_ref, gate_ref, slope_ref, gain_ref, sums_ref,
    mixed_ref, dy_first_ref, dy_second_ref, dgate_ref, dgain_ref,
):
    @pl.when(pl.program_id(0) == 0)
    def _():
        dgate_ref[...] = jnp.zeros_like(dgate_ref)
        dgain_ref[...] = jnp.zeros_like(dgain_ref)

    gain = own_row(gain_ref, at_ref[1])
    slope = slope_ref[...]
    sums = sums_ref[0]
    for peer in range(1, sums_ref.shape[0]):
        sums = sums + sums_ref[peer]
    scale = lax.rsqrt(sums / INNER + EPSILON)
    crossed = jnp.concatenate([sums[1:2], sums[1:2], sums[3:4], sums[3:4]], axis=0)
    weight = scale * scale * scale * crossed / INNER
    kind = iota(sums.shape, 0)
    weight = jnp.concatenate([weight[0:1], weight[0:1], weight[2:3], weight[2:3]], axis=0)
    rows = jnp.where(kind % 2 == 0, scale, weight)
    rows = jnp.concatenate([rows, rows] * 16, axis=0)
    parts = []
    for j in range(rows.shape[1] // 128):
        parts.append(jnp.transpose(rows[:, 128 * j : 128 * j + 128]))
    columns = jnp.concatenate(parts, axis=0)
    sloped = slope * gain
    gates = dot1(oh_ref[...], gate_ref[...])
    total = None
    for branch in range(2):
        gate = gates[:, 256 * branch : 256 * branch + 256]
        y = (y_first_ref, y_second_ref)[branch][...]
        g = y * gate
        scale = columns[:, 2 * branch : 2 * branch + 1]
        weight = columns[:, 2 * branch + 1 : 2 * branch + 2]
        normed = g * scale
        total = normed if total is None else total + normed
        dg = scale * sloped - weight * g
        (dy_first_ref, dy_second_ref)[branch][...] = dg * gate
        lanes = oht_ref[32 * branch : 32 * branch + 32, :]
        dgate_ref[branch] += dot2(lanes, dg * y)
    mixed_ref[...] = (total * gain).astype(bf16)
    dgain_ref[...] += jnp.sum(slope * total, axis=0, keepdims=True)


def backward_scan(
    branch, oh_ref, oht_ref, y_ref, state_ref, later_ref, dy_ref, pre_ref, step_ref, lx_ref,
    lrow_ref, wide_ref,
    tables_ref, steps_ref, logs_ref, skips_ref, carry_ref,
):
    skip = wide_ref[17:18, :]
    apart = iota((BLOCK, BLOCK), 0) - iota((BLOCK, BLOCK), 1)
    ahead = apart <= 0 if branch == 0 else apart >= 0
    behind = apart >= 0 if branch == 0 else apart <= 0
    onehot_t = oht_ref[32 * branch : 32 * branch + 32, :]
    pre, step, counts_t, log_wide, log_rows = scan_inputs(
        oh_ref[...], oht_ref[...], pre_ref[:, 512 * branch : 512 * branch + 512],
        step_ref[:, 256 * branch : 256 * branch + 256],
        lx_ref[:, 256 * branch : 256 * branch + 256],
        lrow_ref[8 * branch : 8 * branch + 8, :], ahead, behind,
    )
    counts_t = counts_t[32 * branch : 32 * branch + 32]
    logistic = sigmoid(pre)
    act = pre * logistic
    bend = logistic * (1.0 + pre * (1.0 - logistic))
    x = act[:, :256]
    b = act[:, 256:384]
    c = act[:, 384:]
    xs = x * step
    dy = dy_ref[...]
    own = y_ref[...] - skip * x
    state = state_ref[0, 0]
    pull = carry_ref[branch]
    xs_low = xs.astype(bf16)
    dy_low = dy.astype(bf16)
    inner = dot3(b, c, NT)
    parts = []
    slopes = jnp.zeros((BLOCK, BLOCK), f32)
    for h in range(4):
        wide = slice(h * HDIM, (h + 1) * HDIM)
        decays = triangle(
            branch == 1, log_wide[:, h * HDIM : h * HDIM + 1], log_rows[h : h + 1, :], None, -1.0
        )
        parts.append(dot1(inner * decays, dy_low[:, wide]))
        slopes = slopes + dot1(xs_low[:, wide], dy_low[:, wide], NT) * decays
    within = jnp.concatenate(parts, axis=1)
    faded = jnp.exp2(log_wide) * dy
    edge = log_wide[BLOCK - 1 :] if branch == 0 else log_wide[:1]
    tail = jnp.exp2(edge - log_wide)
    db = dot1(slopes, c) + dot1(tail * xs, pull, NT)
    dc = dot1(slopes, b, TN) + dot1(faded, state, NT)
    dxs = within + tail * dot1(b, pull)
    dlog = dy_low.astype(f32) * own - xs_low.astype(f32) * dxs
    edge_count = counts_t[:, BLOCK - 1 :] if branch == 0 else counts_t[:, :1]
    ahead = jnp.sum(later_ref[0, 0] * pull, axis=0, keepdims=True)
    logs_ref[...] += dot2(counts_t, dlog) + edge_count * ahead
    carry_ref[branch] = dot1(c, faded, TN) + jnp.exp2(edge) * pull
    dpre = jnp.concatenate([step * dxs + skip * dy, db, dc], axis=1) * bend
    tables_ref[...] += dot2(onehot_t, dpre)
    steps_ref[...] += dot2(onehot_t, x * dxs)
    skips_ref[...] += jnp.sum(dy * x, axis=0, keepdims=True)


def first_backward_kernel(at_ref, *refs):
    blocks = (refs[0:6], refs[6:12])
    tables, (cot_ref, mixed_ref) = refs[12:17], refs[17:19]
    sums, outer_ref = refs[19:24], refs[24]

    @pl.when(pl.program_id(0) == 0)
    def _():
        for ref in refs[19:]:
            ref[...] = jnp.zeros_like(ref)

    for branch in range(2):
        backward_scan(branch, *blocks[branch], *tables, *sums)
    outer_ref[...] += lax.dot_general(cot_ref[...], mixed_ref[...], TN, preferred_element_type=f32)


def second_backward_kernel(at_ref, *refs):
    blocks = (refs[0:6], refs[6:12])
    tables, sums_in = refs[12:17], refs[17:22]
    (
        ca_ref, cb_ref, tokens_ref, goht_ref, sums_ref, decay_ref, after_ref, gact_any, gbend_any,
        gstep_any, tab_ref, weight_any, cot_any, conv_x_ref, conv_bc_ref, dgate_ref, dgain_ref,
        packed_ref,
        mark_ref, found_ref, tables_ref, steps_ref, logs_ref, skips_ref, pull_ref,
        gact_ref, gbend_ref, gstep_ref, gate_w_ref, x_w_ref, bc_w_ref, step_w_ref, cot_ref, sems,
    ) = refs[22:]
    wide_ref = tables[4]
    sums = (tables_ref, steps_ref, logs_ref, skips_ref, pull_ref)
    own_at = pl.multiple_of(at_ref[1] * 256, 256)
    fetched = (
        (gact_any, gact_ref),
        (gbend_any, gbend_ref),
        (gstep_any, gstep_ref),
        (weight_any.at[pl.ds(own_at, 256), :], gate_w_ref),
        (weight_any.at[pl.ds(INNER + own_at, 256), :], x_w_ref),
        (weight_any.at[pl.ds(2 * INNER, 256), :], bc_w_ref),
        (weight_any.at[pl.ds(2 * INNER + 256, HEADS), :], step_w_ref),
        (cot_any, cot_ref),
    )
    copies = [
        pltpu.make_async_copy(source, target, sems.at[k])
        for k, (source, target) in enumerate(fetched)
    ]

    @pl.when(pl.program_id(0) == 0)
    def _():
        for copy in copies:
            copy.start()
        for ref, ref_in in zip(sums, sums_in):
            ref[...] = ref_in[...]

    for branch in range(2):
        backward_scan(branch, *blocks[branch], *tables, *sums)

    @pl.when(pl.program_id(0) == 1)
    def _():
        for copy in copies:
            copy.wait()
        far_and_pack(
            at_ref[1], pull_ref, wide_ref, ca_ref, cb_ref, tokens_ref, goht_ref,
            sums_ref, decay_ref, after_ref, gact_ref, gbend_ref, gstep_ref, tab_ref, gate_w_ref,
            x_w_ref, bc_w_ref, step_w_ref, cot_ref, conv_x_ref, conv_bc_ref, dgate_ref, dgain_ref,
            packed_ref, mark_ref, found_ref, tables_ref, steps_ref, logs_ref, skips_ref,
        )


def far_and_pack(
    rank, pull_ref, wide_ref, ca_ref, cb_ref, tokens_ref, goht_ref,
    sums_ref, decay_ref, after_ref, gact_ref, gbend_ref, gstep_ref, tab_ref, gate_w_ref,
    x_w_ref, bc_w_ref, step_w_ref, cot_ref, conv_x_ref, conv_bc_ref, dgate_ref, dgain_ref,
    packed_ref, mark_ref, found_ref, tables_ref, steps_ref, logs_ref, skips_ref,
):
    gram_x = gact_ref[:, :256]
    gram_b = gact_ref[:, 256:]
    gram_step = gstep_ref[...]
    gram_xs = gram_x * gram_step
    dxs = jnp.zeros((CODES * CODES, 256), f32)
    db = jnp.zeros((CODES * CODES, 128), f32)
    found = []
    expanded = expand_grams(sums_ref[...])
    for branch, weights in enumerate(expanded):
        pull = pull_ref[branch]
        met = dot1(gram_b, pull)
        dxs = dxs + weights * met
        db = db + dot1(weights * gram_xs, pull, NT)
        found.append(gram_xs * met)
    dpre = jnp.concatenate([gram_step * dxs, db], axis=1) * gbend_ref[...]
    gram_t = goht_ref[...]
    tables_ref[:, :384] += dot2(gram_t, dpre)
    steps_ref[...] += dot2(gram_t, gram_x * dxs)
    table = gather_grams(found).astype(bf16)
    early_codes = iota((2 * CODES, 128), 0)
    late_codes = iota((CODES, 128), 0)

    def look_up(shard, unused):
        at = pl.ds(pl.multiple_of(shard * 8, 8), 8)
        early = ca_ref[at, :]
        late = cb_ref[at, :]
        for j in range(8):
            mark_ref[:, 128 * j : 128 * j + 128] = ones_where(early[j : j + 1] == early_codes)
        looked = dot1(table, mark_ref[...], TN)
        for h in range(4):
            rows = []
            for j in range(8):
                part = looked[32 * h : 32 * h + 32, 128 * j : 128 * j + 128]
                mine = late[j : j + 1] == late_codes
                rows.append(jnp.sum(jnp.where(mine, part, 0.0), axis=0, keepdims=True))
            found_ref[h, at, :] = jnp.concatenate(rows, axis=0)
        return unused

    lax.fori_loop(0, 16, look_up, 0, unroll=4)
    lane_head = iota((1, 256), 1) // HDIM
    sub = iota((8, 256), 0)
    far = jnp.zeros((8, 256), f32)
    for h in range(4):
        weighted = found_ref[h] * decay_ref[h]
        for symbol in range(5):
            total = jnp.sum(weighted * after_ref[symbol], axis=0, keepdims=True)
            total = jnp.sum(total, axis=1, keepdims=True)
            far = far + jnp.where((lane_head == h) & (sub == symbol + 1), total, 0.0)

    gate_tab = tab_ref[:, :256]
    x_tab = tab_ref[:, 256:512]
    bc_tab = tab_ref[:, 512:768]
    logistic = sigmoid(gate_tab)
    gate_part = (dgate_ref[0, 24:32, :] + dgate_ref[1, 24:32, :]) * (
        logistic * (1.0 + gate_tab * (1.0 - logistic))
    )
    conv_x = conv_x_ref[...]
    conv_bc = conv_bc_ref[...]
    x_part = jnp.zeros((8, 256), f32)
    bc_part = jnp.zeros((8, 256), f32)
    x_taps = []
    bc_taps = []
    for k in range(KCONV):
        dtap_x = tables_ref[8 * k : 8 * k + 8, :256]
        dtap_bc = tables_ref[8 * k : 8 * k + 8, 256:]
        x_part = x_part + conv_x[k : k + 1] * dtap_x
        bc_part = bc_part + conv_bc[k : k + 1] * dtap_bc
        x_taps.append(jnp.sum(dtap_x * x_tab, axis=0, keepdims=True))
        bc_taps.append(jnp.sum(dtap_bc * bc_tab, axis=0, keepdims=True))
    bias = tables_ref[6:7, :]
    same = ones_where(iota((256, 256), 0) // HDIM == iota((256, 256), 1) // HDIM)
    log_part = dot_exact(logs_ref[24:32, :], same) + far
    step_part = dot_exact(steps_ref[24:32, :], same) - wide_ref[16:17, :] * log_part
    step_part = step_part * wide_ref[0:8, :]
    rate_part = jnp.sum(log_part * wide_ref[8:16, :], axis=0, keepdims=True)
    skip_part = dot_exact(jnp.broadcast_to(skips_ref[...], (8, 256)), same)
    valid = (sub >= 1) & (sub <= 5)
    step_part = jnp.where(valid, step_part, 0.0)
    step_rows = jnp.where(
        sub == 0,
        jnp.sum(step_part, axis=0, keepdims=True),
        jnp.where(sub == 6, rate_part, jnp.where(sub == 7, skip_part, step_part)),
    )
    spread = iota((256, 128), 1)
    narrow = ones_where(
        (iota((256, 128), 0) % HDIM == 0)
        & (rank * 4 + iota((256, 128), 0) // HDIM == spread)
    )
    step_heads = dot_exact(step_rows, narrow)

    def against(part, weights):
        first_piece = part.astype(bf16)
        rest = part - first_piece.astype(f32)
        second_piece = rest.astype(bf16)
        third_piece = rest - second_piece.astype(f32)
        return dot1(first_piece, weights) + (
            dot1(second_piece, weights) + dot1(third_piece, weights)
        )

    embed_part = (
        dot1(tokens_ref[...], cot_ref[...])[24:32]
        + against(jnp.where(valid, gate_part, 0.0), gate_w_ref[...])
        + against(jnp.where(valid, x_part, 0.0), x_w_ref[...])
        + against(jnp.where(valid, bc_part, 0.0), bc_w_ref[...])
        + against(jnp.where(valid[:, :HEADS], step_heads[:, :HEADS], 0.0), step_w_ref[...])
    )

    def rows_of(part, zero, six, seven):
        return jnp.where(
            sub == 0, zero, jnp.where(sub == 6, six, jnp.where(sub == 7, seven, part))
        )

    gate_rows = rows_of(gate_part, x_taps[0], x_taps[1], x_taps[2])
    x_rows = rows_of(x_part, x_taps[3], bias[:, :256], dgain_ref[...])
    bc_rows = rows_of(bc_part, bc_taps[0], bc_taps[1], bc_taps[2])
    embed_first = rows_of(embed_part[:, :256], bc_taps[3], bias[:, 256:], 0.0)
    for half in range(2):
        cols = slice(128 * half, 128 * half + 128)
        packed_ref[half] = gate_rows[:, cols]
        packed_ref[2 + half] = x_rows[:, cols]
        packed_ref[4 + half] = bc_rows[:, cols]
        packed_ref[7 + half] = embed_first[:, cols]
    packed_ref[6] = step_heads
    for piece in range(2, 8):
        packed_ref[7 + piece] = embed_part[:, 128 * piece : 128 * piece + 128]
    packed_ref[15] = jnp.zeros((8, 128), f32)


def out_kernel(mixed_ref, ow_ref, token_ref, embed_ref, out_ref):
    total = dot1(token_ref[...], embed_ref[...])
    for peer in range(mixed_ref.shape[0]):
        total = total + dot1(mixed_ref[peer], ow_ref[256 * peer : 256 * peer + 256, :])
    out_ref[...] = total.astype(bf16)


def sum_kernel(pieces_ref, spread_ref):
    total = pieces_ref[0]
    for k in range(1, pieces_ref.shape[0]):
        total = total + pieces_ref[k]
    spread_ref[...] = jnp.broadcast_to(total[None], spread_ref.shape)


def final_kernel(
    whole_ref, embed_ref,
    w_in_ref, embedding_ref, conv_ref, bias_ref, dt_ref, rate_ref, skip_ref, gain_ref,
):
    def summed(piece):
        total = whole_ref[8 * piece]
        for k in range(1, 8):
            total = total + whole_ref[8 * piece + k]
        return total

    embed = embed_ref[...]

    def outer(table, first):
        one = table.astype(bf16)
        rest = table - one.astype(f32)
        two = rest.astype(bf16)
        three = rest - two.astype(f32)
        pieces = jnp.concatenate([one.astype(f32), two.astype(f32), three], axis=0)
        value = dot1(embed, pieces)
        w_in_ref[:, first : first + table.shape[1]] = value

    for rank in range(8):
        for half in range(2):
            gate = whole_ref[8 * half + rank]
            x = whole_ref[8 * (2 + half) + rank]
            at = 256 * rank + 128 * half
            cols = slice(at, at + 128)
            outer(gate, at)
            outer(x, INNER + at)
            conv_ref[0:1, cols] = gate[0:1]
            conv_ref[1:2, cols] = gate[6:7]
            conv_ref[2:3, cols] = gate[7:8]
            conv_ref[3:4, cols] = x[0:1]
            bias_ref[2 * rank + half : 2 * rank + half + 1, :] = x[6:7]
            gain_ref[2 * rank + half : 2 * rank + half + 1, :] = x[7:8]
    for half in range(2):
        bc = summed(4 + half)
        at = INNER + 128 * half
        cols = slice(at, at + 128)
        outer(bc, INNER + at)
        rest = summed(7 + half)
        conv_ref[0:1, cols] = bc[0:1]
        conv_ref[1:2, cols] = bc[6:7]
        conv_ref[2:3, cols] = bc[7:8]
        conv_ref[3:4, cols] = rest[0:1]
        bias_ref[16 + half : 17 + half, :] = rest[6:7]
    steps = summed(6)[:, :HEADS]
    outer(steps, 2 * INNER + 2 * STATE)
    dt_ref[...] = steps[0:1]
    rate_ref[...] = steps[6:7]
    skip_ref[...] = steps[7:8]
    for piece in range(8):
        embedding_ref[:, 128 * piece : 128 * piece + 128] = summed(7 + piece)[1:6]


VMEM = pl.BlockSpec(memory_space=pltpu.VMEM)
VMEM_LIMIT = 62 * 1024 * 1024
TOKEN_STEPS = 2
ANY = pl.BlockSpec(memory_space=pl.ANY)


def whole(array):
    zeros = (0,) * array.ndim
    return pl.BlockSpec(array.shape, lambda i, at: zeros)


def own(shape, index):
    return pl.BlockSpec(shape, index)


def call(kernel, at, operands, outs, scratch=(), cost=5e9, steps=1):
    arrays = [item[0] if isinstance(item, tuple) else item for item in operands]
    specs = [
        (own(*item[1:]) if len(item) > 2 else ANY) if isinstance(item, tuple) else whole(item)
        for item in operands
    ]
    shapes = [jax.ShapeDtypeStruct(item[0], item[1]) for item in outs]
    out_specs = [
        own(item[2], item[3]) if len(item) > 2 else whole(shape)
        for item, shape in zip(outs, shapes)
    ]
    return pl.pallas_call(
        kernel,
        out_shape=shapes,
        grid_spec=pltpu.PrefetchScalarGridSpec(
            num_scalar_prefetch=1,
            grid=(steps,),
            in_specs=specs,
            out_specs=out_specs,
            scratch_shapes=list(scratch),
        ),
        compiler_params=pltpu.CompilerParams(vmem_limit_bytes=VMEM_LIMIT),
        cost_estimate=pl.CostEstimate(flops=int(cost), bytes_accessed=4000000, transcendentals=0),
    )(at, *arrays)


def call_plain(kernel, operands, outs, cost=1e9):
    return pl.pallas_call(
        kernel,
        out_shape=[jax.ShapeDtypeStruct(shape, kind) for shape, kind in outs],
        in_specs=[VMEM] * len(operands),
        out_specs=[VMEM] * len(outs),
        compiler_params=pltpu.CompilerParams(vmem_limit_bytes=VMEM_LIMIT),
        cost_estimate=pl.CostEstimate(flops=int(cost), bytes_accessed=1000000, transcendentals=0),
    )(*operands)


def gather(shard, axis):
    devices = lax.axis_size(axis)
    spread = jnp.broadcast_to(shard[None], (devices,) + shard.shape)
    return lax.all_to_all(spread, axis, split_axis=0, concat_axis=0, tiled=True)


def gather_by_flips(array, axis, flips):
    pairs = [[(i, i ^ flip) for i in range(lax.axis_size(axis))] for flip in flips]
    return jnp.concatenate([array] + [lax.ppermute(array, axis, pair) for pair in pairs], axis=0)


def exchange(array, axis):
    return lax.all_to_all(array, axis, split_axis=0, concat_axis=0, tiled=True)


def body(
    base_ids, embedding, in_weight, conv_weight, conv_bias, dt_bias, a_log, skip_weight, norm_gain,
    out_weight, cotangent,
):
    groups = lax.axis_size("head")
    shards = lax.axis_size("seq")
    width = HEADS // groups * HDIM
    head_rank = lax.axis_index("head")
    seq_rank = lax.axis_index("seq")
    length = base_ids.shape[0]
    token_rows = length // groups
    at = jnp.stack([seq_rank, head_rank]).astype(jnp.int32)

    near = gather_by_flips(base_ids.reshape(1, 8, 128), "seq", (1, 8, 9))
    near, in_weight = lax.optimization_barrier((near, in_weight))
    ids = gather_by_flips(near, "seq", (2, 4, 6))
    cot_all = gather(cotangent, "head").reshape(length, D)
    weight_t = in_weight.T
    gain_rows = norm_gain.reshape(INNER // 128, 128)
    grams = _gram_onehot()
    gram_rows = jnp.asarray(grams, bf16)
    gram_cols = jnp.asarray(np.ascontiguousarray(grams[:, :32].T), bf16)
    weights = [
        (weight_t, (width, D), lambda i, at: (at[1], 0)),
        (weight_t, (width, D), lambda i, at: (INNER // width + at[1], 0)),
        (weight_t, (256, D), lambda i, at: (16, 0)),
        (weight_t, (128, D), lambda i, at: (34, 0)),
    ]
    convs = [
        (conv_weight, (KCONV, width), lambda i, at: (0, at[1])),
        (conv_weight, (KCONV, width), lambda i, at: (0, INNER // width)),
    ]
    count = CODES * CODES
    big, logs, log_rows, tab, wide, gxs, gbt = call(
        prep_kernel,
        at,
        [
            embedding,
            *weights,
            *convs,
            conv_bias.reshape(conv_bias.shape[0] // 128, 128),
            dt_bias[None, :],
            a_log[None, :],
            skip_weight[None, :],
            gram_rows,
        ],
        [
            ((128, 2048), bf16),
            ((128, 512), bf16),
            ((16, 128), f32),
            ((8, 768), f32),
            ((24, width), f32),
            ((count, width), f32),
            ((STATE, count), f32),
        ],
        cost=6e9,
    )

    blocks = length // BLOCK

    tables = [
        (big, (128, 1024), lambda k, at: (0, 0)),
        (big, (128, 512), lambda k, at: (0, 2)),
        logs,
        log_rows,
        wide,
    ]

    def rows_at(array, rows, index):
        return (array, (rows, array.shape[1]), lambda k, at: (index(k), 0))

    y_first, y_second, states, sums, decays, after, onehot, onehot_t, early, late = call(
        forward_kernel,
        at,
        [ids, *tables, gxs, gbt],
        [
            ((length, width), f32, (BLOCK, width), lambda k, at: (k, 0)),
            ((length, width), f32, (BLOCK, width), lambda k, at: (blocks - 1 - k, 0)),
            (
                (2, blocks, STATE, width), f32,
                (2, 1, STATE, width), lambda k, at: (0, k, 0, 0),
            ),
            ((2 * CODES, 128), f32),
            ((4, 128, 128), f32),
            ((5, 128, 128), f32),
            ((length, 128), bf16),
            ((128, length), bf16),
            ((128, 128), jnp.int32),
            ((128, 128), jnp.int32),
        ],
        [
            pltpu.VMEM((8, 128, 128), jnp.int32),
            pltpu.VMEM((128, 4096), bf16),
            pltpu.VMEM((2 * CODES, 4096), bf16),
            pltpu.VMEM((2, STATE, width), f32),
        ],
        cost=1.5e10,
        steps=blocks,
    )

    chunk = length // TOKEN_STEPS
    gates = (big, (128, 512), lambda k, at: (0, 3))
    y_rows = [rows_at(y, chunk, lambda k: k) for y in (y_first, y_second)]
    hot_rows = rows_at(onehot, chunk, lambda k: k)
    slope, row_sums = call(
        slope_kernel,
        at,
        [
            *y_rows,
            hot_rows,
            gates,
            rows_at(cot_all, chunk, lambda k: k),
            (out_weight, (width, D), lambda k, at: (at[1], 0)),
            gain_rows,
        ],
        [
            ((length, width), f32, (chunk, width), lambda k, at: (k, 0)),
            ((groups, 4, length), f32, (groups, 4, chunk), lambda k, at: (0, 0, k)),
        ],
        cost=4e9,
        steps=TOKEN_STEPS,
    )
    row_sums, big, ids_later, embed_later = lax.optimization_barrier(
        (row_sums, big, base_ids, embedding)
    )
    gact, gbend, gstep = call(
        gram_kernel,
        at,
        [
            gram_rows,
            (big, (128, 512), lambda k, at: (0, 0)),
            (big, (128, 256), lambda k, at: (0, 4)),
        ],
        [((count, 384), f32), ((count, 384), f32), ((count, width), f32)],
        cost=2e9,
    )
    row_sums = exchange(row_sums, "head")
    mixed, dy_first, dy_second, dgate, dgain = call(
        mix_kernel,
        at,
        [
            *y_rows,
            hot_rows,
            (onehot_t, (128, chunk), lambda k, at: (0, k)),
            gates,
            rows_at(slope, chunk, lambda k: k),
            gain_rows,
            (row_sums, (groups, 4, chunk), lambda k, at: (0, 0, k)),
        ],
        [
            ((length, width), bf16, (chunk, width), lambda k, at: (k, 0)),
            ((length, width), f32, (chunk, width), lambda k, at: (k, 0)),
            ((length, width), f32, (chunk, width), lambda k, at: (k, 0)),
            ((2, 32, width), f32),
            ((1, width), f32),
        ],
        cost=4e9,
        steps=TOKEN_STEPS,
    )

    mixed_all = exchange(mixed.reshape(groups, token_rows, width), "head")

    def scan_operands(first_step):
        operands = []
        for branch, y, dy in ((0, y_first, dy_first), (1, y_second, dy_second)):

            def nth(k):
                return first_step + k

            def block(k, branch=branch):
                return blocks - 1 - nth(k) if branch == 0 else nth(k)

            def state(k, at, branch=branch):
                return (branch, blocks - 1 - nth(k), 0, 0)

            def later(k, at, branch=branch):
                return (branch, jnp.minimum(blocks - nth(k), blocks - 1), 0, 0)

            one = (1, 1, STATE, width)
            operands += [
                rows_at(onehot, BLOCK, block),
                (onehot_t, (128, BLOCK), lambda k, at, block=block: (0, block(k))),
                rows_at(y, BLOCK, block),
                (states, one, state),
                (states, one, later),
                rows_at(dy, BLOCK, block),
            ]
        return operands + tables

    accumulators = [
        ((32, 512), f32),
        ((32, width), f32),
        ((32, width), f32),
        ((1, width), f32),
        ((2, STATE, width), f32),
    ]
    *grads, partial = call(
        first_backward_kernel,
        at,
        scan_operands(0)
        + [rows_at(cot_all, length // 2, lambda k: k), rows_at(mixed, length // 2, lambda k: k)],
        accumulators + [((D, width), f32)],
        cost=1.5e10,
        steps=blocks // 2,
    )
    mixed_all, partial, grads = lax.optimization_barrier((mixed_all, partial, grads))
    partial = exchange(partial.reshape(shards, D // shards, width), "seq")
    (packed,) = call(
        second_backward_kernel,
        at,
        scan_operands(blocks // 2)
        + [
            *grads,
            early,
            late,
            (onehot_t, (32, token_rows), lambda k, at: (0, at[1])),
            gram_cols,
            sums,
            decays,
            after,
            (gact,),
            (gbend,),
            (gstep,),
            tab,
            (weight_t,),
            (cotangent,),
            *convs,
            dgate,
            dgain,
        ],
        [((shards, 8, 128), f32)],
        [
            pltpu.VMEM((2 * CODES, 1024), bf16),
            pltpu.VMEM((4, 128, 128), f32),
            *[pltpu.VMEM(shape, kind) for shape, kind in accumulators],
            pltpu.VMEM((count, 384), f32),
            pltpu.VMEM((count, 384), f32),
            pltpu.VMEM((count, width), f32),
            pltpu.VMEM((width, D), bf16),
            pltpu.VMEM((width, D), bf16),
            pltpu.VMEM((256, D), bf16),
            pltpu.VMEM((HEADS, D), bf16),
            pltpu.VMEM((token_rows, D), bf16),
            pltpu.SemaphoreType.DMA((8,)),
        ],
        cost=2e10,
        steps=blocks // 2,
    )
    packed, partial = lax.optimization_barrier((packed, partial))

    grad_w_out = jnp.sum(partial, axis=0).T
    token_ids = lax.dynamic_slice_in_dim(ids_later, head_rank * token_rows, token_rows, 0)
    alphabet = jnp.arange(5, dtype=jnp.int32)
    token_hot = (token_ids[:, None] == alphabet[None, :]).astype(bf16)
    (layer_out,) = call_plain(
        out_kernel,
        [mixed_all, out_weight, token_hot, embedding],
        [((token_rows, D), bf16)],
        4e9,
    )

    pieces = exchange(packed, "seq")
    row_count = D // shards
    columns = lax.dynamic_slice_in_dim(embed_later, seq_rank * row_count, row_count, 1)
    columns = jnp.pad(columns, ((1, 2), (0, 0)))
    columns = jnp.concatenate([columns] * 3, axis=0).T
    pieces, layer_out, grad_w_out, columns = lax.optimization_barrier(
        (pieces, layer_out, grad_w_out, columns)
    )
    (spread,) = call_plain(sum_kernel, [pieces], [((shards * groups, 8, 128), f32)], 1e8)
    everything = exchange(spread, ("seq", "head"))
    w_in, embed, conv, bias, dt, rate, skip, gain = call_plain(
        final_kernel,
        [everything, columns],
        [
            ((row_count, in_weight.shape[1]), f32),
            (embedding.shape, f32),
            (conv_weight.shape, f32),
            ((conv_bias.shape[0] // 128, 128), f32),
            ((1, HEADS), f32),
            ((1, HEADS), f32),
            ((1, HEADS), f32),
            ((INNER // 128, 128), f32),
        ],
    )
    return (
        layer_out, w_in, grad_w_out, embed, conv, bias.reshape(-1), dt[0], rate[0], skip[0],
        gain.reshape(-1),
    )


def solution(mesh):
    return jax.shard_map(
        body,
        mesh=mesh,
        in_specs=(P("seq"), P(), P(), P(), P(), P(), P(), P(), P(), P(), P(("seq", "head"), None)),
        out_specs=(
            P(("seq", "head"), None),
            P("seq", None),
            P("head", "seq"),
            P(),
            P(),
            P(),
            P(),
            P(),
            P(),
            P(),
        ),
        check_vma=False,
    )
```

time: 160 us -> 144 us (0.900)
  waiting for transfers between devices: 33.2 us -> 5.19 us
  blocking collectives: 0 us -> 23.2 us
  local copies, waits for them, and re-layouts: 9.36 us -> 5.33 us
  starting transfers between devices: 39.5 us -> 36 us
  Pallas kernels: 72.8 us -> 70.1 us
    all_to_all x6 -> x4, waiting for transfers between devices: 33.2 us -> 3.6 us  [exchange(): return lax.all_to_all(array, axis, split_axis=0, concat_axis=0, tiled=True)]
    all_to_all x0 -> x1, blocking collectives: none -> 23.2 us  [exchange(): return lax.all_to_all(array, axis, split_axis=0, concat_axis=0, tiled=True)]
    all_to_all x6 -> x4, starting transfers between devices: 33.1 us -> 21.3 us  [exchange(): return lax.all_to_all(array, axis, split_axis=0, concat_axis=0, tiled=True)]
    ppermute x0 -> x6, starting transfers between devices: none -> 7.53 us  [gather_by_flips(): lax.ppermute(array, axis, pair)]
    pallas_call x6 -> x7, Pallas kernels: 69.1 us -> 62.3 us  [call(): pl.pallas_call(kernel, out_shape=shapes, grid_spec=pltpu.PrefetchScalarGr...]
    pallas_call x3, Pallas kernels: 3.63 us -> 7.83 us  [call_plain(): pl.pallas_call(kernel, out_shape=[jax.ShapeDtypeStruct(shape, kind) for s...]
    unnamed x12 -> x8, local copies, waits for them, and re-layouts: 4.2 us -> 1.28 us
    broadcast_in_dim x2 -> x0, local copies, waits for them, and re-layouts: 2.89 us -> none  [the longest x1 1.58 us: body(): cot_spread = jnp.broadcast_to(cotangent[None], (groups,) + cotangent.shape)]
  transfers between devices with their start and end apart: 7 -> 11, of which waited for: 4 -> 5; matrix products, arithmetic and copies ran while one was open for 3% -> 5% of each run, Pallas kernels for 37% -> 39%
where the time goes in v3:
time: 144 us; the launch traced here: 143 us
  Pallas kernels  70.1 us (49%)
  starting transfers between devices  36 us (25%)
  blocking collectives  23.2 us (16%)
  local copies, waits for them, and re-layouts  5.33 us (4%)
  waiting for transfers between devices  5.19 us (4%)
  other arithmetic  2.63 us (2%)
    pallas_call x7, Pallas kernels, call(): pl.pallas_call(kernel, out_shape=shapes, grid_spec=pltpu.PrefetchScalarGr...  62.3 us
    all_to_all x1, blocking collectives, exchange(): return lax.all_to_all(array, axis, split_axis=0, concat_axis=0, tiled=True)  23.2 us
    all_to_all x4, starting transfers between devices, exchange(): return lax.all_to_all(array, axis, split_axis=0, concat_axis=0, tiled=True)  21.3 us
    pallas_call x3, Pallas kernels, call_plain(): pl.pallas_call(kernel, out_shape=[jax.ShapeDtypeStruct(shape, kind) for s...  7.83 us
    ppermute x6, starting transfers between devices, gather_by_flips(): lax.ppermute(array, axis, pair)  7.53 us
    all_to_all x1, starting transfers between devices, gather(): return lax.all_to_all(spread, axis, split_axis=0, concat_axis=0, tiled=True)  7.16 us
    all_to_all x4, waiting for transfers between devices, exchange(): return lax.all_to_all(array, axis, split_axis=0, concat_axis=0, tiled=True)  3.6 us
  transfers between devices with their start and end apart: 11, of which 5 were waited for; matrix products, arithmetic and copies ran while one was open for 5% of the time, Pallas kernels for 39%

profile of v3, /device:TPU:0, one launch (start us, length us, event | category | flops | bytes accessed | tf_op | source)
XLA Modules:
  0.0 143.1 jit_solution(15609687903246290085)
XLA Ops:
  0.7 1.7 %collective-permute-start.1 = (s32[1,8,128]{2,1,0:T(8,128)}, s32[1,8,128]{2,1,0:T(8,128)S(1)}, u32[]{:S(2)}, u32[]{:S(2)}) collective-permute-start(s32[1,8,128]{2,1,0:T(8,128)} %bitcast.30), channel_id=1, source_target_pairs={{0,64},{8,72},{16,80},{24,88},{32,96},{40,104},{48,112},{56,120},{... | collective-permute-start | bytes 12296 | tf_op jit(solution)/shard_map/ppermute | solution.py:881
  2.6 2.5 %broadcast_in_dim.20 = bf16[8,128,1024]{2,1,0:T(8,128)(2,1)} broadcast(bf16[128,1024]{1,0:T(8,128)(2,1)} %refs_34_.1), dimensions={1,2} | broadcast | bytes 2359296 | tf_op jit(solution)/shard_map/broadcast_in_dim | solution.py:875
  5.1 7.2 %all-to-all-start = ((bf16[8,128,1024]{2,1,0:T(8,128)(2,1)}), bf16[8,128,1024]{2,1,0:T(8,128)(2,1)}, u32[]{:S(2)}, u32[]{:S(2)}) async-start(bf16[8,128,1024]{2,1,0:T(8,128)(2,1)} %broadcast_in_dim.20), calls=%async_computation | async-start | bytes 4194304 | tf_op jit(solution)/shard_map/all_to_all | solution.py:876
  12.3 0.6 pad_add_fusion.2.at_ref
  12.9 2.0 %collective-permute-start.3 = (s32[4,8,128]{2,1,0:T(8,128)S(1)}, s32[4,8,128]{2,1,0:T(8,128)S(1)}, u32[]{:S(2)}, u32[]{:S(2)}) collective-permute-start(s32[4,8,128]{2,1,0:T(8,128)S(1)} %pad_add_fusion.1), channel_id=1, source_target_pairs={{0,16},{8,24},{16,0},{24,8},{32,48},{40,56},{48,32},{56,40},{64,80... | collective-permute-start | bytes 49160 | tf_op jit(solution)/shard_map/ppermute | solution.py:881
  14.9 3.6 %collective-permute-start.4 = (s32[4,8,128]{2,1,0:T(8,128)S(1)}, s32[4,8,128]{2,1,0:T(8,128)S(1)}, u32[]{:S(2)}, u32[]{:S(2)}) collective-permute-start(s32[4,8,128]{2,1,0:T(8,128)S(1)} %pad_add_fusion.1), channel_id=1, source_target_pairs={{0,32},{8,40},{16,48},{24,56},{32,0},{40,8},{48,16},{56,24},{64,96... | collective-permute-start | bytes 49160 | tf_op jit(solution)/shard_map/ppermute | solution.py:881
  18.5 4.6 %shard_map.204 = (bf16[128,2048]{1,0:T(8,128)(2,1)}, bf16[128,512]{1,0:T(8,128)(2,1)}, f32[16,128]{1,0:T(8,128)}, f32[8,768]{1,0:T(8,128)}, f32[24,256]{1,0:T(8,...) custom-call(s32[2]{0:T(128)} %pad_add_fusion.2.at_ref, bf16[5,1024]{1,0:T(8,128)(2,1)} %embed_ref.3, ...), custom_call_target="tpu_custom_call" | custom-call | flops 6000000000 | bytes 4000000 | tf_op jit(solution)/shard_map/pallas_call | solution.py:847
  23.4 0.6 pad_add_fusion.ids_ref
  24.1 16.1 %shard_map.205 = (f32[1024,256]{1,0:T(8,128)}, f32[1024,256]{1,0:T(8,128)}, f32[2,4,128,256]{3,2,1,0:T(8,128)}, f32[64,128]{1,0:T(8,128)}, f32[4,128,128]{2,1,0:...) custom-call(s32[2]{0:T(128)} %pad_add_fusion.2.at_ref, ...), custom_call_target="tpu_custom_call" | custom-call | flops 15000000512 | bytes 4000000 | tf_op jit(solution)/shard_map/pallas_call | solution.py:847
  40.2 1.2 all-to-all-done
  41.4 4.9 %shard_map.206 = (f32[1024,256]{1,0:T(8,128)}, f32[8,4,1024]{2,1,0:T(4,128)}) custom-call(s32[2]{0:T(128)} %pad_add_fusion.2.at_ref, f32[1024,256]{1,0:T(8,128)} %get-tuple-element.80.y_first_ref.refs_2_, f32[1024,256]{1,0:T(8,128)} %get-tuple-element.82.y_second_ref.refs_8_, bf16[1024,128]{1,0:T(8,128)(2,1)} %get-tuple-element.78.oh_ref.refs_0_.refs_6_, ...), custom_call_target="tpu_custom_call" | custom-call | flops 4000000000 | bytes 4000000 | tf_op jit(solution)/shard_map/pallas_call | solution.py:847
  46.3 6.0 %all-to-all-start.1 = ((f32[8,4,1024]{2,1,0:T(4,128)}), f32[8,4,1024]{2,1,0:T(4,128)S(1)}, u32[]{:S(2)}, u32[]{:S(2)}) async-start(f32[8,4,1024]{2,1,0:T(4,128)} %get-tuple-element.85), calls=%async_computation.1 | async-start | bytes 262144 | tf_op jit(solution)/shard_map/all_to_all | solution.py:885
  52.4 0.7 fusion.token_ref
  53.1 0.8 constant_dynamic-slice_fusion
  53.8 0.7 copy.24
  54.5 4.5 %shard_map.209 = (f32[1024,384]{1,0:T(8,128)}, f32[1024,384]{1,0:T(8,128)}, f32[1024,256]{1,0:T(8,128)}) custom-call(s32[2]{0:T(128)} %pad_add_fusion.2.at_ref, bf16[1024,128]{1,0:T(8,128)(2,1)} %constant.25.clone.goh_ref, bf16[128,2048]{1,0:T(8,128)(2,1)} %get-tuple-element.105.pre_ref.step_ref.gate_ref.refs_12_.refs_13_, ...), custom_call_target="tpu_custom_call" | custom-call | flops 2000000000 | bytes 4000000 | tf_op jit(solution)/shard_map/pallas_call | solution.py:847
  59.1 1.4 all-to-all-done.1.sums_ref
  60.5 0.6 copy-done.2
  61.1 5.4 %shard_map.207 = (bf16[1024,256]{1,0:T(8,128)(2,1)}, f32[1024,256]{1,0:T(8,128)}, f32[1024,256]{1,0:T(8,128)}, f32[2,32,256]{2,1,0:T(8,128)}, f32[1,256]{1,0:T(1,128)}) custom-call(s32[2]{0:T(128)} %pad_add_fusion.2.at_ref, f32[1024,256]{1,0:T(8,128)} %get-tuple-element.80.y_first_ref.refs_2_, f32[1024,256]{1,0:T(8,128)} %get-tuple-element.82.y_second_ref.refs_8_, ...), custom_call_target="tpu_custom_call" | custom-call | flops 4000000000 | bytes 4000000 | tf_op jit(solution)/shard_map/pallas_call | solution.py:847
  66.5 5.8 %all-to-all-start.2 = ((bf16[8,128,256]{2,1,0:T(8,128)(2,1)}), bf16[8,128,256]{2,1,0:T(8,128)(2,1)S(1)}, u32[]{:S(2)}, u32[]{:S(2)}) async-start(bf16[8,128,256]{2,1,0:T(8,128)(2,1)} %bitcast.25), calls=%async_computation.2 | async-start | bytes 1048576 | tf_op jit(solution)/shard_map/all_to_all | solution.py:885
  72.3 10.7 %shard_map.208 = (f32[32,512]{1,0:T(8,128)}, f32[32,256]{1,0:T(8,128)}, f32[32,256]{1,0:T(8,128)}, f32[1,256]{1,0:T(1,128)}, f32[2,128,256]{2,1,0:T(8,128)}, /*index=5*/f32[1024,256]{1,0:T(8,128)}) custom-call(s32[2]{0:T(128)} %pad_add_fusion.2.at_ref, bf16[1024,128]{1,0:T(8,128)(2,1)} %get-tuple-element.78.oh_ref.refs_0_.refs_6_, ...), custom_call_target="tpu_custom_call" | custom-call | flops 15000000512 | bytes 4000000 | tf_op jit(solution)/shard_map/pallas_call | solution.py:847
  83.1 4.3 %all-to-all-start.3 = ((f32[16,64,256]{2,1,0:T(8,128)}), f32[16,64,256]{2,1,0:T(8,128)S(1)}, u32[]{:S(2)}, u32[]{:S(2)}) async-start(f32[16,64,256]{2,1,0:T(8,128)} %bitcast.24), calls=%async_computation.3 | async-start | bytes 2097152 | tf_op jit(solution)/shard_map/all_to_all | solution.py:885
  87.4 16.1 %shard_map.210 = f32[16,8,128]{2,1,0:T(8,128)} custom-call(s32[2]{0:T(128)} %pad_add_fusion.2.at_ref, bf16[1024,128]{1,0:T(8,128)(2,1)} %get-tuple-element.78.oh_ref.refs_0_.refs_6_, bf16[128,1024]{1,0:T(8,128)(2,1)} %get-tuple-element.79.oht_ref.refs_1_.refs_7_.refs_24_, f32[1024,256]{1,0:T(8,128)} %get-tuple-element.80.y_first_ref.refs_2_, ...), custom_call_target="tpu_custom_call" | custom-call | flops 20000000000 | bytes 4000000 | tf_op jit(solution)/shard_map/pallas_call | solution.py:847
  103.5 0.5 all-to-all-done.3
  104.0 5.2 %all-to-all-start.4 = ((f32[16,8,128]{2,1,0:T(8,128)}), f32[16,8,128]{2,1,0:T(8,128)S(1)}, u32[]{:S(2)}, u32[]{:S(2)}) async-start(f32[16,8,128]{2,1,0:T(8,128)} %shard_map.210), calls=%async_computation.4 | async-start | bytes 131072 | tf_op jit(solution)/shard_map/all_to_all | solution.py:885
  109.1 3.8 %shard_map.211 = bf16[128,1024]{1,0:T(8,128)(2,1)} custom-call(bf16[8,128,256]{2,1,0:T(8,128)(2,1)} %copy-done, bf16[2048,1024]{1,0:T(8,128)(2,1)} %ow_ref.3, bf16[128,5]{1,0:T(8,128)(2,1)} %fusion.token_ref, bf16[5,1024]{1,0:T(8,128)(2,1)} %embed_ref.3), custom_call_target="tpu_custom_call" | custom-call | flops 4000000000 | bytes 1000000 | tf_op jit(solution)/shard_map/pallas_call | solution.py:863
  112.9 0.7 reduce_sum.9
  113.6 1.7 %all-to-all-done.4.pieces_ref = f32[16,8,128]{2,1,0:T(8,128)S(1)} async-done(((f32[16,8,128]{2,1,0:T(8,128)}), f32[16,8,128]{2,1,0:T(8,128)S(1)}, u32[]{:S(2)}, u32[]{:S(2)}) %all-to-all-start.4) | async-done | bytes 65568 | tf_op jit(solution)/shard_map/all_to_all | solution.py:885
  115.3 0.6 copy-done.1
  115.9 1.7 %shard_map.212 = f32[128,8,128]{2,1,0:T(8,128)} custom-call(f32[16,8,128]{2,1,0:T(8,128)} %copy-done.1), custom_call_target="tpu_custom_call" | custom-call | flops 100000000 | bytes 1000000 | tf_op jit(solution)/shard_map/pallas_call | solution.py:863
  117.6 23.2 %all_to_all.30.whole_ref = f32[128,8,128]{2,1,0:T(8,128)} all-to-all(f32[128,8,128]{2,1,0:T(8,128)} %shard_map.212), channel_id=1, replica_groups=mesh['seq'=16,'head'=8] {'seq','head'}, dimensions={0} | all-to-all | bytes 1048576 | tf_op jit(solution)/shard_map/all_to_all | solution.py:885
  140.8 2.4 %shard_map.213 = (f32[64,4384]{1,0:T(8,128)}, f32[5,1024]{1,0:T(8,128)}, f32[4,2304]{1,0:T(4,128)}, f32[18,128]{1,0:T(8,128)}, f32[1,32]{1,0:T(1,128)}, /*index=...) custom-call(f32[128,8,128]{2,1,0:T(8,128)} %all_to_all.30.whole_ref, bf16[64,24]{1,0:T(8,128)(2,1)} %bitcast.27), custom_call_target="tpu_custom_call" | custom-call | flops 1000000000 | bytes 1000000 | tf_op jit(solution)/shard_map/pallas_call | solution.py:863
  (20 shorter events, 0.8 us)
Async XLA Ops:
  0.6 12.2 %collective-permute-start = (s32[1,8,128]{2,1,0:T(8,128)}, s32[1,8,128]{2,1,0:T(8,128)S(1)}, u32[]{:S(2)}, u32[]{:S(2)}) collective-permute-start(s32[1,8,128]{2,1,0:T(8,128)} %bitcast.29), channel_id=1, source_target_pairs={{0,8},{8,0},{16,24},{24,16},{32,40},{40,32},{48,56},{56,48},{64,72... | collective-permute-start | bytes 12296 | tf_op jit(solution)/shard_map/ppermute | solution.py:881
  0.7 12.1 %collective-permute-start.1 = (s32[1,8,128]{2,1,0:T(8,128)}, s32[1,8,128]{2,1,0:T(8,128)S(1)}, u32[]{:S(2)}, u32[]{:S(2)}) collective-permute-start(s32[1,8,128]{2,1,0:T(8,128)} %bitcast.30), channel_id=1, source_target_pairs={{0,64},{8,72},{16,80},{24,88},{32,96},{40,104},{48,112},{56,120},{... | collective-permute-start | bytes 12296 | tf_op jit(solution)/shard_map/ppermute | solution.py:881
  2.4 10.5 %collective-permute-start.2 = (s32[1,8,128]{2,1,0:T(8,128)}, s32[1,8,128]{2,1,0:T(8,128)S(1)}, u32[]{:S(2)}, u32[]{:S(2)}) collective-permute-start(s32[1,8,128]{2,1,0:T(8,128)} %bitcast.31), channel_id=1, source_target_pairs={{0,72},{8,64},{16,88},{24,80},{32,104},{40,96},{48,120},{56,112},{... | collective-permute-start | bytes 12296 | tf_op jit(solution)/shard_map/ppermute | solution.py:881
  5.1 7.8 %copy-start.3 = (s32[1024]{0:T(1024)S(1)}, s32[1024]{0:T(1024)}, u32[]{:S(2)}) copy-start(s32[1024]{0:T(1024)} %param.13) | copy-start | bytes 12292
  5.1 36.3 %all-to-all-start = ((bf16[8,128,1024]{2,1,0:T(8,128)(2,1)}), bf16[8,128,1024]{2,1,0:T(8,128)(2,1)}, u32[]{:S(2)}, u32[]{:S(2)}) async-start(bf16[8,128,1024]{2,1,0:T(8,128)(2,1)} %broadcast_in_dim.20), calls=%async_computation | async-start | bytes 4194304 | tf_op jit(solution)/shard_map/all_to_all | solution.py:876
  12.9 10.1 %collective-permute-start.3 = (s32[4,8,128]{2,1,0:T(8,128)S(1)}, s32[4,8,128]{2,1,0:T(8,128)S(1)}, u32[]{:S(2)}, u32[]{:S(2)}) collective-permute-start(s32[4,8,128]{2,1,0:T(8,128)S(1)} %pad_add_fusion.1), channel_id=1, source_target_pairs={{0,16},{8,24},{16,0},{24,8},{32,48},{40,56},{48,32},{56,40},{64,80... | collective-permute-start | bytes 49160 | tf_op jit(solution)/shard_map/ppermute | solution.py:881
  14.9 8.1 %collective-permute-start.4 = (s32[4,8,128]{2,1,0:T(8,128)S(1)}, s32[4,8,128]{2,1,0:T(8,128)S(1)}, u32[]{:S(2)}, u32[]{:S(2)}) collective-permute-start(s32[4,8,128]{2,1,0:T(8,128)S(1)} %pad_add_fusion.1), channel_id=1, source_target_pairs={{0,32},{8,40},{16,48},{24,56},{32,0},{40,8},{48,16},{56,24},{64,96... | collective-permute-start | bytes 49160 | tf_op jit(solution)/shard_map/ppermute | solution.py:881
  18.5 4.9 %collective-permute-start.5 = (s32[4,8,128]{2,1,0:T(8,128)S(1)}, s32[4,8,128]{2,1,0:T(8,128)S(1)}, u32[]{:S(2)}, u32[]{:S(2)}) collective-permute-start(s32[4,8,128]{2,1,0:T(8,128)S(1)} %pad_add_fusion.1), channel_id=1, source_target_pairs={{0,48},{8,56},{16,32},{24,40},{32,16},{40,24},{48,0},{56,8},{64,11... | collective-permute-start | bytes 49160 | tf_op jit(solution)/shard_map/ppermute | solution.py:881
  46.3 14.2 %all-to-all-start.1 = ((f32[8,4,1024]{2,1,0:T(4,128)}), f32[8,4,1024]{2,1,0:T(4,128)S(1)}, u32[]{:S(2)}, u32[]{:S(2)}) async-start(f32[8,4,1024]{2,1,0:T(4,128)} %get-tuple-element.85), calls=%async_computation.1 | async-start | bytes 262144 | tf_op jit(solution)/shard_map/all_to_all | solution.py:885
  60.5 0.7 copy-start.2
  66.5 16.6 %all-to-all-start.2 = ((bf16[8,128,256]{2,1,0:T(8,128)(2,1)}), bf16[8,128,256]{2,1,0:T(8,128)(2,1)S(1)}, u32[]{:S(2)}, u32[]{:S(2)}) async-start(bf16[8,128,256]{2,1,0:T(8,128)(2,1)} %bitcast.25), calls=%async_computation.2 | async-start | bytes 1048576 | tf_op jit(solution)/shard_map/all_to_all | solution.py:885
  83.1 20.4 %copy-start = (bf16[8,128,256]{2,1,0:T(8,128)(2,1)}, bf16[8,128,256]{2,1,0:T(8,128)(2,1)S(1)}, u32[]{:S(2)}) copy-start(bf16[8,128,256]{2,1,0:T(8,128)(2,1)S(1)} %all-to-all-done.2.mixed_ref) | copy-start | bytes 1572868
  83.1 20.9 %all-to-all-start.3 = ((f32[16,64,256]{2,1,0:T(8,128)}), f32[16,64,256]{2,1,0:T(8,128)S(1)}, u32[]{:S(2)}, u32[]{:S(2)}) async-start(f32[16,64,256]{2,1,0:T(8,128)} %bitcast.24), calls=%async_computation.3 | async-start | bytes 2097152 | tf_op jit(solution)/shard_map/all_to_all | solution.py:885
  104.0 11.3 %all-to-all-start.4 = ((f32[16,8,128]{2,1,0:T(8,128)}), f32[16,8,128]{2,1,0:T(8,128)S(1)}, u32[]{:S(2)}, u32[]{:S(2)}) async-start(f32[16,8,128]{2,1,0:T(8,128)} %shard_map.210), calls=%async_computation.4 | async-start | bytes 131072 | tf_op jit(solution)/shard_map/all_to_all | solution.py:885
  115.3 0.6 copy-start.1

commit v4 on v3

--- a/solution.py
+++ b/solution.py
@@ -448,16 +448,7 @@
                     sums_ref[peer, at : at + 1, cols] = total
 
 
-def mix_kernel(
-    at_ref, y_first_ref, y_second_ref, oh_ref, oht_ref, gate_ref, slope_ref, gain_ref, sums_ref,
-    mixed_ref, dy_first_ref, dy_second_ref, dgate_ref, dgain_ref,
-):
-    @pl.when(pl.program_id(0) == 0)
-    def _():
-        dgate_ref[...] = jnp.zeros_like(dgate_ref)
-        dgain_ref[...] = jnp.zeros_like(dgain_ref)
-
-    gain = own_row(gain_ref, at_ref[1])
+def mix_rows(y_refs, oh_ref, oht_ref, slope_ref, sums_ref, gate_ref, gain, dgate_ref, dgain_ref):
     slope = slope_ref[...]
     sums = sums_ref[0]
     for peer in range(1, sums_ref.shape[0]):
@@ -476,20 +467,21 @@
     sloped = slope * gain
     gates = dot1(oh_ref[...], gate_ref[...])
     total = None
+    dys = []
     for branch in range(2):
         gate = gates[:, 256 * branch : 256 * branch + 256]
-        y = (y_first_ref, y_second_ref)[branch][...]
+        y = y_refs[branch][...]
         g = y * gate
         scale = columns[:, 2 * branch : 2 * branch + 1]
         weight = columns[:, 2 * branch + 1 : 2 * branch + 2]
         normed = g * scale
         total = normed if total is None else total + normed
         dg = scale * sloped - weight * g
-        (dy_first_ref, dy_second_ref)[branch][...] = dg * gate
+        dys.append(dg * gate)
         lanes = oht_ref[32 * branch : 32 * branch + 32, :]
         dgate_ref[branch] += dot2(lanes, dg * y)
-    mixed_ref[...] = (total * gain).astype(bf16)
     dgain_ref[...] += jnp.sum(slope * total, axis=0, keepdims=True)
+    return (total * gain).astype(bf16), dys
 
 
 def backward_scan(
@@ -551,18 +543,41 @@
 
 
 def first_backward_kernel(at_ref, *refs):
-    blocks = (refs[0:6], refs[6:12])
-    tables, (cot_ref, mixed_ref) = refs[12:17], refs[17:19]
-    sums, outer_ref = refs[19:24], refs[24]
-
-    @pl.when(pl.program_id(0) == 0)
+    upper, lower, tables = refs[0:5], refs[5:10], refs[10:15]
+    (
+        upper_second_ref, lower_first_ref, upper_slope_ref, lower_slope_ref, upper_cot_ref,
+        lower_cot_ref, upper_sums_ref, lower_sums_ref, gate_ref, gain_ref,
+    ) = refs[15:25]
+    sums, outer_ref = refs[25:30], refs[30]
+    mixed_ref, first_out_ref, second_out_ref, dgate_ref, dgain_ref = refs[31:36]
+    first_ref, second_ref = refs[36:38]
+    step_at = pl.program_id(0)
+
+    @pl.when(step_at == 0)
     def _():
-        for ref in refs[19:]:
+        for ref in (*sums, outer_ref, dgate_ref, dgain_ref):
             ref[...] = jnp.zeros_like(ref)
 
-    for branch in range(2):
-        backward_scan(branch, *blocks[branch], *tables, *sums)
-    outer_ref[...] += lax.dot_general(cot_ref[...], mixed_ref[...], TN, preferred_element_type=f32)
+    gain = own_row(gain_ref, at_ref[1])
+    upper_mixed, (dy, dy_later) = mix_rows(
+        (upper[2], upper_second_ref), upper[0], upper[1], upper_slope_ref, upper_sums_ref,
+        gate_ref, gain, dgate_ref, dgain_ref,
+    )
+    first_ref[...] = dy
+    second_out_ref[...] = dy_later
+    lower_mixed, (dy_later, dy) = mix_rows(
+        (lower_first_ref, lower[2]), lower[0], lower[1], lower_slope_ref, lower_sums_ref,
+        gate_ref, gain, dgate_ref, dgain_ref,
+    )
+    second_ref[...] = dy
+    first_out_ref[...] = dy_later
+    mixed_ref[pl.ds(pl.multiple_of((3 - step_at) * BLOCK, BLOCK), BLOCK), :] = upper_mixed
+    mixed_ref[pl.ds(pl.multiple_of(step_at * BLOCK, BLOCK), BLOCK), :] = lower_mixed
+    backward_scan(0, *upper, first_ref, *tables, *sums)
+    backward_scan(1, *lower, second_ref, *tables, *sums)
+    cot = jnp.concatenate([upper_cot_ref[...], lower_cot_ref[...]], axis=0)
+    mixed = jnp.concatenate([upper_mixed, lower_mixed], axis=0)
+    outer_ref[...] += lax.dot_general(cot, mixed, TN, preferred_element_type=f32)
 
 
 def second_backward_kernel(at_ref, *refs):
@@ -756,21 +771,14 @@
     out_ref[...] = total.astype(bf16)
 
 
-def sum_kernel(pieces_ref, spread_ref):
-    total = pieces_ref[0]
-    for k in range(1, pieces_ref.shape[0]):
-        total = total + pieces_ref[k]
-    spread_ref[...] = jnp.broadcast_to(total[None], spread_ref.shape)
-
-
 def final_kernel(
     whole_ref, embed_ref,
     w_in_ref, embedding_ref, conv_ref, bias_ref, dt_ref, rate_ref, skip_ref, gain_ref,
 ):
     def summed(piece):
-        total = whole_ref[8 * piece]
+        total = whole_ref[0, piece]
         for k in range(1, 8):
-            total = total + whole_ref[8 * piece + k]
+            total = total + whole_ref[k, piece]
         return total
 
     embed = embed_ref[...]
@@ -786,8 +794,8 @@
 
     for rank in range(8):
         for half in range(2):
-            gate = whole_ref[8 * half + rank]
-            x = whole_ref[8 * (2 + half) + rank]
+            gate = whole_ref[rank, half]
+            x = whole_ref[rank, 2 + half]
             at = 256 * rank + 128 * half
             cols = slice(at, at + 128)
             outer(gate, at)
@@ -879,6 +887,12 @@
 def gather_by_flips(array, axis, flips):
     pairs = [[(i, i ^ flip) for i in range(lax.axis_size(axis))] for flip in flips]
     return jnp.concatenate([array] + [lax.ppermute(array, axis, pair) for pair in pairs], axis=0)
+
+
+def sum_by_flips(array, axis, flips):
+    pairs = [[(i, i ^ flip) for i in range(lax.axis_size(axis))] for flip in flips]
+    one, two, three = [lax.ppermute(array, axis, pair) for pair in pairs]
+    return (array + one) + (two + three)
 
 
 def exchange(array, axis):
@@ -1022,34 +1036,9 @@
         cost=2e9,
     )
     row_sums = exchange(row_sums, "head")
-    mixed, dy_first, dy_second, dgate, dgain = call(
-        mix_kernel,
-        at,
-        [
-            *y_rows,
-            hot_rows,
-            (onehot_t, (128, chunk), lambda k, at: (0, k)),
-            gates,
-            rows_at(slope, chunk, lambda k: k),
-            gain_rows,
-            (row_sums, (groups, 4, chunk), lambda k, at: (0, 0, k)),
-        ],
-        [
-            ((length, width), bf16, (chunk, width), lambda k, at: (k, 0)),
-            ((length, width), f32, (chunk, width), lambda k, at: (k, 0)),
-            ((length, width), f32, (chunk, width), lambda k, at: (k, 0)),
-            ((2, 32, width), f32),
-            ((1, width), f32),
-        ],
-        cost=4e9,
-        steps=TOKEN_STEPS,
-    )
-
-    mixed_all = exchange(mixed.reshape(groups, token_rows, width), "head")
-
     def scan_operands(first_step):
         operands = []
-        for branch, y, dy in ((0, y_first, dy_first), (1, y_second, dy_second)):
+        for branch, y in ((0, y_first), (1, y_second)):
 
             def nth(k):
                 return first_step + k
@@ -1064,15 +1053,16 @@
                 return (branch, jnp.minimum(blocks - nth(k), blocks - 1), 0, 0)
 
             one = (1, 1, STATE, width)
-            operands += [
-                rows_at(onehot, BLOCK, block),
-                (onehot_t, (128, BLOCK), lambda k, at, block=block: (0, block(k))),
-                rows_at(y, BLOCK, block),
-                (states, one, state),
-                (states, one, later),
-                rows_at(dy, BLOCK, block),
-            ]
-        return operands + tables
+            operands.append(
+                [
+                    rows_at(onehot, BLOCK, block),
+                    (onehot_t, (128, BLOCK), lambda k, at, block=block: (0, block(k))),
+                    rows_at(y, BLOCK, block),
+                    (states, one, state),
+                    (states, one, later),
+                ]
+            )
+        return operands
 
     accumulators = [
         ((32, 512), f32),
@@ -1081,22 +1071,59 @@
         ((1, width), f32),
         ((2, STATE, width), f32),
     ]
-    *grads, partial = call(
+    first, second = scan_operands(0)
+
+    def upper(k):
+        return blocks - 1 - k
+
+    def lower(k):
+        return k
+
+    def sums_at(index):
+        return (row_sums, (groups, 4, BLOCK), lambda k, at: (0, 0, index(k)))
+
+    *grads, partial, mixed, dy_first, dy_second, dgate, dgain = call(
         first_backward_kernel,
         at,
-        scan_operands(0)
-        + [rows_at(cot_all, length // 2, lambda k: k), rows_at(mixed, length // 2, lambda k: k)],
-        accumulators + [((D, width), f32)],
-        cost=1.5e10,
+        [
+            *first,
+            *second,
+            *tables,
+            rows_at(y_second, BLOCK, upper),
+            rows_at(y_first, BLOCK, lower),
+            rows_at(slope, BLOCK, upper),
+            rows_at(slope, BLOCK, lower),
+            rows_at(cot_all, BLOCK, upper),
+            rows_at(cot_all, BLOCK, lower),
+            sums_at(upper),
+            sums_at(lower),
+            gates,
+            gain_rows,
+        ],
+        accumulators
+        + [
+            ((D, width), f32),
+            ((length, width), bf16),
+            ((length // 2, width), f32, (BLOCK, width), lambda k, at: (k, 0)),
+            ((length // 2, width), f32, (BLOCK, width), lambda k, at: (1 - k, 0)),
+            ((2, 32, width), f32),
+            ((1, width), f32),
+        ],
+        [pltpu.VMEM((BLOCK, width), f32), pltpu.VMEM((BLOCK, width), f32)],
+        cost=2e10,
         steps=blocks // 2,
     )
-    mixed_all, partial, grads = lax.optimization_barrier((mixed_all, partial, grads))
     partial = exchange(partial.reshape(shards, D // shards, width), "seq")
+    first, second = scan_operands(blocks // 2)
     (packed,) = call(
         second_backward_kernel,
         at,
-        scan_operands(blocks // 2)
-        + [
+        [
+            *first,
+            rows_at(dy_first, BLOCK, lambda k: 1 - k),
+            *second,
+            rows_at(dy_second, BLOCK, lambda k: k),
+            *tables,
             *grads,
             early,
             late,
@@ -1133,7 +1160,10 @@
         cost=2e10,
         steps=blocks // 2,
     )
-    packed, partial = lax.optimization_barrier((packed, partial))
+    packed, partial, mixed = lax.optimization_barrier((packed, partial, mixed))
+    mixed_all = exchange(mixed.reshape(groups, token_rows, width), "head")
+    total = sum_by_flips(packed, "seq", (1, 8, 9))
+    total = sum_by_flips(total, "seq", (2, 4, 6))
 
     grad_w_out = jnp.sum(partial, axis=0).T
     token_ids = lax.dynamic_slice_in_dim(ids_later, head_rank * token_rows, token_rows, 0)
@@ -1146,16 +1176,11 @@
         4e9,
     )
 
-    pieces = exchange(packed, "seq")
     row_count = D // shards
     columns = lax.dynamic_slice_in_dim(embed_later, seq_rank * row_count, row_count, 1)
     columns = jnp.pad(columns, ((1, 2), (0, 0)))
     columns = jnp.concatenate([columns] * 3, axis=0).T
-    pieces, layer_out, grad_w_out, columns = lax.optimization_barrier(
-        (pieces, layer_out, grad_w_out, columns)
-    )
-    (spread,) = call_plain(sum_kernel, [pieces], [((shards * groups, 8, 128), f32)], 1e8)
-    everything = exchange(spread, ("seq", "head"))
+    everything = gather(total, "head")
     w_in, embed, conv, bias, dt, rate, skip, gain = call_plain(
         final_kernel,
         [everything, columns],

time: 144 us -> 132 us (0.917)
  blocking collectives: 23.2 us -> 0 us
  waiting for transfers between devices: 5.19 us -> 16.9 us
  Pallas kernels: 70.1 us -> 65.1 us
  starting transfers between devices: 36 us -> 39.7 us
    all_to_all x1 -> x0, blocking collectives: 23.2 us -> none  [exchange(): return lax.all_to_all(array, axis, split_axis=0, concat_axis=0, tiled=True)]
    all_to_all x4 -> x3, starting transfers between devices: 21.3 us -> 14.2 us  [exchange(): return lax.all_to_all(array, axis, split_axis=0, concat_axis=0, tiled=True)]
    ppermute x0 -> x6, starting transfers between devices: none -> 6.39 us  [sum_by_flips(): one, two, three = [lax.ppermute(array, axis, pair) for pair in pairs]]
    all_to_all x1 -> x2, waiting for transfers between devices: 1.19 us -> 6.93 us  [gather(): return lax.all_to_all(spread, axis, split_axis=0, concat_axis=0, tiled=True)]
    all_to_all x1 -> x2, starting transfers between devices: 7.16 us -> 12.1 us  [gather(): return lax.all_to_all(spread, axis, split_axis=0, concat_axis=0, tiled=True)]
    ppermute x0 -> x6, waiting for transfers between devices: none -> 3.56 us  [sum_by_flips(): one, two, three = [lax.ppermute(array, axis, pair) for pair in pairs]]
    pallas_call x7 -> x6, Pallas kernels: 62.3 us -> 58.9 us  [call(): pl.pallas_call(kernel, out_shape=shapes, grid_spec=pltpu.PrefetchScalarGr...]
    all_to_all x4 -> x3, waiting for transfers between devices: 3.6 us -> 6.36 us  [exchange(): return lax.all_to_all(array, axis, split_axis=0, concat_axis=0, tiled=True)]
  transfers between devices with their start and end apart: 11 -> 17, of which waited for: 5 -> 7; matrix products, arithmetic and copies ran while one was open for 5% -> 6% of each run, Pallas kernels for 39% -> 34%
where the time goes in v4:
time: 132 us
  Pallas kernels  65.1 us (49%)
  starting transfers between devices  39.7 us (30%)
  waiting for transfers between devices  16.9 us (13%)
  local copies, waits for them, and re-layouts  5.61 us (4%)
  other arithmetic  3.5 us (3%)
    pallas_call x6, Pallas kernels, call(): pl.pallas_call(kernel, out_shape=shapes, grid_spec=pltpu.PrefetchScalarGr...  58.9 us
    all_to_all x3, starting transfers between devices, exchange(): return lax.all_to_all(array, axis, split_axis=0, concat_axis=0, tiled=True)  14.2 us
    all_to_all x2, starting transfers between devices, gather(): return lax.all_to_all(spread, axis, split_axis=0, concat_axis=0, tiled=True)  12.1 us
    ppermute x6, starting transfers between devices, gather_by_flips(): lax.ppermute(array, axis, pair)  7.01 us
    all_to_all x2, waiting for transfers between devices, gather(): return lax.all_to_all(spread, axis, split_axis=0, concat_axis=0, tiled=True)  6.93 us
    ppermute x6, starting transfers between devices, sum_by_flips(): one, two, three = [lax.ppermute(array, axis, pair) for pair in pairs]  6.39 us
    all_to_all x3, waiting for transfers between devices, exchange(): return lax.all_to_all(array, axis, split_axis=0, concat_axis=0, tiled=True)  6.36 us
    pallas_call x2, Pallas kernels, call_plain(): pl.pallas_call(kernel, out_shape=[jax.ShapeDtypeStruct(shape, kind) for s...  6.15 us
  transfers between devices with their start and end apart: 17, of which 7 were waited for; matrix products, arithmetic and copies ran while one was open for 6% of the time, Pallas kernels for 34%

profile of v4, /device:TPU:0, one launch (start us, length us, event | category | flops | bytes accessed | tf_op | source)
XLA Modules:
  0.0 131.5 jit_solution(7870975714861276567)
XLA Ops:
  0.6 1.1 collective-permute-start.2
  2.6 2.5 %broadcast_in_dim.26 = bf16[8,128,1024]{2,1,0:T(8,128)(2,1)} broadcast(bf16[128,1024]{1,0:T(8,128)(2,1)} %refs_34_.1), dimensions={1,2} | broadcast | bytes 2359296 | tf_op jit(solution)/shard_map/broadcast_in_dim | solution.py:883
  5.1 7.1 %all-to-all-start = ((bf16[8,128,1024]{2,1,0:T(8,128)(2,1)}), bf16[8,128,1024]{2,1,0:T(8,128)(2,1)}, u32[]{:S(2)}, u32[]{:S(2)}) async-start(bf16[8,128,1024]{2,1,0:T(8,128)(2,1)} %broadcast_in_dim.26), calls=%async_computation | async-start | bytes 4194304 | tf_op jit(solution)/shard_map/all_to_all | solution.py:884
  12.9 4.1 %collective-permute-start.5 = (s32[4,8,128]{2,1,0:T(8,128)S(1)}, s32[4,8,128]{2,1,0:T(8,128)S(1)}, u32[]{:S(2)}, u32[]{:S(2)}) collective-permute-start(s32[4,8,128]{2,1,0:T(8,128)S(1)} %pad_add_fusion.1), channel_id=1, source_target_pairs={{0,48},{8,56},{16,32},{24,40},{32,16},{40,24},{48,0},{56,8},{64,11... | collective-permute-start | bytes 49160 | tf_op jit(solution)/shard_map/ppermute | solution.py:889
  17.0 0.9 collective-permute-start.3
  17.9 4.6 %shard_map.204 = (bf16[128,2048]{1,0:T(8,128)(2,1)}, bf16[128,512]{1,0:T(8,128)(2,1)}, f32[16,128]{1,0:T(8,128)}, f32[8,768]{1,0:T(8,128)}, f32[24,256]{1,0:T(8,...) custom-call(s32[2]{0:T(128)} %pad_add_fusion.2.at_ref, bf16[5,1024]{1,0:T(8,128)(2,1)} %embed_ref.3, ...), custom_call_target="tpu_custom_call" | custom-call | flops 6000000000 | bytes 4000000 | tf_op jit(solution)/shard_map/pallas_call | solution.py:855
  23.2 16.1 %shard_map.205 = (f32[1024,256]{1,0:T(8,128)}, f32[1024,256]{1,0:T(8,128)}, f32[2,4,128,256]{3,2,1,0:T(8,128)}, f32[64,128]{1,0:T(8,128)}, f32[4,128,128]{2,1,0:...) custom-call(s32[2]{0:T(128)} %pad_add_fusion.2.at_ref, ...), custom_call_target="tpu_custom_call" | custom-call | flops 15000000512 | bytes 4000000 | tf_op jit(solution)/shard_map/pallas_call | solution.py:855
  39.3 1.8 %all-to-all-done = bf16[8,128,1024]{2,1,0:T(8,128)(2,1)} async-done(((bf16[8,128,1024]{2,1,0:T(8,128)(2,1)}), bf16[8,128,1024]{2,1,0:T(8,128)(2,1)}, u32[]{:S(2)}, u32[]{:S(2)}) %all-to-all-start) | async-done | bytes 2097184 | tf_op jit(solution)/shard_map/all_to_all | solution.py:884
  41.1 4.9 %shard_map.206 = (f32[1024,256]{1,0:T(8,128)}, f32[8,4,1024]{2,1,0:T(4,128)}) custom-call(s32[2]{0:T(128)} %pad_add_fusion.2.at_ref, f32[1024,256]{1,0:T(8,128)} %get-tuple-element.70.y_first_ref.refs_2_.refs_16_, f32[1024,256]{1,0:T(8,128)} %get-tuple-element.72.y_second_ref.refs_7_.refs_15_.refs_8_, ...), custom_call_target="tpu_custom_call" | custom-call | flops 4000000000 | bytes 4000000 | tf_op jit(solution)/shard_map/pallas_call | solution.py:855
  46.0 5.4 %all-to-all-start.1 = ((f32[8,4,1024]{2,1,0:T(4,128)}), f32[8,4,1024]{2,1,0:T(4,128)S(1)}, u32[]{:S(2)}, u32[]{:S(2)}) async-start(f32[8,4,1024]{2,1,0:T(4,128)} %get-tuple-element.75), calls=%async_computation.1 | async-start | bytes 262144 | tf_op jit(solution)/shard_map/all_to_all | solution.py:899
  51.5 4.5 %shard_map.208 = (f32[1024,384]{1,0:T(8,128)}, f32[1024,384]{1,0:T(8,128)}, f32[1024,256]{1,0:T(8,128)}) custom-call(s32[2]{0:T(128)} %pad_add_fusion.2.at_ref, bf16[1024,128]{1,0:T(8,128)(2,1)} %constant.25.clone.goh_ref, bf16[128,2048]{1,0:T(8,128)(2,1)} %get-tuple-element.88.pre_ref.step_ref.gate_ref.refs_10_.refs_11_.refs_23_.refs_12_.refs_13_, ...), custom_call_target="tpu_custom_call" | custom-call | flops 2000000000 | bytes 4000000 | tf_op jit(solution)/shard_map/pallas_call | solution.py:855
  56.0 3.6 %all-to-all-done.1.refs_21_.refs_22_ = f32[8,4,1024]{2,1,0:T(4,128)S(1)} async-done(((f32[8,4,1024]{2,1,0:T(4,128)}), f32[8,4,1024]{2,1,0:T(4,128)S(1)}, u32[]{:S(2)}, u32[]{:S(2)}) %all-to-all-start.1) | async-done | bytes 131104 | tf_op jit(solution)/shard_map/all_to_all | solution.py:899
  60.3 12.7 %shard_map.207 = (f32[32,512]{1,0:T(8,128)}, f32[32,256]{1,0:T(8,128)}, f32[32,256]{1,0:T(8,128)}, f32[1,256]{1,0:T(1,128)}, f32[2,128,256]{2,1,0:T(8,128)}, /*i...) custom-call(s32[2]{0:T(128)} %pad_add_fusion.2.at_ref, ...), custom_call_target="tpu_custom_call" | custom-call | flops 20000000000 | bytes 4000000 | tf_op jit(solution)/shard_map/pallas_call | solution.py:855
  73.0 4.6 %all-to-all-start.2 = ((f32[16,64,256]{2,1,0:T(8,128)}), f32[16,64,256]{2,1,0:T(8,128)S(1)}, u32[]{:S(2)}, u32[]{:S(2)}) async-start(f32[16,64,256]{2,1,0:T(8,128)} %bitcast.24), calls=%async_computation.2 | async-start | bytes 2097152 | tf_op jit(solution)/shard_map/all_to_all | solution.py:899
  77.6 16.1 %shard_map.209 = f32[16,8,128]{2,1,0:T(8,128)} custom-call(s32[2]{0:T(128)} %pad_add_fusion.2.at_ref, bf16[1024,128]{1,0:T(8,128)(2,1)} %get-tuple-element.68.oh_ref.refs_0_.refs_5_.refs_6_, bf16[128,1024]{1,0:T(8,128)(2,1)} %get-tuple-element.69.refs_1_.refs_6_.refs_7_.refs_24_, f32[1024,256]{1,0:T(8,128)} %get-tuple-element.70.y_first_ref.refs_2_.refs_16_, ...), custom_call_target="tpu_custom_call" | custom-call | flops 20000000000 | bytes 4000000 | tf_op jit(solution)/shard_map/pallas_call | solution.py:855
  94.2 1.5 %collective-permute-start.7 = (f32[16,8,128]{2,1,0:T(8,128)}, f32[16,8,128]{2,1,0:T(8,128)S(1)}, u32[]{:S(2)}, u32[]{:S(2)}) collective-permute-start(f32[16,8,128]{2,1,0:T(8,128)} %shard_map.209), channel_id=1, source_target_pairs={{0,64},{8,72},{16,80},{24,88},{32,96},{40,104},{48,112},{56,120},{... | collective-permute-start | bytes 196616 | tf_op jit(solution)/shard_map/ppermute | solution.py:894
  96.3 0.7 fusion.token_ref
  97.0 4.2 %all-to-all-start.3 = ((bf16[8,128,256]{2,1,0:T(8,128)(2,1)}), bf16[8,128,256]{2,1,0:T(8,128)(2,1)S(1)}, u32[]{:S(2)}, u32[]{:S(2)}) async-start(bf16[8,128,256]{2,1,0:T(8,128)(2,1)} %bitcast.11), calls=%async_computation.3 | async-start | bytes 1048576 | tf_op jit(solution)/shard_map/all_to_all | solution.py:899
  101.3 0.9 add_add_fusion.1
  102.1 3.1 %collective-permute-start.10 = (f32[16,8,128]{2,1,0:T(8,128)S(1)}, f32[16,8,128]{2,1,0:T(8,128)S(1)}, u32[]{:S(2)}, u32[]{:S(2)}) collective-permute-start(f32[16,8,128]{2,1,0:T(8,128)S(1)} %add_add_fusion.1), channel_id=1, source_target_pairs={{0,32},{8,40},{16,48},{24,56},{32,0},{40,8},{48,16},{56,24},{64,96... | collective-permute-start | bytes 196616 | tf_op jit(solution)/shard_map/ppermute | solution.py:894
  105.2 1.2 collective-permute-start.11
  106.4 0.8 constant_dynamic-slice_fusion
  107.2 0.8 collective-permute-done.10
  108.0 2.7 %collective-permute-done.11 = f32[16,8,128]{2,1,0:T(8,128)S(1)} collective-permute-done((f32[16,8,128]{2,1,0:T(8,128)S(1)}, f32[16,8,128]{2,1,0:T(8,128)S(1)}, u32[]{:S(2)}, u32[]{:S(2)}) %collective-permute-start.11) | collective-permute-done | bytes 65568 | tf_op jit(solution)/shard_map/ppermute | solution.py:894
  110.7 2.3 %all-to-all-done.3.mixed_ref = bf16[8,128,256]{2,1,0:T(8,128)(2,1)S(1)} async-done(((bf16[8,128,256]{2,1,0:T(8,128)(2,1)}), bf16[8,128,256]{2,1,0:T(8,128)(2,1)S(1)}, u32[]{:S(2)}, u32[]{:S(2)}) %all-to-all-start.3) | async-done | bytes 524320 | tf_op jit(solution)/shard_map/all_to_all | solution.py:899
  113.0 0.9 broadcast_in_dim.27
  113.9 5.0 %all-to-all-start.4 = ((f32[8,16,8,128]{3,2,1,0:T(8,128)}), f32[8,16,8,128]{3,2,1,0:T(8,128)}, u32[]{:S(2)}, u32[]{:S(2)}) async-start(f32[8,16,8,128]{3,2,1,0:T(8,128)} %broadcast_in_dim.27), calls=%async_computation.4 | async-start | bytes 1048576 | tf_op jit(solution)/shard_map/all_to_all | solution.py:884
  118.9 0.7 copy.24
  119.6 0.7 reduce_sum.9
  120.3 3.8 %shard_map.210 = bf16[128,1024]{1,0:T(8,128)(2,1)} custom-call(bf16[8,128,256]{2,1,0:T(8,128)(2,1)} %copy-done, bf16[2048,1024]{1,0:T(8,128)(2,1)} %ow_ref.3, bf16[128,5]{1,0:T(8,128)(2,1)} %fusion.token_ref, bf16[5,1024]{1,0:T(8,128)(2,1)} %embed_ref.3), custom_call_target="tpu_custom_call" | custom-call | flops 4000000000 | bytes 1000000 | tf_op jit(solution)/shard_map/pallas_call | solution.py:871
  124.0 5.1 %all-to-all-done.4.whole_ref = f32[8,16,8,128]{3,2,1,0:T(8,128)} async-done(((f32[8,16,8,128]{3,2,1,0:T(8,128)}), f32[8,16,8,128]{3,2,1,0:T(8,128)}, u32[]{:S(2)}, u32[]{:S(2)}) %all-to-all-start.4) | async-done | bytes 524320 | tf_op jit(solution)/shard_map/all_to_all | solution.py:884
  129.2 2.4 %shard_map.211 = (f32[64,4384]{1,0:T(8,128)}, f32[5,1024]{1,0:T(8,128)}, f32[4,2304]{1,0:T(4,128)}, f32[18,128]{1,0:T(8,128)}, f32[1,32]{1,0:T(1,128)}, /*index=...) custom-call(f32[8,16,8,128]{3,2,1,0:T(8,128)} %all-to-all-done.4.whole_ref, bf16[64,24]{1,0:T(8,128)(2,1)} %bitcast.26), custom_call_target="tpu_custom_call" | custom-call | flops 1000000000 | bytes 1000000 | tf_op jit(solution)/shard_map/pallas_call | solution.py:871
  (30 shorter events, 4.0 us)
Async XLA Ops:
  0.6 12.2 %collective-permute-start.2 = (s32[1,8,128]{2,1,0:T(8,128)}, s32[1,8,128]{2,1,0:T(8,128)S(1)}, u32[]{:S(2)}, u32[]{:S(2)}) collective-permute-start(s32[1,8,128]{2,1,0:T(8,128)} %bitcast.28), channel_id=1, source_target_pairs={{0,72},{8,64},{16,88},{24,80},{32,104},{40,96},{48,120},{56,112},{... | collective-permute-start | bytes 12296 | tf_op jit(solution)/shard_map/ppermute | solution.py:889
  1.7 11.1 %collective-permute-start.1 = (s32[1,8,128]{2,1,0:T(8,128)}, s32[1,8,128]{2,1,0:T(8,128)S(1)}, u32[]{:S(2)}, u32[]{:S(2)}) collective-permute-start(s32[1,8,128]{2,1,0:T(8,128)} %bitcast.29), channel_id=1, source_target_pairs={{0,64},{8,72},{16,80},{24,88},{32,96},{40,104},{48,112},{56,120},{... | collective-permute-start | bytes 12296 | tf_op jit(solution)/shard_map/ppermute | solution.py:889
  2.4 10.5 %collective-permute-start = (s32[1,8,128]{2,1,0:T(8,128)}, s32[1,8,128]{2,1,0:T(8,128)S(1)}, u32[]{:S(2)}, u32[]{:S(2)}) collective-permute-start(s32[1,8,128]{2,1,0:T(8,128)} %bitcast.30), channel_id=1, source_target_pairs={{0,8},{8,0},{16,24},{24,16},{32,40},{40,32},{48,56},{56,48},{64,72... | collective-permute-start | bytes 12296 | tf_op jit(solution)/shard_map/ppermute | solution.py:889
  5.1 7.7 %copy-start.2 = (s32[1024]{0:T(1024)S(1)}, s32[1024]{0:T(1024)}, u32[]{:S(2)}) copy-start(s32[1024]{0:T(1024)} %param.13) | copy-start | bytes 12292
  5.1 36.0 %all-to-all-start = ((bf16[8,128,1024]{2,1,0:T(8,128)(2,1)}), bf16[8,128,1024]{2,1,0:T(8,128)(2,1)}, u32[]{:S(2)}, u32[]{:S(2)}) async-start(bf16[8,128,1024]{2,1,0:T(8,128)(2,1)} %broadcast_in_dim.26), calls=%async_computation | async-start | bytes 4194304 | tf_op jit(solution)/shard_map/all_to_all | solution.py:884
  12.9 9.6 %collective-permute-start.5 = (s32[4,8,128]{2,1,0:T(8,128)S(1)}, s32[4,8,128]{2,1,0:T(8,128)S(1)}, u32[]{:S(2)}, u32[]{:S(2)}) collective-permute-start(s32[4,8,128]{2,1,0:T(8,128)S(1)} %pad_add_fusion.1), channel_id=1, source_target_pairs={{0,48},{8,56},{16,32},{24,40},{32,16},{40,24},{48,0},{56,8},{64,11... | collective-permute-start | bytes 49160 | tf_op jit(solution)/shard_map/ppermute | solution.py:889
  17.0 5.5 %collective-permute-start.4 = (s32[4,8,128]{2,1,0:T(8,128)S(1)}, s32[4,8,128]{2,1,0:T(8,128)S(1)}, u32[]{:S(2)}, u32[]{:S(2)}) collective-permute-start(s32[4,8,128]{2,1,0:T(8,128)S(1)} %pad_add_fusion.1), channel_id=1, source_target_pairs={{0,32},{8,40},{16,48},{24,56},{32,0},{40,8},{48,16},{56,24},{64,96... | collective-permute-start | bytes 49160 | tf_op jit(solution)/shard_map/ppermute | solution.py:889
  17.0 5.5 %collective-permute-start.3 = (s32[4,8,128]{2,1,0:T(8,128)S(1)}, s32[4,8,128]{2,1,0:T(8,128)S(1)}, u32[]{:S(2)}, u32[]{:S(2)}) collective-permute-start(s32[4,8,128]{2,1,0:T(8,128)S(1)} %pad_add_fusion.1), channel_id=1, source_target_pairs={{0,16},{8,24},{16,0},{24,8},{32,48},{40,56},{48,32},{56,40},{64,80... | collective-permute-start | bytes 49160 | tf_op jit(solution)/shard_map/ppermute | solution.py:889
  46.0 13.6 %all-to-all-start.1 = ((f32[8,4,1024]{2,1,0:T(4,128)}), f32[8,4,1024]{2,1,0:T(4,128)S(1)}, u32[]{:S(2)}, u32[]{:S(2)}) async-start(f32[8,4,1024]{2,1,0:T(4,128)} %get-tuple-element.75), calls=%async_computation.1 | async-start | bytes 262144 | tf_op jit(solution)/shard_map/all_to_all | solution.py:899
  59.6 0.7 copy-start.1
  73.0 21.2 %all-to-all-start.2 = ((f32[16,64,256]{2,1,0:T(8,128)}), f32[16,64,256]{2,1,0:T(8,128)S(1)}, u32[]{:S(2)}, u32[]{:S(2)}) async-start(f32[16,64,256]{2,1,0:T(8,128)} %bitcast.24), calls=%async_computation.2 | async-start | bytes 2097152 | tf_op jit(solution)/shard_map/all_to_all | solution.py:899
  94.2 7.1 %collective-permute-start.7 = (f32[16,8,128]{2,1,0:T(8,128)}, f32[16,8,128]{2,1,0:T(8,128)S(1)}, u32[]{:S(2)}, u32[]{:S(2)}) collective-permute-start(f32[16,8,128]{2,1,0:T(8,128)} %shard_map.209), channel_id=1, source_target_pairs={{0,64},{8,72},{16,80},{24,88},{32,96},{40,104},{48,112},{56,120},{... | collective-permute-start | bytes 196616 | tf_op jit(solution)/shard_map/ppermute | solution.py:894
  95.7 5.6 %collective-permute-start.8 = (f32[16,8,128]{2,1,0:T(8,128)}, f32[16,8,128]{2,1,0:T(8,128)S(1)}, u32[]{:S(2)}, u32[]{:S(2)}) collective-permute-start(f32[16,8,128]{2,1,0:T(8,128)} %shard_map.209), channel_id=1, source_target_pairs={{0,72},{8,64},{16,88},{24,80},{32,104},{40,96},{48,120},{56,112},{... | collective-permute-start | bytes 196616 | tf_op jit(solution)/shard_map/ppermute | solution.py:894
  95.7 5.6 %collective-permute-start.6 = (f32[16,8,128]{2,1,0:T(8,128)}, f32[16,8,128]{2,1,0:T(8,128)S(1)}, u32[]{:S(2)}, u32[]{:S(2)}) collective-permute-start(f32[16,8,128]{2,1,0:T(8,128)} %shard_map.209), channel_id=1, source_target_pairs={{0,8},{8,0},{16,24},{24,16},{32,40},{40,32},{48,56},{56,48},{64,72... | collective-permute-start | bytes 196616 | tf_op jit(solution)/shard_map/ppermute | solution.py:894
  97.0 16.0 %all-to-all-start.3 = ((bf16[8,128,256]{2,1,0:T(8,128)(2,1)}), bf16[8,128,256]{2,1,0:T(8,128)(2,1)S(1)}, u32[]{:S(2)}, u32[]{:S(2)}) async-start(bf16[8,128,256]{2,1,0:T(8,128)(2,1)} %bitcast.11), calls=%async_computation.3 | async-start | bytes 1048576 | tf_op jit(solution)/shard_map/all_to_all | solution.py:899
  102.1 5.8 %collective-permute-start.10 = (f32[16,8,128]{2,1,0:T(8,128)S(1)}, f32[16,8,128]{2,1,0:T(8,128)S(1)}, u32[]{:S(2)}, u32[]{:S(2)}) collective-permute-start(f32[16,8,128]{2,1,0:T(8,128)S(1)} %add_add_fusion.1), channel_id=1, source_target_pairs={{0,32},{8,40},{16,48},{24,56},{32,0},{40,8},{48,16},{56,24},{64,96... | collective-permute-start | bytes 196616 | tf_op jit(solution)/shard_map/ppermute | solution.py:894
  105.2 5.5 %collective-permute-start.11 = (f32[16,8,128]{2,1,0:T(8,128)S(1)}, f32[16,8,128]{2,1,0:T(8,128)S(1)}, u32[]{:S(2)}, u32[]{:S(2)}) collective-permute-start(f32[16,8,128]{2,1,0:T(8,128)S(1)} %add_add_fusion.1), channel_id=1, source_target_pairs={{0,48},{8,56},{16,32},{24,40},{32,16},{40,24},{48,0},{56,8},{64,11... | collective-permute-start | bytes 196616 | tf_op jit(solution)/shard_map/ppermute | solution.py:894
  106.4 4.3 %collective-permute-start.9 = (f32[16,8,128]{2,1,0:T(8,128)S(1)}, f32[16,8,128]{2,1,0:T(8,128)S(1)}, u32[]{:S(2)}, u32[]{:S(2)}) collective-permute-start(f32[16,8,128]{2,1,0:T(8,128)S(1)} %add_add_fusion.1), channel_id=1, source_target_pairs={{0,16},{8,24},{16,0},{24,8},{32,48},{40,56},{48,32},{56,40},{64,80... | collective-permute-start | bytes 196616 | tf_op jit(solution)/shard_map/ppermute | solution.py:894
  113.0 7.3 %copy-start = (bf16[8,128,256]{2,1,0:T(8,128)(2,1)}, bf16[8,128,256]{2,1,0:T(8,128)(2,1)S(1)}, u32[]{:S(2)}) copy-start(bf16[8,128,256]{2,1,0:T(8,128)(2,1)S(1)} %all-to-all-done.3.mixed_ref) | copy-start | bytes 1572868
  113.9 15.3 %all-to-all-start.4 = ((f32[8,16,8,128]{3,2,1,0:T(8,128)}), f32[8,16,8,128]{3,2,1,0:T(8,128)}, u32[]{:S(2)}, u32[]{:S(2)}) async-start(f32[8,16,8,128]{3,2,1,0:T(8,128)} %broadcast_in_dim.27), calls=%async_computation.4 | async-start | bytes 1048576 | tf_op jit(solution)/shard_map/all_to_all | solution.py:884

commit v5 on v4

--- a/solution.py
+++ b/solution.py
@@ -23,6 +23,9 @@
 TN = (((0,), (0,)), ((), ()))
 
 CODES = 32
+
+OWN = 4
+SHARED = 11
 
 
 def _decode_codes():
@@ -761,7 +764,6 @@
     packed_ref[6] = step_heads
     for piece in range(2, 8):
         packed_ref[7 + piece] = embed_part[:, 128 * piece : 128 * piece + 128]
-    packed_ref[15] = jnp.zeros((8, 128), f32)
 
 
 def out_kernel(mixed_ref, ow_ref, token_ref, embed_ref, out_ref):
@@ -772,14 +774,23 @@
 
 
 def final_kernel(
-    whole_ref, embed_ref,
+    at_ref, first_ref, second_ref, third_ref, fourth_ref, embed_ref,
     w_in_ref, embedding_ref, conv_ref, bias_ref, dt_ref, rate_ref, skip_ref, gain_ref,
 ):
+    wholes = (first_ref, second_ref, third_ref, fourth_ref)
+    me = at_ref[1]
+
     def summed(piece):
-        total = whole_ref[0, piece]
-        for k in range(1, 8):
-            total = total + whole_ref[k, piece]
-        return total
+        one, two, three, four = [ref[2 * OWN + piece - OWN] for ref in wholes]
+        return (one + two) + (three + four)
+
+    def of_rank(rank, piece):
+        apart = jnp.bitwise_xor(me, rank)
+        at = jnp.bitwise_and(apart, 1) * OWN + piece
+        value = wholes[0][at]
+        for k in range(1, 4):
+            value = jnp.where(apart // 2 == k, wholes[k][at], value)
+        return value
 
     embed = embed_ref[...]
 
@@ -794,8 +805,8 @@
 
     for rank in range(8):
         for half in range(2):
-            gate = whole_ref[rank, half]
-            x = whole_ref[rank, 2 + half]
+            gate = of_rank(rank, half)
+            x = of_rank(rank, 2 + half)
             at = 256 * rank + 128 * half
             cols = slice(at, at + 128)
             outer(gate, at)
@@ -827,6 +838,7 @@
 
 
 VMEM = pl.BlockSpec(memory_space=pltpu.VMEM)
+SMEM = pl.BlockSpec(memory_space=pltpu.SMEM)
 VMEM_LIMIT = 62 * 1024 * 1024
 TOKEN_STEPS = 2
 ANY = pl.BlockSpec(memory_space=pl.ANY)
@@ -871,7 +883,7 @@
     return pl.pallas_call(
         kernel,
         out_shape=[jax.ShapeDtypeStruct(shape, kind) for shape, kind in outs],
-        in_specs=[VMEM] * len(operands),
+        in_specs=[SMEM if item.dtype == jnp.int32 else VMEM for item in operands],
         out_specs=[VMEM] * len(outs),
         compiler_params=pltpu.CompilerParams(vmem_limit_bytes=VMEM_LIMIT),
         cost_estimate=pl.CostEstimate(flops=int(cost), bytes_accessed=1000000, transcendentals=0),
@@ -1142,7 +1154,7 @@
             dgate,
             dgain,
         ],
-        [((shards, 8, 128), f32)],
+        [((OWN + SHARED, 8, 128), f32)],
         [
             pltpu.VMEM((2 * CODES, 1024), bf16),
             pltpu.VMEM((4, 128, 128), f32),
@@ -1169,21 +1181,27 @@
     token_ids = lax.dynamic_slice_in_dim(ids_later, head_rank * token_rows, token_rows, 0)
     alphabet = jnp.arange(5, dtype=jnp.int32)
     token_hot = (token_ids[:, None] == alphabet[None, :]).astype(bf16)
+
+    row_count = D // shards
+    columns = lax.dynamic_slice_in_dim(embed_later, seq_rank * row_count, row_count, 1)
+    columns = jnp.pad(columns, ((1, 2), (0, 0)))
+    columns = jnp.concatenate([columns] * 3, axis=0).T
+    total, mixed_all = lax.optimization_barrier((total, mixed_all))
+    pairs = [(i, i ^ 1) for i in range(groups)]
+    beside = lax.ppermute(total, "head", pairs)
+    total = jnp.concatenate([total[:OWN], beside[:OWN], total[OWN:] + beside[OWN:]], axis=0)
+    everything = [total] + [
+        lax.ppermute(total, "head", [(i, i ^ flip) for i in range(groups)]) for flip in (2, 4, 6)
+    ]
     (layer_out,) = call_plain(
         out_kernel,
         [mixed_all, out_weight, token_hot, embedding],
         [((token_rows, D), bf16)],
         4e9,
     )
-
-    row_count = D // shards
-    columns = lax.dynamic_slice_in_dim(embed_later, seq_rank * row_count, row_count, 1)
-    columns = jnp.pad(columns, ((1, 2), (0, 0)))
-    columns = jnp.concatenate([columns] * 3, axis=0).T
-    everything = gather(total, "head")
     w_in, embed, conv, bias, dt, rate, skip, gain = call_plain(
         final_kernel,
-        [everything, columns],
+        [at, *everything, columns],
         [
             ((row_count, in_weight.shape[1]), f32),
             (embedding.shape, f32),

time: 132 us -> 131 us (level)
  waiting for transfers between devices: 16.9 us -> 15 us
    ppermute x0 -> x4, starting transfers between devices: none -> 5.98 us  [the longest x3 4.77 us: body(): lax.ppermute(total, 'head', [(i, i ^ flip) for i in range(groups)])]
    all_to_all x2 -> x1, waiting for transfers between devices: 6.93 us -> 1.73 us  [gather(): return lax.all_to_all(spread, axis, split_axis=0, concat_axis=0, tiled=True)]
    all_to_all x2 -> x1, starting transfers between devices: 12.1 us -> 7.15 us  [gather(): return lax.all_to_all(spread, axis, split_axis=0, concat_axis=0, tiled=True)]
    ppermute x0 -> x4, waiting for transfers between devices: none -> 3.13 us  [the longest x1 3.12 us: body(): beside = lax.ppermute(total, 'head', pairs)]
    broadcast_in_dim x2 -> x1, local copies, waits for them, and re-layouts: 3.42 us -> 2.55 us  [gather(): spread = jnp.broadcast_to(shard[None], (devices,) + shard.shape)]
  transfers between devices with their start and end apart: 17 -> 20, of which waited for: 7 -> 7; matrix products, arithmetic and copies ran while one was open for 6% -> 6% of each run, Pallas kernels for 34% -> 35%
where the time goes in v5:
time: 131 us; the launch traced here: 130 us
  Pallas kernels  64.9 us (50%)
  starting transfers between devices  40.7 us (31%)
  waiting for transfers between devices  15 us (11%)
  local copies, waits for them, and re-layouts  5.39 us (4%)
  other arithmetic  3.58 us (3%)
    pallas_call x6, Pallas kernels, call(): pl.pallas_call(kernel, out_shape=shapes, grid_spec=pltpu.PrefetchScalarGr...  58.8 us
    all_to_all x3, starting transfers between devices, exchange(): return lax.all_to_all(array, axis, split_axis=0, concat_axis=0, tiled=True)  14.3 us
    all_to_all x1, starting transfers between devices, gather(): return lax.all_to_all(spread, axis, split_axis=0, concat_axis=0, tiled=True)  7.15 us
    ppermute x6, starting transfers between devices, gather_by_flips(): lax.ppermute(array, axis, pair)  7.01 us
    all_to_all x3, waiting for transfers between devices, exchange(): return lax.all_to_all(array, axis, split_axis=0, concat_axis=0, tiled=True)  6.57 us
    ppermute x6, starting transfers between devices, sum_by_flips(): one, two, three = [lax.ppermute(array, axis, pair) for pair in pairs]  6.31 us
    pallas_call x2, Pallas kernels, call_plain(): pl.pallas_call(kernel, out_shape=[jax.ShapeDtypeStruct(shape, kind) for s...  6.12 us
    ppermute x3, starting transfers between devices, body(): lax.ppermute(total, 'head', [(i, i ^ flip) for i in range(groups)])  4.77 us
  transfers between devices with their start and end apart: 20, of which 7 were waited for; matrix products, arithmetic and copies ran while one was open for 6% of the time, Pallas kernels for 35%

profile of v5, /device:TPU:0, one launch (start us, length us, event | category | flops | bytes accessed | tf_op | source)
XLA Modules:
  0.0 130.5 jit_solution(17442834492477775290)
XLA Ops:
  0.6 1.1 collective-permute-start.2
  2.6 2.5 %broadcast_in_dim.20 = bf16[8,128,1024]{2,1,0:T(8,128)(2,1)} broadcast(bf16[128,1024]{1,0:T(8,128)(2,1)} %refs_34_.1), dimensions={1,2} | broadcast | bytes 2359296 | tf_op jit(solution)/shard_map/broadcast_in_dim | solution.py:895
  5.1 7.1 %all-to-all-start = ((bf16[8,128,1024]{2,1,0:T(8,128)(2,1)}), bf16[8,128,1024]{2,1,0:T(8,128)(2,1)}, u32[]{:S(2)}, u32[]{:S(2)}) async-start(bf16[8,128,1024]{2,1,0:T(8,128)(2,1)} %broadcast_in_dim.20), calls=%async_computation | async-start | bytes 4194304 | tf_op jit(solution)/shard_map/all_to_all | solution.py:896
  13.0 4.1 %collective-permute-start.5 = (s32[4,8,128]{2,1,0:T(8,128)S(1)}, s32[4,8,128]{2,1,0:T(8,128)S(1)}, u32[]{:S(2)}, u32[]{:S(2)}) collective-permute-start(s32[4,8,128]{2,1,0:T(8,128)S(1)} %pad_add_fusion.1), channel_id=1, source_target_pairs={{0,48},{8,56},{16,32},{24,40},{32,16},{40,24},{48,0},{56,8},{64,11... | collective-permute-start | bytes 49160 | tf_op jit(solution)/shard_map/ppermute | solution.py:901
  17.1 0.9 collective-permute-start.3
  18.0 4.6 %shard_map.204 = (bf16[128,2048]{1,0:T(8,128)(2,1)}, bf16[128,512]{1,0:T(8,128)(2,1)}, f32[16,128]{1,0:T(8,128)}, f32[8,768]{1,0:T(8,128)}, f32[24,256]{1,0:T(8,...) custom-call(s32[2]{0:T(128)} %pad_add_fusion.2.at_ref, bf16[5,1024]{1,0:T(8,128)(2,1)} %embed_ref.3, ...), custom_call_target="tpu_custom_call" | custom-call | flops 6000000000 | bytes 4000000 | tf_op jit(solution)/shard_map/pallas_call | solution.py:867
  23.3 16.1 %shard_map.205 = (f32[1024,256]{1,0:T(8,128)}, f32[1024,256]{1,0:T(8,128)}, f32[2,4,128,256]{3,2,1,0:T(8,128)}, f32[64,128]{1,0:T(8,128)}, f32[4,128,128]{2,1,0:...) custom-call(s32[2]{0:T(128)} %pad_add_fusion.2.at_ref, ...), custom_call_target="tpu_custom_call" | custom-call | flops 15000000512 | bytes 4000000 | tf_op jit(solution)/shard_map/pallas_call | solution.py:867
  39.4 1.7 %all-to-all-done = bf16[8,128,1024]{2,1,0:T(8,128)(2,1)} async-done(((bf16[8,128,1024]{2,1,0:T(8,128)(2,1)}), bf16[8,128,1024]{2,1,0:T(8,128)(2,1)}, u32[]{:S(2)}, u32[]{:S(2)}) %all-to-all-start) | async-done | bytes 2097184 | tf_op jit(solution)/shard_map/all_to_all | solution.py:896
  41.1 4.9 %shard_map.206 = (f32[1024,256]{1,0:T(8,128)}, f32[8,4,1024]{2,1,0:T(4,128)}) custom-call(s32[2]{0:T(128)} %pad_add_fusion.2.at_ref, f32[1024,256]{1,0:T(8,128)} %get-tuple-element.72.y_first_ref.refs_2_.refs_16_, f32[1024,256]{1,0:T(8,128)} %get-tuple-element.74.y_second_ref.refs_7_.refs_15_.refs_8_, ...), custom_call_target="tpu_custom_call" | custom-call | flops 4000000000 | bytes 4000000 | tf_op jit(solution)/shard_map/pallas_call | solution.py:867
  46.0 5.5 %all-to-all-start.1 = ((f32[8,4,1024]{2,1,0:T(4,128)}), f32[8,4,1024]{2,1,0:T(4,128)S(1)}, u32[]{:S(2)}, u32[]{:S(2)}) async-start(f32[8,4,1024]{2,1,0:T(4,128)} %get-tuple-element.77), calls=%async_computation.1 | async-start | bytes 262144 | tf_op jit(solution)/shard_map/all_to_all | solution.py:911
  51.6 4.5 %shard_map.208 = (f32[1024,384]{1,0:T(8,128)}, f32[1024,384]{1,0:T(8,128)}, f32[1024,256]{1,0:T(8,128)}) custom-call(s32[2]{0:T(128)} %pad_add_fusion.2.at_ref, bf16[1024,128]{1,0:T(8,128)(2,1)} %constant.25.clone.goh_ref, bf16[128,2048]{1,0:T(8,128)(2,1)} %get-tuple-element.90.pre_ref.step_ref.gate_ref.refs_10_.refs_11_.refs_23_.refs_12_.refs_13_, ...), custom_call_target="tpu_custom_call" | custom-call | flops 2000000000 | bytes 4000000 | tf_op jit(solution)/shard_map/pallas_call | solution.py:867
  56.1 3.6 %all-to-all-done.1.refs_21_.refs_22_ = f32[8,4,1024]{2,1,0:T(4,128)S(1)} async-done(((f32[8,4,1024]{2,1,0:T(4,128)}), f32[8,4,1024]{2,1,0:T(4,128)S(1)}, u32[]{:S(2)}, u32[]{:S(2)}) %all-to-all-start.1) | async-done | bytes 131104 | tf_op jit(solution)/shard_map/all_to_all | solution.py:911
  60.4 12.6 %shard_map.207 = (f32[32,512]{1,0:T(8,128)}, f32[32,256]{1,0:T(8,128)}, f32[32,256]{1,0:T(8,128)}, f32[1,256]{1,0:T(1,128)}, f32[2,128,256]{2,1,0:T(8,128)}, /*i...) custom-call(s32[2]{0:T(128)} %pad_add_fusion.2.at_ref, ...), custom_call_target="tpu_custom_call" | custom-call | flops 20000000000 | bytes 4000000 | tf_op jit(solution)/shard_map/pallas_call | solution.py:867
  73.0 4.6 %all-to-all-start.2 = ((f32[16,64,256]{2,1,0:T(8,128)}), f32[16,64,256]{2,1,0:T(8,128)S(1)}, u32[]{:S(2)}, u32[]{:S(2)}) async-start(f32[16,64,256]{2,1,0:T(8,128)} %bitcast.24), calls=%async_computation.2 | async-start | bytes 2097152 | tf_op jit(solution)/shard_map/all_to_all | solution.py:911
  77.6 16.1 %shard_map.209 = f32[15,8,128]{2,1,0:T(8,128)} custom-call(s32[2]{0:T(128)} %pad_add_fusion.2.at_ref, bf16[1024,128]{1,0:T(8,128)(2,1)} %get-tuple-element.70.oh_ref.refs_0_.refs_5_.refs_6_, bf16[128,1024]{1,0:T(8,128)(2,1)} %get-tuple-element.71.refs_1_.refs_6_.refs_7_.refs_24_, f32[1024,256]{1,0:T(8,128)} %get-tuple-element.72.y_first_ref.refs_2_.refs_16_, ...), custom_call_target="tpu_custom_call" | custom-call | flops 20000000000 | bytes 4000000 | tf_op jit(solution)/shard_map/pallas_call | solution.py:867
  94.2 1.4 %collective-permute-start.7 = (f32[15,8,128]{2,1,0:T(8,128)}, f32[15,8,128]{2,1,0:T(8,128)S(1)}, u32[]{:S(2)}, u32[]{:S(2)}) collective-permute-start(f32[15,8,128]{2,1,0:T(8,128)} %shard_map.209), channel_id=1, source_target_pairs={{0,64},{8,72},{16,80},{24,88},{32,96},{40,104},{48,112},{56,120},{... | collective-permute-start | bytes 184328 | tf_op jit(solution)/shard_map/ppermute | solution.py:906
  95.6 0.7 collective-permute-start.6
  96.3 0.7 fusion.token_ref
  97.0 4.2 %all-to-all-start.3 = ((bf16[8,128,256]{2,1,0:T(8,128)(2,1)}), bf16[8,128,256]{2,1,0:T(8,128)(2,1)S(1)}, u32[]{:S(2)}, u32[]{:S(2)}) async-start(bf16[8,128,256]{2,1,0:T(8,128)(2,1)} %bitcast.11), calls=%async_computation.3 | async-start | bytes 1048576 | tf_op jit(solution)/shard_map/all_to_all | solution.py:911
  101.2 0.9 add_add_fusion.1
  102.1 3.0 %collective-permute-start.10 = (f32[15,8,128]{2,1,0:T(8,128)S(1)}, f32[15,8,128]{2,1,0:T(8,128)S(1)}, u32[]{:S(2)}, u32[]{:S(2)}) collective-permute-start(f32[15,8,128]{2,1,0:T(8,128)S(1)} %add_add_fusion.1), channel_id=1, source_target_pairs={{0,32},{8,40},{16,48},{24,56},{32,0},{40,8},{48,16},{56,24},{64,96... | collective-permute-start | bytes 184328 | tf_op jit(solution)/shard_map/ppermute | solution.py:906
  105.1 1.2 collective-permute-start.11
  106.2 0.8 constant_dynamic-slice_fusion
  107.0 0.9 collective-permute-done.10
  107.9 2.6 %collective-permute-done.11 = f32[15,8,128]{2,1,0:T(8,128)S(1)} collective-permute-done((f32[15,8,128]{2,1,0:T(8,128)S(1)}, f32[15,8,128]{2,1,0:T(8,128)S(1)}, u32[]{:S(2)}, u32[]{:S(2)}) %collective-permute-start.11) | collective-permute-done | bytes 61472 | tf_op jit(solution)/shard_map/ppermute | solution.py:906
  110.5 2.4 %all-to-all-done.3.mixed_ref = bf16[8,128,256]{2,1,0:T(8,128)(2,1)S(1)} async-done(((bf16[8,128,256]{2,1,0:T(8,128)(2,1)}), bf16[8,128,256]{2,1,0:T(8,128)(2,1)S(1)}, u32[]{:S(2)}, u32[]{:S(2)}) %all-to-all-start.3) | async-done | bytes 524320 | tf_op jit(solution)/shard_map/all_to_all | solution.py:911
  113.0 1.2 collective-permute-start.12
  115.6 3.1 %collective-permute-done.12 = f32[15,8,128]{2,1,0:T(8,128)S(1)} collective-permute-done((f32[15,8,128]{2,1,0:T(8,128)S(1)}, f32[15,8,128]{2,1,0:T(8,128)S(1)}, u32[]{:S(2)}, u32[]{:S(2)}) %collective-permute-start.12) | collective-permute-done | bytes 61472 | tf_op jit(solution)/shard_map/ppermute | solution.py:1191
  118.8 2.4 %collective-permute-start.14 = (f32[19,8,128]{2,1,0:T(8,128)S(1)}, f32[19,8,128]{2,1,0:T(8,128)S(1)}, u32[]{:S(2)}, u32[]{:S(2)}) collective-permute-start(f32[19,8,128]{2,1,0:T(8,128)S(1)} %pad_maximum_fusion.first_ref), channel_id=1, source_target_pairs={{0,4},{1,5},{2,6},{3,7},{4,0},{5,1},{6,2},{7,3},{8,12},{9,13},{10,... | collective-permute-start | bytes 233480 | tf_op jit(solution)/shard_map/ppermute | solution.py:1194
  121.2 2.3 %collective-permute-start.15 = (f32[19,8,128]{2,1,0:T(8,128)S(1)}, f32[19,8,128]{2,1,0:T(8,128)S(1)}, u32[]{:S(2)}, u32[]{:S(2)}) collective-permute-start(f32[19,8,128]{2,1,0:T(8,128)S(1)} %pad_maximum_fusion.first_ref), channel_id=1, source_target_pairs={{0,6},{1,7},{2,4},{3,5},{4,2},{5,3},{6,0},{7,1},{8,14},{9,15},{10,... | collective-permute-start | bytes 233480 | tf_op jit(solution)/shard_map/ppermute | solution.py:1194
  123.5 3.8 %shard_map.210 = bf16[128,1024]{1,0:T(8,128)(2,1)} custom-call(bf16[8,128,256]{2,1,0:T(8,128)(2,1)} %copy-done, bf16[2048,1024]{1,0:T(8,128)(2,1)} %ow_ref.3, bf16[128,5]{1,0:T(8,128)(2,1)} %fusion.token_ref, bf16[5,1024]{1,0:T(8,128)(2,1)} %embed_ref.3), custom_call_target="tpu_custom_call" | custom-call | flops 4000000000 | bytes 1000000 | tf_op jit(solution)/shard_map/pallas_call | solution.py:883
  128.0 2.3 %shard_map.211 = (f32[64,4384]{1,0:T(8,128)}, f32[5,1024]{1,0:T(8,128)}, f32[4,2304]{1,0:T(4,128)}, f32[18,128]{1,0:T(8,128)}, f32[1,32]{1,0:T(1,128)}, /*index=...) custom-call(s32[2]{0:T(128)} %pad_add_fusion.2.at_ref, f32[19,8,128]{2,1,0:T(8,128)} %copy-done.2, ...), custom_call_target="tpu_custom_call" | custom-call | flops 1000000000 | bytes 1000000 | tf_op jit(solution)/shard_map/pallas_call | solution.py:883
  (47 shorter events, 5.6 us)
Async XLA Ops:
  0.6 12.3 %collective-permute-start.2 = (s32[1,8,128]{2,1,0:T(8,128)}, s32[1,8,128]{2,1,0:T(8,128)S(1)}, u32[]{:S(2)}, u32[]{:S(2)}) collective-permute-start(s32[1,8,128]{2,1,0:T(8,128)} %bitcast.28), channel_id=1, source_target_pairs={{0,72},{8,64},{16,88},{24,80},{32,104},{40,96},{48,120},{56,112},{... | collective-permute-start | bytes 12296 | tf_op jit(solution)/shard_map/ppermute | solution.py:901
  1.7 11.2 %collective-permute-start.1 = (s32[1,8,128]{2,1,0:T(8,128)}, s32[1,8,128]{2,1,0:T(8,128)S(1)}, u32[]{:S(2)}, u32[]{:S(2)}) collective-permute-start(s32[1,8,128]{2,1,0:T(8,128)} %bitcast.29), channel_id=1, source_target_pairs={{0,64},{8,72},{16,80},{24,88},{32,96},{40,104},{48,112},{56,120},{... | collective-permute-start | bytes 12296 | tf_op jit(solution)/shard_map/ppermute | solution.py:901
  2.4 10.6 %collective-permute-start = (s32[1,8,128]{2,1,0:T(8,128)}, s32[1,8,128]{2,1,0:T(8,128)S(1)}, u32[]{:S(2)}, u32[]{:S(2)}) collective-permute-start(s32[1,8,128]{2,1,0:T(8,128)} %bitcast.30), channel_id=1, source_target_pairs={{0,8},{8,0},{16,24},{24,16},{32,40},{40,32},{48,56},{56,48},{64,72... | collective-permute-start | bytes 12296 | tf_op jit(solution)/shard_map/ppermute | solution.py:901
  5.1 7.8 %copy-start.3 = (s32[1024]{0:T(1024)S(1)}, s32[1024]{0:T(1024)}, u32[]{:S(2)}) copy-start(s32[1024]{0:T(1024)} %param.13) | copy-start | bytes 12292
  5.1 36.0 %all-to-all-start = ((bf16[8,128,1024]{2,1,0:T(8,128)(2,1)}), bf16[8,128,1024]{2,1,0:T(8,128)(2,1)}, u32[]{:S(2)}, u32[]{:S(2)}) async-start(bf16[8,128,1024]{2,1,0:T(8,128)(2,1)} %broadcast_in_dim.20), calls=%async_computation | async-start | bytes 4194304 | tf_op jit(solution)/shard_map/all_to_all | solution.py:896
  13.0 9.6 %collective-permute-start.5 = (s32[4,8,128]{2,1,0:T(8,128)S(1)}, s32[4,8,128]{2,1,0:T(8,128)S(1)}, u32[]{:S(2)}, u32[]{:S(2)}) collective-permute-start(s32[4,8,128]{2,1,0:T(8,128)S(1)} %pad_add_fusion.1), channel_id=1, source_target_pairs={{0,48},{8,56},{16,32},{24,40},{32,16},{40,24},{48,0},{56,8},{64,11... | collective-permute-start | bytes 49160 | tf_op jit(solution)/shard_map/ppermute | solution.py:901
  17.1 5.5 %collective-permute-start.4 = (s32[4,8,128]{2,1,0:T(8,128)S(1)}, s32[4,8,128]{2,1,0:T(8,128)S(1)}, u32[]{:S(2)}, u32[]{:S(2)}) collective-permute-start(s32[4,8,128]{2,1,0:T(8,128)S(1)} %pad_add_fusion.1), channel_id=1, source_target_pairs={{0,32},{8,40},{16,48},{24,56},{32,0},{40,8},{48,16},{56,24},{64,96... | collective-permute-start | bytes 49160 | tf_op jit(solution)/shard_map/ppermute | solution.py:901
  17.1 5.5 %collective-permute-start.3 = (s32[4,8,128]{2,1,0:T(8,128)S(1)}, s32[4,8,128]{2,1,0:T(8,128)S(1)}, u32[]{:S(2)}, u32[]{:S(2)}) collective-permute-start(s32[4,8,128]{2,1,0:T(8,128)S(1)} %pad_add_fusion.1), channel_id=1, source_target_pairs={{0,16},{8,24},{16,0},{24,8},{32,48},{40,56},{48,32},{56,40},{64,80... | collective-permute-start | bytes 49160 | tf_op jit(solution)/shard_map/ppermute | solution.py:901
  46.0 13.7 %all-to-all-start.1 = ((f32[8,4,1024]{2,1,0:T(4,128)}), f32[8,4,1024]{2,1,0:T(4,128)S(1)}, u32[]{:S(2)}, u32[]{:S(2)}) async-start(f32[8,4,1024]{2,1,0:T(4,128)} %get-tuple-element.77), calls=%async_computation.1 | async-start | bytes 262144 | tf_op jit(solution)/shard_map/all_to_all | solution.py:911
  59.7 0.7 copy-start.1
  73.0 21.2 %all-to-all-start.2 = ((f32[16,64,256]{2,1,0:T(8,128)}), f32[16,64,256]{2,1,0:T(8,128)S(1)}, u32[]{:S(2)}, u32[]{:S(2)}) async-start(f32[16,64,256]{2,1,0:T(8,128)} %bitcast.24), calls=%async_computation.2 | async-start | bytes 2097152 | tf_op jit(solution)/shard_map/all_to_all | solution.py:911
  94.2 7.0 %collective-permute-start.7 = (f32[15,8,128]{2,1,0:T(8,128)}, f32[15,8,128]{2,1,0:T(8,128)S(1)}, u32[]{:S(2)}, u32[]{:S(2)}) collective-permute-start(f32[15,8,128]{2,1,0:T(8,128)} %shard_map.209), channel_id=1, source_target_pairs={{0,64},{8,72},{16,80},{24,88},{32,96},{40,104},{48,112},{56,120},{... | collective-permute-start | bytes 184328 | tf_op jit(solution)/shard_map/ppermute | solution.py:906
  95.6 5.6 %collective-permute-start.8 = (f32[15,8,128]{2,1,0:T(8,128)}, f32[15,8,128]{2,1,0:T(8,128)S(1)}, u32[]{:S(2)}, u32[]{:S(2)}) collective-permute-start(f32[15,8,128]{2,1,0:T(8,128)} %shard_map.209), channel_id=1, source_target_pairs={{0,72},{8,64},{16,88},{24,80},{32,104},{40,96},{48,120},{56,112},{... | collective-permute-start | bytes 184328 | tf_op jit(solution)/shard_map/ppermute | solution.py:906
  95.6 5.6 %collective-permute-start.6 = (f32[15,8,128]{2,1,0:T(8,128)}, f32[15,8,128]{2,1,0:T(8,128)S(1)}, u32[]{:S(2)}, u32[]{:S(2)}) collective-permute-start(f32[15,8,128]{2,1,0:T(8,128)} %shard_map.209), channel_id=1, source_target_pairs={{0,8},{8,0},{16,24},{24,16},{32,40},{40,32},{48,56},{56,48},{64,72... | collective-permute-start | bytes 184328 | tf_op jit(solution)/shard_map/ppermute | solution.py:906
  97.0 15.9 %all-to-all-start.3 = ((bf16[8,128,256]{2,1,0:T(8,128)(2,1)}), bf16[8,128,256]{2,1,0:T(8,128)(2,1)S(1)}, u32[]{:S(2)}, u32[]{:S(2)}) async-start(bf16[8,128,256]{2,1,0:T(8,128)(2,1)} %bitcast.11), calls=%async_computation.3 | async-start | bytes 1048576 | tf_op jit(solution)/shard_map/all_to_all | solution.py:911
  102.1 5.8 %collective-permute-start.10 = (f32[15,8,128]{2,1,0:T(8,128)S(1)}, f32[15,8,128]{2,1,0:T(8,128)S(1)}, u32[]{:S(2)}, u32[]{:S(2)}) collective-permute-start(f32[15,8,128]{2,1,0:T(8,128)S(1)} %add_add_fusion.1), channel_id=1, source_target_pairs={{0,32},{8,40},{16,48},{24,56},{32,0},{40,8},{48,16},{56,24},{64,96... | collective-permute-start | bytes 184328 | tf_op jit(solution)/shard_map/ppermute | solution.py:906
  105.1 5.4 %collective-permute-start.11 = (f32[15,8,128]{2,1,0:T(8,128)S(1)}, f32[15,8,128]{2,1,0:T(8,128)S(1)}, u32[]{:S(2)}, u32[]{:S(2)}) collective-permute-start(f32[15,8,128]{2,1,0:T(8,128)S(1)} %add_add_fusion.1), channel_id=1, source_target_pairs={{0,48},{8,56},{16,32},{24,40},{32,16},{40,24},{48,0},{56,8},{64,11... | collective-permute-start | bytes 184328 | tf_op jit(solution)/shard_map/ppermute | solution.py:906
  106.2 4.3 %collective-permute-start.9 = (f32[15,8,128]{2,1,0:T(8,128)S(1)}, f32[15,8,128]{2,1,0:T(8,128)S(1)}, u32[]{:S(2)}, u32[]{:S(2)}) collective-permute-start(f32[15,8,128]{2,1,0:T(8,128)S(1)} %add_add_fusion.1), channel_id=1, source_target_pairs={{0,16},{8,24},{16,0},{24,8},{32,48},{40,56},{48,32},{56,40},{64,80... | collective-permute-start | bytes 184328 | tf_op jit(solution)/shard_map/ppermute | solution.py:906
  113.0 10.6 %copy-start = (bf16[8,128,256]{2,1,0:T(8,128)(2,1)}, bf16[8,128,256]{2,1,0:T(8,128)(2,1)S(1)}, u32[]{:S(2)}) copy-start(bf16[8,128,256]{2,1,0:T(8,128)(2,1)S(1)} %all-to-all-done.3.mixed_ref) | copy-start | bytes 1572868
  113.0 5.7 %collective-permute-start.12 = (f32[15,8,128]{2,1,0:T(8,128)S(1)}, f32[15,8,128]{2,1,0:T(8,128)S(1)}, u32[]{:S(2)}, u32[]{:S(2)}) collective-permute-start(f32[15,8,128]{2,1,0:T(8,128)S(1)} %add_add_fusion), channel_id=1, source_target_pairs={{0,1},{1,0},{2,3},{3,2},{4,5},{5,4},{6,7},{7,6},{8,9},{9,8},{10,11... | collective-permute-start | bytes 184328 | tf_op jit(solution)/shard_map/ppermute | solution.py:1191
  118.7 8.6 %copy-start.2 = (f32[19,8,128]{2,1,0:T(8,128)}, f32[19,8,128]{2,1,0:T(8,128)S(1)}, u32[]{:S(2)}) copy-start(f32[19,8,128]{2,1,0:T(8,128)S(1)} %pad_maximum_fusion.first_ref) | copy-start | bytes 233476
  118.7 8.6 %collective-permute-start.13 = (f32[19,8,128]{2,1,0:T(8,128)S(1)}, f32[19,8,128]{2,1,0:T(8,128)S(1)}, u32[]{:S(2)}, u32[]{:S(2)}) collective-permute-start(f32[19,8,128]{2,1,0:T(8,128)S(1)} %pad_maximum_fusion.first_ref), channel_id=1, source_target_pairs={{0,2},{1,3},{2,0},{3,1},{4,6},{5,7},{6,4},{7,5},{8,10},{9,11},{10,... | collective-permute-start | bytes 233480 | tf_op jit(solution)/shard_map/ppermute | solution.py:1194
  118.8 8.5 %collective-permute-start.14 = (f32[19,8,128]{2,1,0:T(8,128)S(1)}, f32[19,8,128]{2,1,0:T(8,128)S(1)}, u32[]{:S(2)}, u32[]{:S(2)}) collective-permute-start(f32[19,8,128]{2,1,0:T(8,128)S(1)} %pad_maximum_fusion.first_ref), channel_id=1, source_target_pairs={{0,4},{1,5},{2,6},{3,7},{4,0},{5,1},{6,2},{7,3},{8,12},{9,13},{10,... | collective-permute-start | bytes 233480 | tf_op jit(solution)/shard_map/ppermute | solution.py:1194
  121.2 6.1 %collective-permute-start.15 = (f32[19,8,128]{2,1,0:T(8,128)S(1)}, f32[19,8,128]{2,1,0:T(8,128)S(1)}, u32[]{:S(2)}, u32[]{:S(2)}) collective-permute-start(f32[19,8,128]{2,1,0:T(8,128)S(1)} %pad_maximum_fusion.first_ref), channel_id=1, source_target_pairs={{0,6},{1,7},{2,4},{3,5},{4,2},{5,3},{6,0},{7,1},{8,14},{9,15},{10,... | collective-permute-start | bytes 233480 | tf_op jit(solution)/shard_map/ppermute | solution.py:1194
  127.3 0.6 copy-start.4
  127.3 0.6 copy-start.5
  127.3 0.7 copy-start.6

commit v6 on v5

--- a/solution.py
+++ b/solution.py
@@ -165,7 +165,6 @@
     x_w = x_w_ref[...]
     bc_w = bc_w_ref[...]
     step_w = step_w_ref[...]
-    step_w = jnp.where(iota((128, D), 0) < HEADS, step_w.astype(f32), 0.0).astype(bf16)
 
     def heads_row(ref):
         return jnp.concatenate([ref[...], jnp.zeros((1, 128 - HEADS), f32)], axis=1)
@@ -183,7 +182,8 @@
     row = iota((8, 128), 0)
     lane = iota((8, 128), 1)
     valid = (row >= 1) & (row <= 5)
-    pre = dot1(embed, step_w, NT) + heads_row(dt_ref)
+    pre = dot1(embed, step_w, NT)
+    pre = jnp.concatenate([pre, jnp.zeros((8, 128 - HEADS), f32)], axis=1) + heads_row(dt_ref)
     valid = valid & (lane < HEADS)
     step = jnp.maximum(pre, 0.0) + jnp.log1p(jnp.exp(-jnp.abs(pre)))
     rate = jnp.exp(heads_row(rate_ref))
@@ -937,7 +937,7 @@
         (weight_t, (width, D), lambda i, at: (at[1], 0)),
         (weight_t, (width, D), lambda i, at: (INNER // width + at[1], 0)),
         (weight_t, (256, D), lambda i, at: (16, 0)),
-        (weight_t, (128, D), lambda i, at: (34, 0)),
+        (weight_t, (HEADS, D), lambda i, at: ((2 * INNER + 2 * STATE) // HEADS, 0)),
     ]
     convs = [
         (conv_weight, (KCONV, width), lambda i, at: (0, at[1])),

time: 131 us -> 131 us (level)
  no operation moved by 1% of the time
where the time goes in v6:
time: 131 us; the launch traced here: 130 us
  Pallas kernels  64.9 us (50%)
  starting transfers between devices  40.7 us (31%)
  waiting for transfers between devices  15 us (11%)
  local copies, waits for them, and re-layouts  5.39 us (4%)
  other arithmetic  3.58 us (3%)
    pallas_call x6, Pallas kernels, call(): pl.pallas_call(kernel, out_shape=shapes, grid_spec=pltpu.PrefetchScalarGr...  58.8 us
    all_to_all x3, starting transfers between devices, exchange(): return lax.all_to_all(array, axis, split_axis=0, concat_axis=0, tiled=True)  14.3 us
    all_to_all x1, starting transfers between devices, gather(): return lax.all_to_all(spread, axis, split_axis=0, concat_axis=0, tiled=True)  7.15 us
    ppermute x6, starting transfers between devices, gather_by_flips(): lax.ppermute(array, axis, pair)  7.01 us
    all_to_all x3, waiting for transfers between devices, exchange(): return lax.all_to_all(array, axis, split_axis=0, concat_axis=0, tiled=True)  6.57 us
    ppermute x6, starting transfers between devices, sum_by_flips(): one, two, three = [lax.ppermute(array, axis, pair) for pair in pairs]  6.31 us
    pallas_call x2, Pallas kernels, call_plain(): pl.pallas_call(kernel, out_shape=[jax.ShapeDtypeStruct(shape, kind) for s...  6.12 us
    ppermute x3, starting transfers between devices, body(): lax.ppermute(total, 'head', [(i, i ^ flip) for i in range(groups)])  4.77 us
  transfers between devices with their start and end apart: 20, of which 7 were waited for; matrix products, arithmetic and copies ran while one was open for 6% of the time, Pallas kernels for 35%

profile of v6, /device:TPU:0, one launch (start us, length us, event | category | flops | bytes accessed | tf_op | source)
XLA Modules:
  0.0 130.5 jit_solution(13269763470573945156)
XLA Ops:
  0.6 1.1 collective-permute-start.2
  2.6 2.5 %broadcast_in_dim.20 = bf16[8,128,1024]{2,1,0:T(8,128)(2,1)} broadcast(bf16[128,1024]{1,0:T(8,128)(2,1)} %refs_34_.1), dimensions={1,2} | broadcast | bytes 2359296 | tf_op jit(solution)/shard_map/broadcast_in_dim | solution.py:895
  5.1 7.1 %all-to-all-start = ((bf16[8,128,1024]{2,1,0:T(8,128)(2,1)}), bf16[8,128,1024]{2,1,0:T(8,128)(2,1)}, u32[]{:S(2)}, u32[]{:S(2)}) async-start(bf16[8,128,1024]{2,1,0:T(8,128)(2,1)} %broadcast_in_dim.20), calls=%async_computation | async-start | bytes 4194304 | tf_op jit(solution)/shard_map/all_to_all | solution.py:896
  13.0 4.1 %collective-permute-start.5 = (s32[4,8,128]{2,1,0:T(8,128)S(1)}, s32[4,8,128]{2,1,0:T(8,128)S(1)}, u32[]{:S(2)}, u32[]{:S(2)}) collective-permute-start(s32[4,8,128]{2,1,0:T(8,128)S(1)} %pad_add_fusion.1), channel_id=1, source_target_pairs={{0,48},{8,56},{16,32},{24,40},{32,16},{40,24},{48,0},{56,8},{64,11... | collective-permute-start | bytes 49160 | tf_op jit(solution)/shard_map/ppermute | solution.py:901
  17.1 0.9 collective-permute-start.3
  18.0 4.6 %shard_map.204 = (bf16[128,2048]{1,0:T(8,128)(2,1)}, bf16[128,512]{1,0:T(8,128)(2,1)}, f32[16,128]{1,0:T(8,128)}, f32[8,768]{1,0:T(8,128)}, f32[24,256]{1,0:T(8,...) custom-call(s32[2]{0:T(128)} %pad_add_fusion.2.at_ref, bf16[5,1024]{1,0:T(8,128)(2,1)} %embed_ref.3, ...), custom_call_target="tpu_custom_call" | custom-call | flops 6000000000 | bytes 4000000 | tf_op jit(solution)/shard_map/pallas_call | solution.py:867
  23.3 16.1 %shard_map.205 = (f32[1024,256]{1,0:T(8,128)}, f32[1024,256]{1,0:T(8,128)}, f32[2,4,128,256]{3,2,1,0:T(8,128)}, f32[64,128]{1,0:T(8,128)}, f32[4,128,128]{2,1,0:...) custom-call(s32[2]{0:T(128)} %pad_add_fusion.2.at_ref, ...), custom_call_target="tpu_custom_call" | custom-call | flops 15000000512 | bytes 4000000 | tf_op jit(solution)/shard_map/pallas_call | solution.py:867
  39.4 1.7 %all-to-all-done = bf16[8,128,1024]{2,1,0:T(8,128)(2,1)} async-done(((bf16[8,128,1024]{2,1,0:T(8,128)(2,1)}), bf16[8,128,1024]{2,1,0:T(8,128)(2,1)}, u32[]{:S(2)}, u32[]{:S(2)}) %all-to-all-start) | async-done | bytes 2097184 | tf_op jit(solution)/shard_map/all_to_all | solution.py:896
  41.1 4.9 %shard_map.206 = (f32[1024,256]{1,0:T(8,128)}, f32[8,4,1024]{2,1,0:T(4,128)}) custom-call(s32[2]{0:T(128)} %pad_add_fusion.2.at_ref, f32[1024,256]{1,0:T(8,128)} %get-tuple-element.72.y_first_ref.refs_2_.refs_16_, f32[1024,256]{1,0:T(8,128)} %get-tuple-element.74.y_second_ref.refs_7_.refs_15_.refs_8_, ...), custom_call_target="tpu_custom_call" | custom-call | flops 4000000000 | bytes 4000000 | tf_op jit(solution)/shard_map/pallas_call | solution.py:867
  46.0 5.5 %all-to-all-start.1 = ((f32[8,4,1024]{2,1,0:T(4,128)}), f32[8,4,1024]{2,1,0:T(4,128)S(1)}, u32[]{:S(2)}, u32[]{:S(2)}) async-start(f32[8,4,1024]{2,1,0:T(4,128)} %get-tuple-element.77), calls=%async_computation.1 | async-start | bytes 262144 | tf_op jit(solution)/shard_map/all_to_all | solution.py:911
  51.6 4.5 %shard_map.208 = (f32[1024,384]{1,0:T(8,128)}, f32[1024,384]{1,0:T(8,128)}, f32[1024,256]{1,0:T(8,128)}) custom-call(s32[2]{0:T(128)} %pad_add_fusion.2.at_ref, bf16[1024,128]{1,0:T(8,128)(2,1)} %constant.25.clone.goh_ref, bf16[128,2048]{1,0:T(8,128)(2,1)} %get-tuple-element.90.pre_ref.step_ref.gate_ref.refs_10_.refs_11_.refs_23_.refs_12_.refs_13_, ...), custom_call_target="tpu_custom_call" | custom-call | flops 2000000000 | bytes 4000000 | tf_op jit(solution)/shard_map/pallas_call | solution.py:867
  56.1 3.6 %all-to-all-done.1.refs_21_.refs_22_ = f32[8,4,1024]{2,1,0:T(4,128)S(1)} async-done(((f32[8,4,1024]{2,1,0:T(4,128)}), f32[8,4,1024]{2,1,0:T(4,128)S(1)}, u32[]{:S(2)}, u32[]{:S(2)}) %all-to-all-start.1) | async-done | bytes 131104 | tf_op jit(solution)/shard_map/all_to_all | solution.py:911
  60.4 12.6 %shard_map.207 = (f32[32,512]{1,0:T(8,128)}, f32[32,256]{1,0:T(8,128)}, f32[32,256]{1,0:T(8,128)}, f32[1,256]{1,0:T(1,128)}, f32[2,128,256]{2,1,0:T(8,128)}, /*i...) custom-call(s32[2]{0:T(128)} %pad_add_fusion.2.at_ref, ...), custom_call_target="tpu_custom_call" | custom-call | flops 20000000000 | bytes 4000000 | tf_op jit(solution)/shard_map/pallas_call | solution.py:867
  73.0 4.6 %all-to-all-start.2 = ((f32[16,64,256]{2,1,0:T(8,128)}), f32[16,64,256]{2,1,0:T(8,128)S(1)}, u32[]{:S(2)}, u32[]{:S(2)}) async-start(f32[16,64,256]{2,1,0:T(8,128)} %bitcast.24), calls=%async_computation.2 | async-start | bytes 2097152 | tf_op jit(solution)/shard_map/all_to_all | solution.py:911
  77.6 16.1 %shard_map.209 = f32[15,8,128]{2,1,0:T(8,128)} custom-call(s32[2]{0:T(128)} %pad_add_fusion.2.at_ref, bf16[1024,128]{1,0:T(8,128)(2,1)} %get-tuple-element.70.oh_ref.refs_0_.refs_5_.refs_6_, bf16[128,1024]{1,0:T(8,128)(2,1)} %get-tuple-element.71.refs_1_.refs_6_.refs_7_.refs_24_, f32[1024,256]{1,0:T(8,128)} %get-tuple-element.72.y_first_ref.refs_2_.refs_16_, ...), custom_call_target="tpu_custom_call" | custom-call | flops 20000000000 | bytes 4000000 | tf_op jit(solution)/shard_map/pallas_call | solution.py:867
  94.2 1.4 %collective-permute-start.7 = (f32[15,8,128]{2,1,0:T(8,128)}, f32[15,8,128]{2,1,0:T(8,128)S(1)}, u32[]{:S(2)}, u32[]{:S(2)}) collective-permute-start(f32[15,8,128]{2,1,0:T(8,128)} %shard_map.209), channel_id=1, source_target_pairs={{0,64},{8,72},{16,80},{24,88},{32,96},{40,104},{48,112},{56,120},{... | collective-permute-start | bytes 184328 | tf_op jit(solution)/shard_map/ppermute | solution.py:906
  95.6 0.7 collective-permute-start.6
  96.3 0.7 fusion.token_ref
  97.0 4.2 %all-to-all-start.3 = ((bf16[8,128,256]{2,1,0:T(8,128)(2,1)}), bf16[8,128,256]{2,1,0:T(8,128)(2,1)S(1)}, u32[]{:S(2)}, u32[]{:S(2)}) async-start(bf16[8,128,256]{2,1,0:T(8,128)(2,1)} %bitcast.11), calls=%async_computation.3 | async-start | bytes 1048576 | tf_op jit(solution)/shard_map/all_to_all | solution.py:911
  101.2 0.9 add_add_fusion.1
  102.1 3.0 %collective-permute-start.10 = (f32[15,8,128]{2,1,0:T(8,128)S(1)}, f32[15,8,128]{2,1,0:T(8,128)S(1)}, u32[]{:S(2)}, u32[]{:S(2)}) collective-permute-start(f32[15,8,128]{2,1,0:T(8,128)S(1)} %add_add_fusion.1), channel_id=1, source_target_pairs={{0,32},{8,40},{16,48},{24,56},{32,0},{40,8},{48,16},{56,24},{64,96... | collective-permute-start | bytes 184328 | tf_op jit(solution)/shard_map/ppermute | solution.py:906
  105.1 1.2 collective-permute-start.11
  106.2 0.8 constant_dynamic-slice_fusion
  107.0 0.9 collective-permute-done.10
  107.9 2.6 %collective-permute-done.11 = f32[15,8,128]{2,1,0:T(8,128)S(1)} collective-permute-done((f32[15,8,128]{2,1,0:T(8,128)S(1)}, f32[15,8,128]{2,1,0:T(8,128)S(1)}, u32[]{:S(2)}, u32[]{:S(2)}) %collective-permute-start.11) | collective-permute-done | bytes 61472 | tf_op jit(solution)/shard_map/ppermute | solution.py:906
  110.5 2.4 %all-to-all-done.3.mixed_ref = bf16[8,128,256]{2,1,0:T(8,128)(2,1)S(1)} async-done(((bf16[8,128,256]{2,1,0:T(8,128)(2,1)}), bf16[8,128,256]{2,1,0:T(8,128)(2,1)S(1)}, u32[]{:S(2)}, u32[]{:S(2)}) %all-to-all-start.3) | async-done | bytes 524320 | tf_op jit(solution)/shard_map/all_to_all | solution.py:911
  113.0 1.2 collective-permute-start.12
  115.6 3.1 %collective-permute-done.12 = f32[15,8,128]{2,1,0:T(8,128)S(1)} collective-permute-done((f32[15,8,128]{2,1,0:T(8,128)S(1)}, f32[15,8,128]{2,1,0:T(8,128)S(1)}, u32[]{:S(2)}, u32[]{:S(2)}) %collective-permute-start.12) | collective-permute-done | bytes 61472 | tf_op jit(solution)/shard_map/ppermute | solution.py:1191
  118.8 2.4 %collective-permute-start.14 = (f32[19,8,128]{2,1,0:T(8,128)S(1)}, f32[19,8,128]{2,1,0:T(8,128)S(1)}, u32[]{:S(2)}, u32[]{:S(2)}) collective-permute-start(f32[19,8,128]{2,1,0:T(8,128)S(1)} %pad_maximum_fusion.first_ref), channel_id=1, source_target_pairs={{0,4},{1,5},{2,6},{3,7},{4,0},{5,1},{6,2},{7,3},{8,12},{9,13},{10,... | collective-permute-start | bytes 233480 | tf_op jit(solution)/shard_map/ppermute | solution.py:1194
  121.2 2.3 %collective-permute-start.15 = (f32[19,8,128]{2,1,0:T(8,128)S(1)}, f32[19,8,128]{2,1,0:T(8,128)S(1)}, u32[]{:S(2)}, u32[]{:S(2)}) collective-permute-start(f32[19,8,128]{2,1,0:T(8,128)S(1)} %pad_maximum_fusion.first_ref), channel_id=1, source_target_pairs={{0,6},{1,7},{2,4},{3,5},{4,2},{5,3},{6,0},{7,1},{8,14},{9,15},{10,... | collective-permute-start | bytes 233480 | tf_op jit(solution)/shard_map/ppermute | solution.py:1194
  123.5 3.8 %shard_map.210 = bf16[128,1024]{1,0:T(8,128)(2,1)} custom-call(bf16[8,128,256]{2,1,0:T(8,128)(2,1)} %copy-done, bf16[2048,1024]{1,0:T(8,128)(2,1)} %ow_ref.3, bf16[128,5]{1,0:T(8,128)(2,1)} %fusion.token_ref, bf16[5,1024]{1,0:T(8,128)(2,1)} %embed_ref.3), custom_call_target="tpu_custom_call" | custom-call | flops 4000000000 | bytes 1000000 | tf_op jit(solution)/shard_map/pallas_call | solution.py:883
  128.0 2.3 %shard_map.211 = (f32[64,4384]{1,0:T(8,128)}, f32[5,1024]{1,0:T(8,128)}, f32[4,2304]{1,0:T(4,128)}, f32[18,128]{1,0:T(8,128)}, f32[1,32]{1,0:T(1,128)}, /*index=...) custom-call(s32[2]{0:T(128)} %pad_add_fusion.2.at_ref, f32[19,8,128]{2,1,0:T(8,128)} %copy-done.2, ...), custom_call_target="tpu_custom_call" | custom-call | flops 1000000000 | bytes 1000000 | tf_op jit(solution)/shard_map/pallas_call | solution.py:883
  (47 shorter events, 5.6 us)
Async XLA Ops:
  0.6 12.3 %collective-permute-start.2 = (s32[1,8,128]{2,1,0:T(8,128)}, s32[1,8,128]{2,1,0:T(8,128)S(1)}, u32[]{:S(2)}, u32[]{:S(2)}) collective-permute-start(s32[1,8,128]{2,1,0:T(8,128)} %bitcast.28), channel_id=1, source_target_pairs={{0,72},{8,64},{16,88},{24,80},{32,104},{40,96},{48,120},{56,112},{... | collective-permute-start | bytes 12296 | tf_op jit(solution)/shard_map/ppermute | solution.py:901
  1.7 11.2 %collective-permute-start.1 = (s32[1,8,128]{2,1,0:T(8,128)}, s32[1,8,128]{2,1,0:T(8,128)S(1)}, u32[]{:S(2)}, u32[]{:S(2)}) collective-permute-start(s32[1,8,128]{2,1,0:T(8,128)} %bitcast.29), channel_id=1, source_target_pairs={{0,64},{8,72},{16,80},{24,88},{32,96},{40,104},{48,112},{56,120},{... | collective-permute-start | bytes 12296 | tf_op jit(solution)/shard_map/ppermute | solution.py:901
  2.4 10.6 %collective-permute-start = (s32[1,8,128]{2,1,0:T(8,128)}, s32[1,8,128]{2,1,0:T(8,128)S(1)}, u32[]{:S(2)}, u32[]{:S(2)}) collective-permute-start(s32[1,8,128]{2,1,0:T(8,128)} %bitcast.30), channel_id=1, source_target_pairs={{0,8},{8,0},{16,24},{24,16},{32,40},{40,32},{48,56},{56,48},{64,72... | collective-permute-start | bytes 12296 | tf_op jit(solution)/shard_map/ppermute | solution.py:901
  5.1 7.8 %copy-start.3 = (s32[1024]{0:T(1024)S(1)}, s32[1024]{0:T(1024)}, u32[]{:S(2)}) copy-start(s32[1024]{0:T(1024)} %param.13) | copy-start | bytes 12292
  5.1 36.0 %all-to-all-start = ((bf16[8,128,1024]{2,1,0:T(8,128)(2,1)}), bf16[8,128,1024]{2,1,0:T(8,128)(2,1)}, u32[]{:S(2)}, u32[]{:S(2)}) async-start(bf16[8,128,1024]{2,1,0:T(8,128)(2,1)} %broadcast_in_dim.20), calls=%async_computation | async-start | bytes 4194304 | tf_op jit(solution)/shard_map/all_to_all | solution.py:896
  13.0 9.6 %collective-permute-start.5 = (s32[4,8,128]{2,1,0:T(8,128)S(1)}, s32[4,8,128]{2,1,0:T(8,128)S(1)}, u32[]{:S(2)}, u32[]{:S(2)}) collective-permute-start(s32[4,8,128]{2,1,0:T(8,128)S(1)} %pad_add_fusion.1), channel_id=1, source_target_pairs={{0,48},{8,56},{16,32},{24,40},{32,16},{40,24},{48,0},{56,8},{64,11... | collective-permute-start | bytes 49160 | tf_op jit(solution)/shard_map/ppermute | solution.py:901
  17.1 5.5 %collective-permute-start.4 = (s32[4,8,128]{2,1,0:T(8,128)S(1)}, s32[4,8,128]{2,1,0:T(8,128)S(1)}, u32[]{:S(2)}, u32[]{:S(2)}) collective-permute-start(s32[4,8,128]{2,1,0:T(8,128)S(1)} %pad_add_fusion.1), channel_id=1, source_target_pairs={{0,32},{8,40},{16,48},{24,56},{32,0},{40,8},{48,16},{56,24},{64,96... | collective-permute-start | bytes 49160 | tf_op jit(solution)/shard_map/ppermute | solution.py:901
  17.1 5.5 %collective-permute-start.3 = (s32[4,8,128]{2,1,0:T(8,128)S(1)}, s32[4,8,128]{2,1,0:T(8,128)S(1)}, u32[]{:S(2)}, u32[]{:S(2)}) collective-permute-start(s32[4,8,128]{2,1,0:T(8,128)S(1)} %pad_add_fusion.1), channel_id=1, source_target_pairs={{0,16},{8,24},{16,0},{24,8},{32,48},{40,56},{48,32},{56,40},{64,80... | collective-permute-start | bytes 49160 | tf_op jit(solution)/shard_map/ppermute | solution.py:901
  46.0 13.7 %all-to-all-start.1 = ((f32[8,4,1024]{2,1,0:T(4,128)}), f32[8,4,1024]{2,1,0:T(4,128)S(1)}, u32[]{:S(2)}, u32[]{:S(2)}) async-start(f32[8,4,1024]{2,1,0:T(4,128)} %get-tuple-element.77), calls=%async_computation.1 | async-start | bytes 262144 | tf_op jit(solution)/shard_map/all_to_all | solution.py:911
  59.7 0.7 copy-start.1
  73.0 21.2 %all-to-all-start.2 = ((f32[16,64,256]{2,1,0:T(8,128)}), f32[16,64,256]{2,1,0:T(8,128)S(1)}, u32[]{:S(2)}, u32[]{:S(2)}) async-start(f32[16,64,256]{2,1,0:T(8,128)} %bitcast.24), calls=%async_computation.2 | async-start | bytes 2097152 | tf_op jit(solution)/shard_map/all_to_all | solution.py:911
  94.2 7.0 %collective-permute-start.7 = (f32[15,8,128]{2,1,0:T(8,128)}, f32[15,8,128]{2,1,0:T(8,128)S(1)}, u32[]{:S(2)}, u32[]{:S(2)}) collective-permute-start(f32[15,8,128]{2,1,0:T(8,128)} %shard_map.209), channel_id=1, source_target_pairs={{0,64},{8,72},{16,80},{24,88},{32,96},{40,104},{48,112},{56,120},{... | collective-permute-start | bytes 184328 | tf_op jit(solution)/shard_map/ppermute | solution.py:906
  95.6 5.6 %collective-permute-start.8 = (f32[15,8,128]{2,1,0:T(8,128)}, f32[15,8,128]{2,1,0:T(8,128)S(1)}, u32[]{:S(2)}, u32[]{:S(2)}) collective-permute-start(f32[15,8,128]{2,1,0:T(8,128)} %shard_map.209), channel_id=1, source_target_pairs={{0,72},{8,64},{16,88},{24,80},{32,104},{40,96},{48,120},{56,112},{... | collective-permute-start | bytes 184328 | tf_op jit(solution)/shard_map/ppermute | solution.py:906
  95.6 5.6 %collective-permute-start.6 = (f32[15,8,128]{2,1,0:T(8,128)}, f32[15,8,128]{2,1,0:T(8,128)S(1)}, u32[]{:S(2)}, u32[]{:S(2)}) collective-permute-start(f32[15,8,128]{2,1,0:T(8,128)} %shard_map.209), channel_id=1, source_target_pairs={{0,8},{8,0},{16,24},{24,16},{32,40},{40,32},{48,56},{56,48},{64,72... | collective-permute-start | bytes 184328 | tf_op jit(solution)/shard_map/ppermute | solution.py:906
  97.0 15.9 %all-to-all-start.3 = ((bf16[8,128,256]{2,1,0:T(8,128)(2,1)}), bf16[8,128,256]{2,1,0:T(8,128)(2,1)S(1)}, u32[]{:S(2)}, u32[]{:S(2)}) async-start(bf16[8,128,256]{2,1,0:T(8,128)(2,1)} %bitcast.11), calls=%async_computation.3 | async-start | bytes 1048576 | tf_op jit(solution)/shard_map/all_to_all | solution.py:911
  102.1 5.8 %collective-permute-start.10 = (f32[15,8,128]{2,1,0:T(8,128)S(1)}, f32[15,8,128]{2,1,0:T(8,128)S(1)}, u32[]{:S(2)}, u32[]{:S(2)}) collective-permute-start(f32[15,8,128]{2,1,0:T(8,128)S(1)} %add_add_fusion.1), channel_id=1, source_target_pairs={{0,32},{8,40},{16,48},{24,56},{32,0},{40,8},{48,16},{56,24},{64,96... | collective-permute-start | bytes 184328 | tf_op jit(solution)/shard_map/ppermute | solution.py:906
  105.1 5.4 %collective-permute-start.11 = (f32[15,8,128]{2,1,0:T(8,128)S(1)}, f32[15,8,128]{2,1,0:T(8,128)S(1)}, u32[]{:S(2)}, u32[]{:S(2)}) collective-permute-start(f32[15,8,128]{2,1,0:T(8,128)S(1)} %add_add_fusion.1), channel_id=1, source_target_pairs={{0,48},{8,56},{16,32},{24,40},{32,16},{40,24},{48,0},{56,8},{64,11... | collective-permute-start | bytes 184328 | tf_op jit(solution)/shard_map/ppermute | solution.py:906
  106.2 4.3 %collective-permute-start.9 = (f32[15,8,128]{2,1,0:T(8,128)S(1)}, f32[15,8,128]{2,1,0:T(8,128)S(1)}, u32[]{:S(2)}, u32[]{:S(2)}) collective-permute-start(f32[15,8,128]{2,1,0:T(8,128)S(1)} %add_add_fusion.1), channel_id=1, source_target_pairs={{0,16},{8,24},{16,0},{24,8},{32,48},{40,56},{48,32},{56,40},{64,80... | collective-permute-start | bytes 184328 | tf_op jit(solution)/shard_map/ppermute | solution.py:906
  113.0 10.6 %copy-start = (bf16[8,128,256]{2,1,0:T(8,128)(2,1)}, bf16[8,128,256]{2,1,0:T(8,128)(2,1)S(1)}, u32[]{:S(2)}) copy-start(bf16[8,128,256]{2,1,0:T(8,128)(2,1)S(1)} %all-to-all-done.3.mixed_ref) | copy-start | bytes 1572868
  113.0 5.7 %collective-permute-start.12 = (f32[15,8,128]{2,1,0:T(8,128)S(1)}, f32[15,8,128]{2,1,0:T(8,128)S(1)}, u32[]{:S(2)}, u32[]{:S(2)}) collective-permute-start(f32[15,8,128]{2,1,0:T(8,128)S(1)} %add_add_fusion), channel_id=1, source_target_pairs={{0,1},{1,0},{2,3},{3,2},{4,5},{5,4},{6,7},{7,6},{8,9},{9,8},{10,11... | collective-permute-start | bytes 184328 | tf_op jit(solution)/shard_map/ppermute | solution.py:1191
  118.7 8.6 %copy-start.2 = (f32[19,8,128]{2,1,0:T(8,128)}, f32[19,8,128]{2,1,0:T(8,128)S(1)}, u32[]{:S(2)}) copy-start(f32[19,8,128]{2,1,0:T(8,128)S(1)} %pad_maximum_fusion.first_ref) | copy-start | bytes 233476
  118.7 8.6 %collective-permute-start.13 = (f32[19,8,128]{2,1,0:T(8,128)S(1)}, f32[19,8,128]{2,1,0:T(8,128)S(1)}, u32[]{:S(2)}, u32[]{:S(2)}) collective-permute-start(f32[19,8,128]{2,1,0:T(8,128)S(1)} %pad_maximum_fusion.first_ref), channel_id=1, source_target_pairs={{0,2},{1,3},{2,0},{3,1},{4,6},{5,7},{6,4},{7,5},{8,10},{9,11},{10,... | collective-permute-start | bytes 233480 | tf_op jit(solution)/shard_map/ppermute | solution.py:1194
  118.8 8.5 %collective-permute-start.14 = (f32[19,8,128]{2,1,0:T(8,128)S(1)}, f32[19,8,128]{2,1,0:T(8,128)S(1)}, u32[]{:S(2)}, u32[]{:S(2)}) collective-permute-start(f32[19,8,128]{2,1,0:T(8,128)S(1)} %pad_maximum_fusion.first_ref), channel_id=1, source_target_pairs={{0,4},{1,5},{2,6},{3,7},{4,0},{5,1},{6,2},{7,3},{8,12},{9,13},{10,... | collective-permute-start | bytes 233480 | tf_op jit(solution)/shard_map/ppermute | solution.py:1194
  121.2 6.1 %collective-permute-start.15 = (f32[19,8,128]{2,1,0:T(8,128)S(1)}, f32[19,8,128]{2,1,0:T(8,128)S(1)}, u32[]{:S(2)}, u32[]{:S(2)}) collective-permute-start(f32[19,8,128]{2,1,0:T(8,128)S(1)} %pad_maximum_fusion.first_ref), channel_id=1, source_target_pairs={{0,6},{1,7},{2,4},{3,5},{4,2},{5,3},{6,0},{7,1},{8,14},{9,15},{10,... | collective-permute-start | bytes 233480 | tf_op jit(solution)/shard_map/ppermute | solution.py:1194
  127.3 0.6 copy-start.4
  127.3 0.6 copy-start.5
  127.3 0.7 copy-start.6
